TPU v7x, 512 devices: a whole 4x4x16 slice. The times are simulated.
512 devices in a mesh: dp: 64 (over z, y), head: 8 (over x, core).
Axes of the slice: x: 4, y: 4, z: 16, core: 2. Of those that a mesh axis runs over, the one named last changes fastest.
Arguments:
- tokens: bfloat16 [8192, 1536], P('dp'), may hold values from -6 to 6
- cotangent: bfloat16 [8192, 1536], P('dp'), may hold values from -2 to 2
- w_qkv: bfloat16 [1536, 3, 1024], P(None, None, 'head'), may hold values from -0.15625 to 0.15625
- w_out: bfloat16 [1024, 1536], P('head'), may hold values from -0.5 to 0.5
- qk_gain: float32 [2, 64], replicated, may hold values from 1 to 4.5
- modulation: bfloat16 [32, 3, 1536], replicated, may hold values from -4 to 4
- image_counts: int32 [32], replicated, may hold values from 1 to 768, as said below
Outputs:
- layer_out: bfloat16 [8192, 1536], P(('dp', 'head'))
- input_grad: bfloat16 [8192, 1536], P(('dp', 'head'))
Inputs may be any that keep to these rules, and one draw needn't show every extreme that they name: `image_counts`: the counts sum to 8192; each image's rows are consecutive in the pack, images in the order of this array; 8 of the images, at places drawn anew, hold exactly 768 tokens each, and every other image fewer.
All inputs are finite; a program needn't handle non-finite values.
Results may differ from a plain program's by a relative error of at most 0.028.
The roundings to bfloat16 on the way count: a program that leaves them out, or rounds other values in their place, can miss the bound.
Values may be sent and summed in bfloat16 or wider, within the bound.
No kernel may reach another device: no remote copies, remote signals or barrier semaphores. Data moves between devices by JAX's collectives and lax.ppermute only.
A program may use at most 64 MiB of HBM per device.

v0:
```python
import math

import jax
import jax.numpy as jnp
from jax import lax
from jax.experimental import pallas as pl
from jax.experimental.pallas import tpu as pltpu
from jax.sharding import PartitionSpec as P

EPS = 1e-06
SAME_IMAGE = 512.0
LANES = 128
HEAD = 64
F32 = jnp.float32
BF16 = jnp.bfloat16
VMEM_LIMIT = 24 * 1024 * 1024
ENTER_LIMIT = 60 * 1024 * 1024
VMEM = pl.BlockSpec(memory_space=pltpu.VMEM)
SMEM = pl.BlockSpec(memory_space=pltpu.SMEM)


def rows_dot(a, b):
    return lax.dot_general(a, b, (((1,), (1,)), ((), ())), preferred_element_type=F32)


def block_index():
    return (lax.axis_index("z") * 2 + lax.axis_index("yh")) * 2 + lax.axis_index("yl")


def image_bounds(counts_ref, first_lane):
    lane = lax.broadcasted_iota(jnp.int32, (1, LANES), 1)
    starts = jnp.zeros((1, LANES), jnp.int32)
    ends = jnp.zeros((1, LANES), jnp.int32)
    total = jnp.int32(0)
    for image in range(counts_ref.shape[0]):
        here = lane == first_lane + image
        starts = jnp.where(here, total, starts)
        total = total + counts_ref[image]
        ends = jnp.where(here, total, ends)
    return starts, ends


def modulation_rows(counts_ref, modulation_ref, first, rows):
    starts, ends = image_bounds(counts_ref, 0)
    place = first + lax.broadcasted_iota(jnp.int32, (rows, LANES), 0)
    member = ((place >= starts) & (place < ends)).astype(F32).astype(BF16)
    member = member[:, : modulation_ref.shape[1]]
    return [
        jnp.dot(member, modulation_ref[part], preferred_element_type=F32) for part in range(3)
    ]


def layer_norm(values):
    average = jnp.mean(values, axis=-1, keepdims=True)
    centred = values - average
    inv_std = lax.rsqrt(jnp.mean(centred * centred, axis=-1, keepdims=True) + EPS)
    return centred * inv_std, inv_std


def enter_kernel(
    counts_ref, tokens_ref, cotangent_ref, w_qkv_ref, w_out_ref, modulation_ref, out_ref
):
    rows = tokens_ref.shape[0]
    first = block_index() * rows
    shift, scale, gate = modulation_rows(counts_ref, modulation_ref, first, rows)
    normed, _ = layer_norm(tokens_ref[...].astype(F32))
    hidden = (normed * (1.0 + scale) + shift).astype(BF16)
    q, k, v = (
        jnp.dot(hidden, w_qkv_ref[part], preferred_element_type=F32) for part in range(3)
    )
    d_mixed = (cotangent_ref[...].astype(F32) * gate).astype(BF16)
    d_attn = rows_dot(d_mixed, w_out_ref[...])
    low = lax.broadcasted_iota(jnp.int32, (rows, LANES), 1) < HEAD

    def beside(left, right):
        return jnp.where(low, left, right).astype(BF16)

    q_v = (beside(q, pltpu.roll(v, HEAD, 1)), beside(pltpu.roll(q, HEAD, 1), v))
    k_d = (beside(k, pltpu.roll(d_attn, HEAD, 1)), beside(pltpu.roll(k, HEAD, 1), d_attn))
    for place in range(out_ref.shape[0]):
        out_ref[place, :, 0:LANES] = q_v[place % 2]
        out_ref[place, :, LANES:] = k_d[place % 2]


def enter(counts, tokens, cotangent, w_parts, w_out, modulation, quad):
    return pl.pallas_call(
        enter_kernel,
        out_shape=jax.ShapeDtypeStruct((quad, tokens.shape[0], 2 * LANES), BF16),
        in_specs=[SMEM] + [VMEM] * 5,
        out_specs=VMEM,
        compiler_params=pltpu.CompilerParams(vmem_limit_bytes=ENTER_LIMIT),
    )(counts, tokens, cotangent, w_parts, w_out, modulation)


LOG2_E = math.log2(math.e)
INV_ROOT = 1.0 / math.sqrt(HEAD)
CHUNK = 256
TILE = 64
MAIN = 6
REACH_CHUNKS = 4


def low_lanes():
    return lax.broadcasted_iota(jnp.int32, (1, LANES), 1) < HEAD


def lower_mean(values):
    return jnp.sum(jnp.where(low_lanes(), values, 0.0), axis=-1, keepdims=True) * (1.0 / HEAD)


def lower_sums(values):
    ones = (lax.broadcasted_iota(jnp.int32, (LANES, LANES), 0) < HEAD).astype(F32).astype(BF16)
    squares = values * values
    large = squares.astype(BF16)
    small = (squares - large.astype(F32)).astype(BF16)
    large = jnp.dot(large, ones, preferred_element_type=F32)
    return large + jnp.dot(small, ones, preferred_element_type=F32)


def place_block(source, place, starts, ends, gains_ref, stores):
    low = low_lanes()
    rows = source.shape[0]
    at = place + lax.broadcasted_iota(jnp.int32, (rows, LANES), 0)
    same = ((at >= starts) & (at < ends)).astype(F32)
    first = source[:, 0:LANES].astype(F32)
    second = source[:, LANES:].astype(F32)

    def normed(raw, gain):
        mean = lower_sums(raw) * (1.0 / HEAD)
        return (raw * lax.rsqrt(mean + EPS) * gain).astype(BF16).astype(F32)

    keys = normed(second, gains_ref[1:2, :])
    queries = normed(first, gains_ref[0:1, :]) * INV_ROOT
    q_store, k_store, v_store, d_store, kv_store = stores
    q_store[...] = jnp.where(low, queries, same * SAME_IMAGE).astype(BF16)
    k_store[...] = jnp.where(low, keys, same).astype(BF16)
    v_store[...] = jnp.where(low, 0.0, first).astype(BF16)
    d_store[...] = second.astype(BF16)
    kv_store[...] = jnp.where(low, keys, first).astype(BF16).T


def window_facts(counts_ref):
    half = lax.axis_index("yh")
    origin = (block_index() // 4 - 1) * 2 * CHUNK
    own_at = (2 + half) * CHUNK
    starts, ends = image_bounds(counts_ref, HEAD)
    left_from = jnp.int32(-CHUNK)
    right_to = jnp.int32((MAIN + 1) * CHUNK)
    total = -origin
    for image in range(counts_ref.shape[0]):
        left_from = jnp.where(total <= own_at, total, left_from)
        ended = total >= own_at + CHUNK
        total = total + counts_ref[image]
        right_to = jnp.where((total >= own_at + CHUNK) & jnp.logical_not(ended), total, right_to)
    return half, own_at, starts - origin, ends - origin, left_from, right_to


def by_eight(values):
    return values.reshape(values.shape[0] // 8, 8, values.shape[1])


def add_tiles(s_ref, g_ref, rows, highest, total, grads):
    for piece in range(rows // TILE):
        at = slice(piece * TILE, (piece + 1) * TILE)
        weights = jnp.exp2(s_ref[at, :] * LOG2_E - highest)
        total = total + jnp.sum(by_eight(weights), axis=0)
        grads = grads + jnp.sum(by_eight(weights * g_ref[at, :]), axis=0)
    return total, grads


def rows_max(values):
    return jnp.max(by_eight(values), axis=0)


def near_kernel(
    counts_ref,
    gains_ref,
    first_ref,
    quad_ref,
    second_ref,
    qx_ref,
    kx_ref,
    vx_ref,
    dx_ref,
    kv_ref,
    so_ref,
    go_ref,
    sn_ref,
    gn_ref,
    stats_ref,
    s_ref,
    g_ref,
):
    half, own_at, starts, ends, left_from, right_to = window_facts(counts_ref)
    block_rows = CHUNK // 2

    def place(source, begin):
        begin = pl.multiple_of(begin, block_rows)
        at = pl.ds(begin, block_rows)
        stores = [ref.at[at, :] for ref in (qx_ref, kx_ref, vx_ref, dx_ref)]
        place_block(source, begin, starts, ends, gains_ref, stores + [kv_ref.at[:, at]])

    to_first = jnp.where(lax.rem(lax.axis_index("z"), 2) == 0, 2 * CHUNK, -2 * CHUNK)
    for block in range(4):
        at = slice(block * block_rows, (block + 1) * block_rows)
        begin = 2 * CHUNK + block * block_rows
        place(quad_ref.at[at], begin)
        place(first_ref.at[at], begin + to_first)
        place(second_ref.at[at], begin - to_first)

    own_rows = pl.ds(pl.multiple_of(own_at, CHUNK), CHUNK)
    q_own = qx_ref[own_rows, :]
    d_own = dx_ref[own_rows, :]
    highest = jnp.full((8, CHUNK), -jnp.inf, F32)
    for piece in range(MAIN):
        at = slice(piece * CHUNK, (piece + 1) * CHUNK)
        scores = rows_dot(kx_ref[at, :], q_own)
        so_ref[at, :] = scores
        highest = jnp.maximum(highest, rows_max(scores))
        go_ref[at, :] = rows_dot(vx_ref[at, :], d_own)
    stats_ref[MAIN, :, :] = highest

    left_key = jnp.clip((left_from + CHUNK) // CHUNK - 1, 0, MAIN - REACH_CHUNKS)
    right_key = jnp.clip((right_to - 1) // CHUNK - (REACH_CHUNKS - 1), 0, MAIN - REACH_CHUNKS)

    def one_chunk(step, carry):
        slot = step + jnp.where(step >= 2 + half, 1, 0)
        begin = slot * CHUNK

        @pl.when((begin < right_to) & (begin + CHUNK > left_from))
        def _():
            at = pl.ds(pl.multiple_of(begin, CHUNK), CHUNK)
            key = jnp.where(begin < own_at, left_key, right_key) * CHUNK
            q_block = qx_ref[at, :]
            d_block = dx_ref[at, :]
            highest = jnp.full((8, CHUNK), -jnp.inf, F32)
            for piece in range(REACH_CHUNKS):
                keys_at = pl.ds(pl.multiple_of(key + piece * CHUNK, CHUNK), CHUNK)
                here = slice(piece * CHUNK, (piece + 1) * CHUNK)
                scores = rows_dot(kx_ref[keys_at, :], q_block)
                s_ref[here, :] = scores
                highest = jnp.maximum(highest, rows_max(scores))
                g_ref[here, :] = rows_dot(vx_ref[keys_at, :], d_block)
            highest = jnp.max(highest, axis=0, keepdims=True) * LOG2_E
            zeros = jnp.zeros((8, CHUNK), F32)
            total, grads = add_tiles(s_ref, g_ref, REACH_CHUNKS * CHUNK, highest, zeros, zeros)
            stats_ref[slot, 0:1, :] = highest
            stats_ref[slot, 1:2, :] = jnp.sum(total, axis=0, keepdims=True)
            stats_ref[slot, 2:3, :] = jnp.sum(grads, axis=0, keepdims=True)
            near_at = pl.ds(pl.multiple_of(own_at - key, CHUNK), CHUNK)
            sn_ref[slot, :, :] = s_ref[near_at, :]
            gn_ref[slot, :, :] = g_ref[near_at, :]

        return carry

    lax.fori_loop(0, MAIN - 1, one_chunk, 0)


def attend_near(counts, gains, first, quad, second):
    rows = MAIN * CHUNK
    head_rows = jax.ShapeDtypeStruct((rows, LANES), BF16)
    scores = jax.ShapeDtypeStruct((rows, CHUNK), F32)
    tiles = jax.ShapeDtypeStruct((MAIN, CHUNK, CHUNK), F32)
    return pl.pallas_call(
        near_kernel,
        out_shape=(head_rows,) * 4
        + (jax.ShapeDtypeStruct((LANES, rows), BF16),)
        + (scores, scores, tiles, tiles, jax.ShapeDtypeStruct((MAIN + 1, 8, CHUNK), F32)),
        in_specs=[SMEM] + [VMEM] * 4,
        out_specs=(VMEM,) * 10,
        scratch_shapes=[pltpu.VMEM((REACH_CHUNKS * CHUNK, CHUNK), F32)] * 2,
        cost_estimate=pl.CostEstimate(
            flops=10000000000, bytes_accessed=1 << 20, transcendentals=1 << 20
        ),
        compiler_params=pltpu.CompilerParams(vmem_limit_bytes=VMEM_LIMIT),
    )(counts, gains, first, quad, second)


def far_kernel(
    counts_ref,
    gains_ref,
    far_ref,
    quad_ref,
    qx_ref,
    kx_ref,
    vx_ref,
    dx_ref,
    kv_ref,
    so_ref,
    go_ref,
    sn_ref,
    gn_ref,
    stats_ref,
    out_ref,
    qf_ref,
    kf_ref,
    vf_ref,
    df_ref,
    kvf_ref,
    s_ref,
    g_ref,
    p_ref,
    d_ref,
    sums_ref,
    dk_ref,
    dv_ref,
    done_ref,
):
    half, own_at, starts, ends, left_from, right_to = window_facts(counts_ref)
    block_rows = CHUNK // 2
    rows = MAIN * CHUNK
    far_at = jnp.where(half == 0, -CHUNK, rows)
    for block in range(2):
        at = slice(block * block_rows, (block + 1) * block_rows)
        stores = [ref.at[at, :] for ref in (qf_ref, kf_ref, vf_ref, df_ref)]
        place_block(
            far_ref.at[at],
            far_at + block * block_rows,
            starts,
            ends,
            gains_ref,
            stores + [kvf_ref.at[:, at]],
        )

    own_rows = pl.ds(pl.multiple_of(own_at, CHUNK), CHUNK)
    q_own = qx_ref[own_rows, :]
    d_own = dx_ref[own_rows, :]
    scores = rows_dot(kf_ref[...], q_own)
    s_ref[0:CHUNK, :] = scores
    g_ref[0:CHUNK, :] = rows_dot(vf_ref[...], d_own)
    highest = jnp.maximum(stats_ref[MAIN, :, :], rows_max(scores))
    highest = jnp.max(highest, axis=0, keepdims=True) * LOG2_E
    zeros = jnp.zeros((8, CHUNK), F32)
    total, grads = add_tiles(so_ref, go_ref, rows, highest, zeros, zeros)
    total, grads = add_tiles(s_ref, g_ref, CHUNK, highest, total, grads)
    scale = 1.0 / jnp.sum(total, axis=0, keepdims=True)
    mean_grad = jnp.sum(grads, axis=0, keepdims=True) * scale

    def write_tile(scores, grads, highest, scale, mean_grad, to):
        probs = jnp.exp2(scores * LOG2_E - highest) * scale
        p_ref[to, :] = probs.astype(BF16)
        d_ref[to, :] = (probs * (grads - mean_grad)).astype(BF16)

    for piece in range(rows // TILE):
        at = slice(piece * TILE, (piece + 1) * TILE)
        write_tile(so_ref[at, :], go_ref[at, :], highest, scale, mean_grad, at)
    for piece in range(CHUNK // TILE):
        at = slice(piece * TILE, (piece + 1) * TILE)
        to = slice(rows + piece * TILE, rows + (piece + 1) * TILE)
        write_tile(s_ref[at, :], g_ref[at, :], highest, scale, mean_grad, to)
    dk_ref[...] = jnp.dot(d_ref[own_rows, :], q_own, preferred_element_type=F32)
    dv_ref[...] = jnp.dot(p_ref[own_rows, :], d_own, preferred_element_type=F32)

    def times_window(values_ref):
        main = jnp.dot(kv_ref[...], values_ref[0:rows, :], preferred_element_type=F32)
        return main + jnp.dot(
            kvf_ref[...], values_ref[rows : rows + CHUNK, :], preferred_element_type=F32
        )

    upper = lax.broadcasted_iota(jnp.int32, (LANES, CHUNK), 0) < HEAD
    own_out = jnp.where(upper, times_window(d_ref) * INV_ROOT, times_window(p_ref)).T

    query_lane = lax.broadcasted_iota(jnp.int32, (1, CHUNK), 1)
    reaches_far = jnp.where(half == 0, left_from < 0, right_to > rows)

    def add_gradients(tiles, begin, q_block, d_block, highest, total, grads):
        place = query_lane + begin
        scale = jnp.where((place >= left_from) & (place < right_to), 1.0 / total, 0.0)
        mean_grad = grads * scale
        for piece in range(CHUNK // TILE):
            scores, given = tiles(piece)
            at = slice(piece * TILE, (piece + 1) * TILE)
            write_tile(scores, given, highest, scale, mean_grad, at)
        dk_ref[...] += jnp.dot(d_ref[0:CHUNK, :], q_block, preferred_element_type=F32)
        dv_ref[...] += jnp.dot(p_ref[0:CHUNK, :], d_block, preferred_element_type=F32)

    def one_chunk(step, carry):
        slot = step + jnp.where(step >= 2 + half, 1, 0)
        begin = slot * CHUNK

        @pl.when((begin < right_to) & (begin + CHUNK > left_from))
        def _():
            at = pl.ds(pl.multiple_of(begin, CHUNK), CHUNK)
            q_block = qx_ref[at, :]
            d_block = dx_ref[at, :]
            sums_ref[...] = stats_ref[slot, :, :]
            same_side = (begin < own_at) == (half == 0)

            @pl.when(reaches_far & same_side)
            def _():
                scores = rows_dot(kf_ref[...], q_block)
                s_ref[0:CHUNK, :] = scores
                g_ref[0:CHUNK, :] = rows_dot(vf_ref[...], d_block)
                before = sums_ref[0:1, :]
                highest = jnp.max(rows_max(scores), axis=0, keepdims=True) * LOG2_E
                highest = jnp.maximum(before, highest)
                total, grads = add_tiles(s_ref, g_ref, CHUNK, highest, zeros, zeros)
                shrink = jnp.exp2(before - highest)
                sums_ref[0:1, :] = highest
                total = jnp.sum(total, axis=0, keepdims=True)
                grads = jnp.sum(grads, axis=0, keepdims=True)
                sums_ref[1:2, :] = sums_ref[1:2, :] * shrink + total
                sums_ref[2:3, :] = sums_ref[2:3, :] * shrink + grads

            def tiles(piece):
                at = slice(piece * TILE, (piece + 1) * TILE)
                return sn_ref[slot, at, :], gn_ref[slot, at, :]

            add_gradients(
                tiles, begin, q_block, d_block, sums_ref[0:1, :], sums_ref[1:2, :], sums_ref[2:3, :]
            )

        return carry

    lax.fori_loop(0, MAIN - 1, one_chunk, 0)

    @pl.when(reaches_far)
    def _():
        q_block = qf_ref[...]
        d_block = df_ref[...]
        key = half * (MAIN // 2) * CHUNK
        highest = jnp.full((8, CHUNK), -jnp.inf, F32)
        for piece in range(REACH_CHUNKS):
            here = slice(piece * CHUNK, (piece + 1) * CHUNK)
            if piece < REACH_CHUNKS - 1:
                keys_at = pl.ds(pl.multiple_of(key + piece * CHUNK, CHUNK), CHUNK)
                keys, values = kx_ref[keys_at, :], vx_ref[keys_at, :]
            else:
                keys, values = kf_ref[...], vf_ref[...]
            scores = rows_dot(keys, q_block)
            s_ref[here, :] = scores
            highest = jnp.maximum(highest, rows_max(scores))
            g_ref[here, :] = rows_dot(values, d_block)
        highest = jnp.max(highest, axis=0, keepdims=True) * LOG2_E
        total, grads = add_tiles(s_ref, g_ref, REACH_CHUNKS * CHUNK, highest, zeros, zeros)

        def tiles(piece):
            at = pl.ds(pl.multiple_of(own_at - key + piece * TILE, TILE), TILE)
            return s_ref[at, :], g_ref[at, :]

        add_gradients(
            tiles,
            far_at,
            q_block,
            d_block,
            highest,
            jnp.sum(total, axis=0, keepdims=True),
            jnp.sum(grads, axis=0, keepdims=True),
        )

    def norm_grad(raw, gain, d_norm):
        inverse = lax.rsqrt(lower_mean(raw * raw) + EPS)
        scaled = d_norm.astype(BF16).astype(F32) * gain
        inner = lower_mean(raw * scaled)
        return inverse * scaled - raw * (inverse * inverse * inverse * inner)

    low = low_lanes()
    own_in_quad = pl.ds(pl.multiple_of(half * CHUNK, CHUNK), CHUNK)
    raw_q = quad_ref[own_in_quad, 0:LANES].astype(F32)
    raw_k = quad_ref[own_in_quad, LANES:].astype(F32)
    d_q = norm_grad(raw_q, gains_ref[0:1, :], own_out)
    d_k = norm_grad(raw_k, gains_ref[1:2, :], dk_ref[...])
    done_ref[:, 0:LANES] = jnp.where(low, d_q, own_out).astype(BF16)
    done_ref[:, LANES:] = jnp.where(low, d_k, dv_ref[...]).astype(BF16)
    share = 16
    for member in range(out_ref.shape[0]):
        block, core = member // 2, member % 2
        for part in range(out_ref.shape[1] // share):
            begin = (block * 8 + part * 2 + core) * share
            out_ref[member, part * share : (part + 1) * share, :] = done_ref[
                begin : begin + share, :
            ]


def attend_far(counts, gains, far, quad, near_parts):
    return pl.pallas_call(
        far_kernel,
        out_shape=jax.ShapeDtypeStruct((4, CHUNK // 4, 2 * LANES), BF16),
        in_specs=[SMEM] + [VMEM] * (3 + len(near_parts)),
        out_specs=VMEM,
        scratch_shapes=[pltpu.VMEM((CHUNK, LANES), BF16)] * 4
        + [pltpu.VMEM((LANES, CHUNK), BF16)]
        + [pltpu.VMEM((REACH_CHUNKS * CHUNK, CHUNK), F32)] * 2
        + [pltpu.VMEM(((MAIN + 1) * CHUNK, CHUNK), BF16)] * 2
        + [pltpu.VMEM((8, CHUNK), F32)]
        + [pltpu.VMEM((CHUNK, LANES), F32)] * 2
        + [pltpu.VMEM((CHUNK, 2 * LANES), BF16)],
        cost_estimate=pl.CostEstimate(
            flops=10000000000, bytes_accessed=1 << 20, transcendentals=1 << 20
        ),
        compiler_params=pltpu.CompilerParams(vmem_limit_bytes=VMEM_LIMIT),
    )(counts, gains, far, quad, *near_parts)


def project_kernel(parts_ref, w_out_ref, w_qkv_ref, w_out_far_ref, w_qkv_far_ref, out_ref):
    rows = parts_ref.shape[1]
    width = w_out_ref.shape[1]
    share = out_ref.shape[1]
    core = lax.axis_index("core")
    low = lax.broadcasted_iota(jnp.int32, (rows, LANES), 1) < HEAD

    def products(which, w_out, w_qkv):
        head0 = parts_ref[which].astype(F32)
        head1 = parts_ref[2 + which].astype(F32)
        a0, a1 = head0[:, :LANES], head1[:, :LANES]
        b0, b1 = head0[:, LANES:], head1[:, LANES:]
        d_q = jnp.where(low, a0, pltpu.roll(a1, HEAD, 1)).astype(BF16)
        attn = jnp.where(low, pltpu.roll(a0, HEAD, 1), a1).astype(BF16)
        d_k = jnp.where(low, b0, pltpu.roll(b1, HEAD, 1)).astype(BF16)
        d_v = jnp.where(low, pltpu.roll(b0, HEAD, 1), b1).astype(BF16)
        mixed = jnp.dot(attn, w_out[...], preferred_element_type=F32)
        d_hidden = rows_dot(d_q, w_qkv[0]) + rows_dot(d_k, w_qkv[1]) + rows_dot(d_v, w_qkv[2])
        return mixed, d_hidden

    mixed, d_hidden = products(core, w_out_ref, w_qkv_ref)
    mixed_far, d_hidden_far = products(1 - core, w_out_far_ref, w_qkv_far_ref)
    mixed = (mixed + mixed_far).astype(BF16)
    d_hidden = (d_hidden + d_hidden_far).astype(BF16)
    for place in range(out_ref.shape[0]):
        at = slice(place * share, (place + 1) * share)
        out_ref[place, :, :width] = mixed[at]
        out_ref[place, :, width:] = d_hidden[at]


def project(parts, w_out, w_parts, w_out_far, w_parts_far, x_count):
    return pl.pallas_call(
        project_kernel,
        out_shape=jax.ShapeDtypeStruct(
            (x_count, parts.shape[1] // x_count, 2 * w_out.shape[1]), BF16
        ),
        in_specs=[VMEM] * 5,
        out_specs=VMEM,
        compiler_params=pltpu.CompilerParams(vmem_limit_bytes=VMEM_LIMIT),
    )(parts, w_out, w_parts, w_out_far, w_parts_far)


def ready_kernel(
    counts_ref,
    tokens_ref,
    cotangent_ref,
    modulation_ref,
    rows_ref,
    factors_ref,
):
    rows = rows_ref.shape[1]
    first_row = (lax.axis_index("x") * 2 + lax.axis_index("core")) * rows
    first = block_index() * tokens_ref.shape[0] + first_row
    _, scale, gate = modulation_rows(counts_ref, modulation_ref, first, rows)
    at = pl.ds(pl.multiple_of(first_row, rows), rows)
    normed, inv_std = layer_norm(tokens_ref[at, :].astype(F32))
    rows_ref[0] = tokens_ref[at, :]
    rows_ref[1] = cotangent_ref[at, :]
    factors_ref[0] = gate
    factors_ref[1] = 1.0 + scale
    factors_ref[2] = normed
    factors_ref[3] = jnp.broadcast_to(inv_std, normed.shape)


def ready(counts, tokens, cotangent, modulation, share):
    width = tokens.shape[1]
    return pl.pallas_call(
        ready_kernel,
        out_shape=(
            jax.ShapeDtypeStruct((2, share, width), BF16),
            jax.ShapeDtypeStruct((4, share, width), F32),
        ),
        in_specs=[SMEM] + [VMEM] * 3,
        out_specs=(VMEM, VMEM),
        compiler_params=pltpu.CompilerParams(vmem_limit_bytes=VMEM_LIMIT),
    )(counts, tokens, cotangent, modulation)


def leave_kernel(rows_ref, factors_ref, shares_ref, layer_ref, grad_ref):
    width = layer_ref.shape[1]
    sums = shares_ref[0].astype(F32)
    for share in range(1, shares_ref.shape[0]):
        sums = sums + shares_ref[share].astype(F32)
    layer = rows_ref[0].astype(F32) + factors_ref[0] * sums[:, :width]
    layer_ref[...] = layer.astype(BF16)
    d_normed = sums[:, width:] * factors_ref[1]
    normed = factors_ref[2]
    input_grad = rows_ref[1].astype(F32) + factors_ref[3] * (
        d_normed
        - jnp.mean(d_normed, axis=-1, keepdims=True)
        - normed * jnp.mean(d_normed * normed, axis=-1, keepdims=True)
    )
    grad_ref[...] = input_grad.astype(BF16)


def leave(rows, factors, shares):
    out = jax.ShapeDtypeStruct(rows.shape[1:], BF16)
    return pl.pallas_call(
        leave_kernel,
        out_shape=(out, out),
        in_specs=[VMEM] * 3,
        out_specs=(VMEM, VMEM),
        compiler_params=pltpu.CompilerParams(vmem_limit_bytes=VMEM_LIMIT),
    )(rows, factors, shares)


def per_device(tokens, cotangent, w_qkv, w_out, qk_gain, modulation, image_counts):
    tok_rows, model_width = tokens.shape
    z_count = lax.axis_size("z")
    x_count = lax.axis_size("x")
    quad = 4
    pair_rows = 2 * tok_rows
    share = tok_rows // (2 * x_count)
    w_parts = w_qkv.transpose(1, 0, 2)
    mod_parts = modulation.transpose(1, 0, 2)
    gains = jnp.pad(qk_gain, ((0, 6), (0, LANES - HEAD)))

    heads = enter(image_counts, tokens, cotangent, w_parts, w_out, mod_parts, quad)
    mine = lax.all_to_all(heads, ("yh", "yl"), 0, 0)
    mine = mine.reshape(quad * tok_rows, 2 * LANES)
    evens = range(0, z_count, 2)
    swaps = [(i, i + 1) for i in evens], [((i - 1) % z_count, i) for i in evens]
    first, second = (
        lax.ppermute(mine, "z", pairs + [(j, i) for i, j in pairs]) for pairs in swaps
    )
    far_half = jnp.where(lax.axis_index("yh") == 0, mine[pair_rows:], mine[:pair_rows])
    halves = 2 * z_count
    far = lax.ppermute(
        far_half,
        ("z", "yh"),
        [(i, (i + (4 if i % 2 == 0 else -4)) % halves) for i in range(halves)],
    )
    _, tokens_late, cotangent_late, mod_late = lax.optimization_barrier(
        (mine, tokens, cotangent, mod_parts)
    )
    rows, factors = ready(image_counts, tokens_late, cotangent_late, mod_late, share)
    near_parts = attend_near(image_counts, gains, first, mine, second)
    _, _, w_parts_late, w_out_late = lax.optimization_barrier((mine, mine, w_parts, w_out))
    w_parts_far, w_out_far = (
        lax.ppermute(w, "core", [(0, 1), (1, 0)]) for w in (w_parts_late, w_out_late)
    )
    parts = attend_far(image_counts, gains, far, mine, near_parts)
    parts = lax.all_to_all(parts, ("yl", "core"), 0, 0)
    partial = project(parts, w_out, w_parts, w_out_far, w_parts_far, x_count)
    shares = lax.all_to_all(partial, "x", 0, 0)
    return leave(rows, factors, shares)


def solution(mesh):
    split = jax.sharding.Mesh(mesh.devices.reshape(16, 2, 2, 4, 2), ("z", "yh", "yl", "x", "core"))
    dp, head = ("z", "yh", "yl"), ("x", "core")
    in_specs = (P(dp, None), P(dp, None), P(None, None, head), P(head, None), P(), P(), P())
    out_specs = (P(dp + head, None), P(dp + head, None))
    return jax.shard_map(
        per_device, mesh=split, in_specs=in_specs, out_specs=out_specs, check_vma=False
    )
```

profile of v0, /device:TPU:16, one launch (start us, length us, event | category | flops | bytes accessed | tf_op | source)
XLA Modules:
  0.0 66.9 jit_solution(8075967110011036786)
XLA Ops:
  0.6 0.0 copy-start.6
  0.6 0.0 copy-start
  0.7 0.0 copy-start.1
  0.7 0.0 copy-start.5
  0.7 3.5 %shard_map.86 = bf16[4,128,256]{2,1,0:T(8,128)(2,1)} custom-call(s32[32]{0:T(128)} %counts_ref.7, bf16[128,1536]{1,0:T(8,128)(2,1)} %tokens_ref.2, bf16[128,1536]{1,0:T(8,128)(2,1)} %cotangent_ref.2, bf16[3,1536,128]{2,1,0:T(8,128)(2,1)} %bitcast.4, bf16[128,1536]{1,0:T(8,128)(2,1)} %w_out_ref.3, bf16[3,32,1536]{2,1,0:T(8,128)(2,1)} %bitcast.7), custom_call_target="tpu_custom_call" | custom-call | tf_op jit(solution)/shard_map/pallas_call | solution.py:86
  4.2 13.1 %all_to_all.15 = bf16[4,128,256]{2,1,0:T(8,128)(2,1)S(1)} all-to-all(bf16[4,128,256]{2,1,0:T(8,128)(2,1)} %shard_map.86), channel_id=1, replica_groups=mesh['z'=16,'yh'=2,'yl'=2,'x'=4,'core'=2] {'yh','yl'}, dimensions={0} | all-to-all | bytes 524288 | tf_op jit(solution)/shard_map/all_to_all | solution.py:613
  17.2 1.9 %collective-permute-start.1 = (bf16[512,256]{1,0:T(8,128)(2,1)S(1)}, bf16[512,256]{1,0:T(8,128)(2,1)S(1)}, u32[]{:S(2)}, u32[]{:S(2)}) collective-permute-start(bf16[512,256]{1,0:T(8,128)(2,1)S(1)} %bitcast.9), channel_id=1, source_target_pairs={{0,32},{64,96},{128,160},{192,224},{256,288},{320,352},{384,416},{... | collective-permute-start | bytes 786440 | tf_op jit(solution)/shard_map/ppermute | solution.py:618
  19.2 8.1 %collective-permute-start.2 = (bf16[512,256]{1,0:T(8,128)(2,1)S(1)}, bf16[512,256]{1,0:T(8,128)(2,1)S(1)}, u32[]{:S(2)}, u32[]{:S(2)}) collective-permute-start(bf16[512,256]{1,0:T(8,128)(2,1)S(1)} %bitcast.10), channel_id=1, source_target_pairs={{480,0},{32,64},{96,128},{160,192},{224,256},{288,320},{352,384},{... | collective-permute-start | bytes 786440 | tf_op jit(solution)/shard_map/ppermute | solution.py:618
  27.3 0.0 copy-done.6
  27.3 3.4 %collective-permute-start = (bf16[256,256]{1,0:T(8,128)(2,1)S(1)}, bf16[256,256]{1,0:T(8,128)(2,1)S(1)}, u32[]{:S(2)}, u32[]{:S(2)}) collective-permute-start(bf16[256,256]{1,0:T(8,128)(2,1)S(1)} %bitcast.13), channel_id=1, source_target_pairs={{0,64},{16,464},{32,96},{48,496},{64,128},{80,16},{96,160},{112,48... | collective-permute-start | bytes 393224 | tf_op jit(solution)/shard_map/ppermute | solution.py:622
  30.7 0.0 copy-done
  30.7 1.9 %collective-permute-start.4 = (bf16[3,1536,128]{2,1,0:T(8,128)(2,1)S(1)}, bf16[3,1536,128]{2,1,0:T(8,128)(2,1)S(1)}, u32[]{:S(2)}, u32[]{:S(2)}) collective-permute-start(bf16[3,1536,128]{2,1,0:T(8,128)(2,1)S(1)} %bitcast.5), channel_id=1, source_target_pairs={{0,1},{1,0},{2,3},{3,2},{4,5},{5,4},{6,7},{7,6},{8,9},{9,8},{10,11... | collective-permute-start | bytes 3538952 | tf_op jit(solution)/shard_map/ppermute | solution.py:634
  32.6 0.0 copy-done.1
  32.7 2.4 %collective-permute-start.3 = (bf16[128,1536]{1,0:T(8,128)(2,1)S(1)}, bf16[128,1536]{1,0:T(8,128)(2,1)S(1)}, u32[]{:S(2)}, u32[]{:S(2)}) collective-permute-start(bf16[128,1536]{1,0:T(8,128)(2,1)S(1)} %copy-done.1), channel_id=1, source_target_pairs={{0,1},{1,0},{2,3},{3,2},{4,5},{5,4},{6,7},{7,6},{8,9},{9,8},{10,11... | collective-permute-start | bytes 1179656 | tf_op jit(solution)/shard_map/ppermute | solution.py:634
  35.1 0.0 collective-permute-done.1.first_ref
  35.1 0.6 collective-permute-done.2.second_ref
  35.7 0.0 copy-done.5
  35.7 4.3 %shard_map.88 = (bf16[1536,128]{1,0:T(8,128)(2,1)S(1)}, bf16[1536,128]{1,0:T(8,128)(2,1)S(1)}, bf16[1536,128]{1,0:T(8,128)(2,1)S(1)}, bf16[1536,128]{1,0:T(8,128...) custom-call(s32[32]{0:T(128)S(1)} %copy-done.5, ...), custom_call_target="tpu_custom_call" | custom-call | flops 10000000000 | bytes 1048576 | tf_op jit(solution)/shard_map/pallas_call | solution.py:264
  40.0 0.0 collective-permute-done.far_ref
  40.0 5.0 %shard_map.89 = bf16[4,64,256]{2,1,0:T(8,128)(2,1)S(1)} custom-call(s32[32]{0:T(128)S(1)} %copy-done.5, f32[8,128]{1,0:T(8,128)S(1)} %pad.4.gains_ref, bf16[256,256]{1,0:T(8,128)(2,1)S(1)} %collective-permute-done.far_ref, bf16[512,256]{1,0:T(8,128)(2,1)S(1)} %bitcast.12, bf16[1536,128]{1,0:T(8,128)(2,1)S(1)} %get-tuple-element.24.qx_ref, ...), custom_call_target="tpu_custom_call" | custom-call | flops 10000000000 | bytes 1048576 | tf_op jit(solution)/shard_map/pallas_call | solution.py:476
  45.0 7.3 %all_to_all.16.parts_ref = bf16[4,64,256]{2,1,0:T(8,128)(2,1)S(1)} all-to-all(bf16[4,64,256]{2,1,0:T(8,128)(2,1)S(1)} %shard_map.89), channel_id=1, replica_groups=mesh['z'=16,'yh'=2,'yl'=2,'x'=4,'core'=2] {'yl','core'}, dimensions={0} | all-to-all | bytes 262144 | tf_op jit(solution)/shard_map/all_to_all | solution.py:637
  52.3 0.0 copy-start.2
  52.3 0.0 copy-start.3
  52.3 0.0 copy-start.4
  52.3 0.0 collective-permute-done.3.w_out_far_ref
  52.3 0.0 collective-permute-done.4.w_qkv_far_ref
  52.3 1.9 %shard_map.90 = bf16[4,16,3072]{2,1,0:T(8,128)(2,1)} custom-call(bf16[4,64,256]{2,1,0:T(8,128)(2,1)S(1)} %all_to_all.16.parts_ref, bf16[128,1536]{1,0:T(8,128)(2,1)S(1)} %copy-done.1, bf16[3,1536,128]{2,1,0:T(8,128)(2,1)S(1)} %bitcast.6, bf16[128,1536]{1,0:T(8,128)(2,1)S(1)} %collective-permute-done.3.w_out_far_ref, ...), custom_call_target="tpu_custom_call" | custom-call | tf_op jit(solution)/shard_map/pallas_call | solution.py:526
  54.2 4.3 %all-to-all-start.2 = ((bf16[4,16,3072]{2,1,0:T(8,128)(2,1)}), bf16[4,16,3072]{2,1,0:T(8,128)(2,1)S(1)}, u32[]{:S(2)}, u32[]{:S(2)}) async-start(bf16[4,16,3072]{2,1,0:T(8,128)(2,1)} %shard_map.90), calls=%async_computation.2 | async-start | bytes 786432 | tf_op jit(solution)/shard_map/all_to_all | solution.py:639
  58.5 0.0 copy-done.2
  58.5 0.0 copy-done.3
  58.5 0.0 copy-done.4
  58.5 0.8 %shard_map.87 = (bf16[2,16,1536]{2,1,0:T(8,128)(2,1)S(1)}, f32[4,16,1536]{2,1,0:T(8,128)S(1)}) custom-call(s32[32]{0:T(128)S(1)} %copy-done.5, bf16[128,1536]{1,0:T(8,128)(2,1)S(1)} %copy-done.2, bf16[128,1536]{1,0:T(8,128)(2,1)S(1)} %copy-done.3, bf16[3,32,1536]{2,1,0:T(8,128)(2,1)S(1)} %bitcast.8), custom_call_target="tpu_custom_call" | custom-call | tf_op jit(solution)/shard_map/pallas_call | solution.py:561
  59.3 6.9 %all-to-all-done.2.shares_ref = bf16[4,16,3072]{2,1,0:T(8,128)(2,1)S(1)} async-done(((bf16[4,16,3072]{2,1,0:T(8,128)(2,1)}), bf16[4,16,3072]{2,1,0:T(8,128)(2,1)S(1)}, u32[]{:S(2)}, u32[]{:S(2)}) %all-to-all-start.2) | async-done | bytes 393248 | tf_op jit(solution)/shard_map/all_to_all | solution.py:639
  66.2 0.7 %shard_map.91 = (bf16[16,1536]{1,0:T(8,128)(2,1)}, bf16[16,1536]{1,0:T(8,128)(2,1)}) custom-call(bf16[2,16,1536]{2,1,0:T(8,128)(2,1)S(1)} %get-tuple-element.22.rows_ref, f32[4,16,1536]{2,1,0:T(8,128)S(1)} %get-tuple-element.23.factors_ref, bf16[4,16,3072]{2,1,0:T(8,128)(2,1)S(1)} %all-to-all-done.2.shares_ref), custom_call_target="tpu_custom_call" | custom-call | tf_op jit(solution)/shard_map/pallas_call | solution.py:592
  (2 shorter events, 0.0 us)
Async XLA Ops:
  0.6 26.7 %copy-start.6 = (f32[2,64]{1,0:T(2,128)S(1)}, f32[2,64]{1,0:T(2,128)}, u32[]{:S(2)}) copy-start(f32[2,64]{1,0:T(2,128)} %param.11) | copy-start | bytes 1540
  0.6 30.1 %copy-start = (bf16[1536,3,128]{2,0,1:T(8,128)(2,1)S(1)}, bf16[1536,3,128]{2,0,1:T(8,128)(2,1)}, u32[]{:S(2)}) copy-start(bf16[1536,3,128]{2,0,1:T(8,128)(2,1)} %param.9) | copy-start | bytes 3538948
  0.7 32.0 %copy-start.1 = (bf16[128,1536]{1,0:T(8,128)(2,1)S(1)}, bf16[128,1536]{1,0:T(8,128)(2,1)}, u32[]{:S(2)}) copy-start(bf16[128,1536]{1,0:T(8,128)(2,1)} %w_out_ref.3) | copy-start | bytes 1179652
  0.7 35.0 %copy-start.5 = (s32[32]{0:T(128)S(1)}, s32[32]{0:T(128)}, u32[]{:S(2)}) copy-start(s32[32]{0:T(128)} %counts_ref.7) | copy-start | bytes 388
  17.2 17.8 %collective-permute-start.1 = (bf16[512,256]{1,0:T(8,128)(2,1)S(1)}, bf16[512,256]{1,0:T(8,128)(2,1)S(1)}, u32[]{:S(2)}, u32[]{:S(2)}) collective-permute-start(bf16[512,256]{1,0:T(8,128)(2,1)S(1)} %bitcast.9), channel_id=1, source_target_pairs={{0,32},{64,96},{128,160},{192,224},{256,288},{320,352},{384,416},{... | collective-permute-start | bytes 786440 | tf_op jit(solution)/shard_map/ppermute | solution.py:618
  19.2 16.5 %collective-permute-start.2 = (bf16[512,256]{1,0:T(8,128)(2,1)S(1)}, bf16[512,256]{1,0:T(8,128)(2,1)S(1)}, u32[]{:S(2)}, u32[]{:S(2)}) collective-permute-start(bf16[512,256]{1,0:T(8,128)(2,1)S(1)} %bitcast.10), channel_id=1, source_target_pairs={{480,0},{32,64},{96,128},{160,192},{224,256},{288,320},{352,384},{... | collective-permute-start | bytes 786440 | tf_op jit(solution)/shard_map/ppermute | solution.py:618
  27.3 12.6 %collective-permute-start = (bf16[256,256]{1,0:T(8,128)(2,1)S(1)}, bf16[256,256]{1,0:T(8,128)(2,1)S(1)}, u32[]{:S(2)}, u32[]{:S(2)}) collective-permute-start(bf16[256,256]{1,0:T(8,128)(2,1)S(1)} %bitcast.13), channel_id=1, source_target_pairs={{0,64},{16,464},{32,96},{48,496},{64,128},{80,16},{96,160},{112,48... | collective-permute-start | bytes 393224 | tf_op jit(solution)/shard_map/ppermute | solution.py:622
  30.7 21.6 %collective-permute-start.4 = (bf16[3,1536,128]{2,1,0:T(8,128)(2,1)S(1)}, bf16[3,1536,128]{2,1,0:T(8,128)(2,1)S(1)}, u32[]{:S(2)}, u32[]{:S(2)}) collective-permute-start(bf16[3,1536,128]{2,1,0:T(8,128)(2,1)S(1)} %bitcast.5), channel_id=1, source_target_pairs={{0,1},{1,0},{2,3},{3,2},{4,5},{5,4},{6,7},{7,6},{8,9},{9,8},{10,11... | collective-permute-start | bytes 3538952 | tf_op jit(solution)/shard_map/ppermute | solution.py:634
  32.7 19.6 %collective-permute-start.3 = (bf16[128,1536]{1,0:T(8,128)(2,1)S(1)}, bf16[128,1536]{1,0:T(8,128)(2,1)S(1)}, u32[]{:S(2)}, u32[]{:S(2)}) collective-permute-start(bf16[128,1536]{1,0:T(8,128)(2,1)S(1)} %copy-done.1), channel_id=1, source_target_pairs={{0,1},{1,0},{2,3},{3,2},{4,5},{5,4},{6,7},{7,6},{8,9},{9,8},{10,11... | collective-permute-start | bytes 1179656 | tf_op jit(solution)/shard_map/ppermute | solution.py:634
  52.3 6.2 %copy-start.2 = (bf16[128,1536]{1,0:T(8,128)(2,1)S(1)}, bf16[128,1536]{1,0:T(8,128)(2,1)}, u32[]{:S(2)}) copy-start(bf16[128,1536]{1,0:T(8,128)(2,1)} %tokens_ref.2) | copy-start | bytes 1179652
  52.3 6.2 %copy-start.3 = (bf16[128,1536]{1,0:T(8,128)(2,1)S(1)}, bf16[128,1536]{1,0:T(8,128)(2,1)}, u32[]{:S(2)}) copy-start(bf16[128,1536]{1,0:T(8,128)(2,1)} %cotangent_ref.2) | copy-start | bytes 1179652
  52.3 6.2 %copy-start.4 = (bf16[32,3,1536]{2,0,1:T(8,128)(2,1)S(1)}, bf16[32,3,1536]{2,0,1:T(8,128)(2,1)}, u32[]{:S(2)}) copy-start(bf16[32,3,1536]{2,0,1:T(8,128)(2,1)} %param.12) | copy-start | bytes 884740
  54.2 12.0 %all-to-all-start.2 = ((bf16[4,16,3072]{2,1,0:T(8,128)(2,1)}), bf16[4,16,3072]{2,1,0:T(8,128)(2,1)S(1)}, u32[]{:S(2)}, u32[]{:S(2)}) async-start(bf16[4,16,3072]{2,1,0:T(8,128)(2,1)} %shard_map.90), calls=%async_computation.2 | async-start | bytes 786432 | tf_op jit(solution)/shard_map/all_to_all | solution.py:639
where the time goes:
time: 67.3 us; the launch traced here: 66.9 us
  starting transfers between devices  22 us (33%)
  blocking collectives  20.3 us (30%)
  Pallas kernels  16.3 us (24%)
  waiting for transfers between devices  7.49 us (11%)
  between operations  0.81 us (1%)
    all_to_all x1, blocking collectives, per_device(): mine = lax.all_to_all(heads, ('yh', 'yl'), 0, 0)  13.1 us
    ppermute x2, starting transfers between devices, per_device(): lax.ppermute(mine, 'z', pairs + [(j, i) for i, j in pairs])  10 us
    all_to_all x1, blocking collectives, per_device(): parts = lax.all_to_all(parts, ('yl', 'core'), 0, 0)  7.26 us
    all_to_all x1, waiting for transfers between devices, per_device(): shares = lax.all_to_all(partial, 'x', 0, 0)  6.91 us
    pallas_call x1, Pallas kernels, attend_far(): pl.pallas_call(far_kernel, out_shape=jax.ShapeDtypeStruct((4, CHUNK // 4,...  5.04 us
    ppermute x2, starting transfers between devices, per_device(): lax.ppermute(w, 'core', [(0, 1), (1, 0)])  4.33 us
    pallas_call x1, Pallas kernels, attend_near(): pl.pallas_call(near_kernel, out_shape=(head_rows,) * 4 + (jax.ShapeDtypeS...  4.31 us
    all_to_all x1, starting transfers between devices, per_device(): shares = lax.all_to_all(partial, 'x', 0, 0)  4.29 us
  transfers between devices with their start and end apart: 6, of which 2 were waited for; matrix products, arithmetic and copies ran while one was open for 0% of the time, Pallas kernels for 15%

commit v1 on v0

--- a/solution.py
+++ b/solution.py
@@ -65,9 +65,9 @@
     shift, scale, gate = modulation_rows(counts_ref, modulation_ref, first, rows)
     normed, _ = layer_norm(tokens_ref[...].astype(F32))
     hidden = (normed * (1.0 + scale) + shift).astype(BF16)
-    q, k, v = (
-        jnp.dot(hidden, w_qkv_ref[part], preferred_element_type=F32) for part in range(3)
-    )
+    weights = jnp.concatenate([w_qkv_ref[part] for part in range(3)], axis=1)
+    qkv = jnp.dot(hidden, weights, preferred_element_type=F32)
+    q, k, v = (qkv[:, part * LANES : (part + 1) * LANES] for part in range(3))
     d_mixed = (cotangent_ref[...].astype(F32) * gate).astype(BF16)
     d_attn = rows_dot(d_mixed, w_out_ref[...])
     low = lax.broadcasted_iota(jnp.int32, (rows, LANES), 1) < HEAD
@@ -126,16 +126,15 @@
     second = source[:, LANES:].astype(F32)
 
     def normed(raw, gain):
-        mean = lower_sums(raw) * (1.0 / HEAD)
-        return (raw * lax.rsqrt(mean + EPS) * gain).astype(BF16).astype(F32)
+        return raw * lax.rsqrt(lower_sums(raw) * (1.0 / HEAD) + EPS) * gain
 
     keys = normed(second, gains_ref[1:2, :])
-    queries = normed(first, gains_ref[0:1, :]) * INV_ROOT
+    queries = normed(first, gains_ref[0:1, :] * INV_ROOT)
     q_store, k_store, v_store, d_store, kv_store = stores
     q_store[...] = jnp.where(low, queries, same * SAME_IMAGE).astype(BF16)
     k_store[...] = jnp.where(low, keys, same).astype(BF16)
     v_store[...] = jnp.where(low, 0.0, first).astype(BF16)
-    d_store[...] = second.astype(BF16)
+    d_store[...] = source[:, LANES:]
     kv_store[...] = jnp.where(low, keys, first).astype(BF16).T
 
 
@@ -499,7 +498,7 @@
     core = lax.axis_index("core")
     low = lax.broadcasted_iota(jnp.int32, (rows, LANES), 1) < HEAD
 
-    def products(which, w_out, w_qkv):
+    def by_column(which):
         head0 = parts_ref[which].astype(F32)
         head1 = parts_ref[2 + which].astype(F32)
         a0, a1 = head0[:, :LANES], head1[:, :LANES]
@@ -508,14 +507,19 @@
         attn = jnp.where(low, pltpu.roll(a0, HEAD, 1), a1).astype(BF16)
         d_k = jnp.where(low, b0, pltpu.roll(b1, HEAD, 1)).astype(BF16)
         d_v = jnp.where(low, pltpu.roll(b0, HEAD, 1), b1).astype(BF16)
-        mixed = jnp.dot(attn, w_out[...], preferred_element_type=F32)
-        d_hidden = rows_dot(d_q, w_qkv[0]) + rows_dot(d_k, w_qkv[1]) + rows_dot(d_v, w_qkv[2])
-        return mixed, d_hidden
-
-    mixed, d_hidden = products(core, w_out_ref, w_qkv_ref)
-    mixed_far, d_hidden_far = products(1 - core, w_out_far_ref, w_qkv_far_ref)
-    mixed = (mixed + mixed_far).astype(BF16)
-    d_hidden = (d_hidden + d_hidden_far).astype(BF16)
+        return attn, [d_q, d_k, d_v]
+
+    attn, grads = by_column(core)
+    attn_far, grads_far = by_column(1 - core)
+    mixed = jnp.dot(
+        jnp.concatenate([attn, attn_far], axis=1),
+        jnp.concatenate([w_out_ref[...], w_out_far_ref[...]], axis=0),
+        preferred_element_type=F32,
+    ).astype(BF16)
+    weights = [ref[part] for ref in (w_qkv_ref, w_qkv_far_ref) for part in range(3)]
+    d_hidden = rows_dot(
+        jnp.concatenate(grads + grads_far, axis=1), jnp.concatenate(weights, axis=1)
+    ).astype(BF16)
     for place in range(out_ref.shape[0]):
         at = slice(place * share, (place + 1) * share)
         out_ref[place, :, :width] = mixed[at]
@@ -617,12 +621,17 @@
     first, second = (
         lax.ppermute(mine, "z", pairs + [(j, i) for i, j in pairs]) for pairs in swaps
     )
-    far_half = jnp.where(lax.axis_index("yh") == 0, mine[pair_rows:], mine[:pair_rows])
-    halves = 2 * z_count
+    halves = 4 * z_count
+    far_half = jnp.where(
+        lax.axis_index("yh") == lax.axis_index("core"), mine[pair_rows:], mine[:pair_rows]
+    )
+
+    def far_source(target):
+        z, yh, core = target // 4, target // 2 % 2, target % 2
+        return (z + (2 if yh else -2)) % z_count * 4 + (yh ^ core) * 2 + core
+
     far = lax.ppermute(
-        far_half,
-        ("z", "yh"),
-        [(i, (i + (4 if i % 2 == 0 else -4)) % halves) for i in range(halves)],
+        far_half, ("z", "yh", "core"), [(far_source(i), i) for i in range(halves)]
     )
     _, tokens_late, cotangent_late, mod_late = lax.optimization_barrier(
         (mine, tokens, cotangent, mod_parts)

time: 67.3 us -> 67.1 us (level)
  the two profiles are of different devices: /device:TPU:16 before, /device:TPU:48 now
where the time goes in v1:
time: 67.1 us; the launch traced here: 66.7 us
  starting transfers between devices  24.4 us (36%)
  Pallas kernels  18.2 us (27%)
  blocking collectives  16.3 us (24%)
  waiting for transfers between devices  6.94 us (10%)
  between operations  0.82 us (1%)
    all_to_all x1, blocking collectives, per_device(): mine = lax.all_to_all(heads, ('yh', 'yl'), 0, 0)  8.77 us
    ppermute x2, starting transfers between devices, per_device(): lax.ppermute(mine, 'z', pairs + [(j, i) for i, j in pairs])  8.21 us
    ppermute x1, starting transfers between devices, per_device(): lax.ppermute(far_half, ('z', 'yh', 'core'), [(far_source(i), i) for i in...  7.56 us
    all_to_all x1, blocking collectives, per_device(): parts = lax.all_to_all(parts, ('yl', 'core'), 0, 0)  7.52 us
    all_to_all x1, waiting for transfers between devices, per_device(): shares = lax.all_to_all(partial, 'x', 0, 0)  6.92 us
    pallas_call x1, Pallas kernels, attend_near(): pl.pallas_call(near_kernel, out_shape=(head_rows,) * 4 + (jax.ShapeDtypeS...  5.76 us
    pallas_call x1, Pallas kernels, attend_far(): pl.pallas_call(far_kernel, out_shape=jax.ShapeDtypeStruct((4, CHUNK // 4,...  5.53 us
    ppermute x2, starting transfers between devices, per_device(): lax.ppermute(w, 'core', [(0, 1), (1, 0)])  4.33 us
  transfers between devices with their start and end apart: 6, of which 1 were waited for; matrix products, arithmetic and copies ran while one was open for 0% of the time, Pallas kernels for 18%

profile of v1, /device:TPU:48, one launch (start us, length us, event | category | flops | bytes accessed | tf_op | source)
XLA Modules:
  0.0 66.7 jit_solution(748822815929863306)
XLA Ops:
  0.6 0.0 copy-start.6
  0.6 0.0 copy-start
  0.7 0.0 copy-start.1
  0.7 0.0 copy-start.5
  0.7 3.6 %shard_map.86 = bf16[4,128,256]{2,1,0:T(8,128)(2,1)} custom-call(s32[32]{0:T(128)} %counts_ref.7, bf16[128,1536]{1,0:T(8,128)(2,1)} %tokens_ref.2, bf16[128,1536]{1,0:T(8,128)(2,1)} %cotangent_ref.2, bf16[3,1536,128]{2,1,0:T(8,128)(2,1)} %bitcast.4, bf16[128,1536]{1,0:T(8,128)(2,1)} %w_out_ref.3, bf16[3,32,1536]{2,1,0:T(8,128)(2,1)} %bitcast.7), custom_call_target="tpu_custom_call" | custom-call | tf_op jit(solution)/shard_map/pallas_call | solution.py:86
  4.3 8.8 %all_to_all.15 = bf16[4,128,256]{2,1,0:T(8,128)(2,1)S(1)} all-to-all(bf16[4,128,256]{2,1,0:T(8,128)(2,1)} %shard_map.86), channel_id=1, replica_groups=mesh['z'=16,'yh'=2,'yl'=2,'x'=4,'core'=2] {'yh','yl'}, dimensions={0} | all-to-all | bytes 524288 | tf_op jit(solution)/shard_map/all_to_all | solution.py:617
  13.1 6.3 %collective-permute-start.1 = (bf16[512,256]{1,0:T(8,128)(2,1)S(1)}, bf16[512,256]{1,0:T(8,128)(2,1)S(1)}, u32[]{:S(2)}, u32[]{:S(2)}) collective-permute-start(bf16[512,256]{1,0:T(8,128)(2,1)S(1)} %bitcast.9), channel_id=1, source_target_pairs={{0,32},{64,96},{128,160},{192,224},{256,288},{320,352},{384,416},{... | collective-permute-start | bytes 786440 | tf_op jit(solution)/shard_map/ppermute | solution.py:622
  19.4 1.9 %collective-permute-start.2 = (bf16[512,256]{1,0:T(8,128)(2,1)S(1)}, bf16[512,256]{1,0:T(8,128)(2,1)S(1)}, u32[]{:S(2)}, u32[]{:S(2)}) collective-permute-start(bf16[512,256]{1,0:T(8,128)(2,1)S(1)} %bitcast.10), channel_id=1, source_target_pairs={{480,0},{32,64},{96,128},{160,192},{224,256},{288,320},{352,384},{... | collective-permute-start | bytes 786440 | tf_op jit(solution)/shard_map/ppermute | solution.py:622
  21.3 0.0 copy-done.6
  21.3 7.6 %collective-permute-start = (bf16[256,256]{1,0:T(8,128)(2,1)S(1)}, bf16[256,256]{1,0:T(8,128)(2,1)S(1)}, u32[]{:S(2)}, u32[]{:S(2)}) collective-permute-start(bf16[256,256]{1,0:T(8,128)(2,1)S(1)} %bitcast.13), channel_id=1, source_target_pairs={{448,0},{465,1},{80,16},{65,17},{480,32},{497,33},{112,48},{97,49}... | collective-permute-start | bytes 393224 | tf_op jit(solution)/shard_map/ppermute | solution.py:633
  28.9 0.0 copy-done
  28.9 1.9 %collective-permute-start.4 = (bf16[3,1536,128]{2,1,0:T(8,128)(2,1)S(1)}, bf16[3,1536,128]{2,1,0:T(8,128)(2,1)S(1)}, u32[]{:S(2)}, u32[]{:S(2)}) collective-permute-start(bf16[3,1536,128]{2,1,0:T(8,128)(2,1)S(1)} %bitcast.5), channel_id=1, source_target_pairs={{0,1},{1,0},{2,3},{3,2},{4,5},{5,4},{6,7},{7,6},{8,9},{9,8},{10,11... | collective-permute-start | bytes 3538952 | tf_op jit(solution)/shard_map/ppermute | solution.py:643
  30.8 0.0 copy-done.1
  30.9 2.4 %collective-permute-start.3 = (bf16[128,1536]{1,0:T(8,128)(2,1)S(1)}, bf16[128,1536]{1,0:T(8,128)(2,1)S(1)}, u32[]{:S(2)}, u32[]{:S(2)}) collective-permute-start(bf16[128,1536]{1,0:T(8,128)(2,1)S(1)} %copy-done.1), channel_id=1, source_target_pairs={{0,1},{1,0},{2,3},{3,2},{4,5},{5,4},{6,7},{7,6},{8,9},{9,8},{10,11... | collective-permute-start | bytes 1179656 | tf_op jit(solution)/shard_map/ppermute | solution.py:643
  33.3 0.0 collective-permute-done.1.first_ref
  33.3 0.0 collective-permute-done.2.second_ref
  33.3 0.0 copy-done.5
  33.3 5.8 %shard_map.88 = (bf16[1536,128]{1,0:T(8,128)(2,1)S(1)}, bf16[1536,128]{1,0:T(8,128)(2,1)S(1)}, bf16[1536,128]{1,0:T(8,128)(2,1)S(1)}, bf16[1536,128]{1,0:T(8,128...) custom-call(s32[32]{0:T(128)S(1)} %copy-done.5, ...), custom_call_target="tpu_custom_call" | custom-call | flops 10000000000 | bytes 1048576 | tf_op jit(solution)/shard_map/pallas_call | solution.py:263
  39.1 0.0 collective-permute-done.far_ref
  39.1 5.5 %shard_map.89 = bf16[4,64,256]{2,1,0:T(8,128)(2,1)S(1)} custom-call(s32[32]{0:T(128)S(1)} %copy-done.5, f32[8,128]{1,0:T(8,128)S(1)} %pad.4.gains_ref, bf16[256,256]{1,0:T(8,128)(2,1)S(1)} %collective-permute-done.far_ref, bf16[512,256]{1,0:T(8,128)(2,1)S(1)} %bitcast.12, bf16[1536,128]{1,0:T(8,128)(2,1)S(1)} %get-tuple-element.24.qx_ref, ...), custom_call_target="tpu_custom_call" | custom-call | flops 10000000000 | bytes 1048576 | tf_op jit(solution)/shard_map/pallas_call | solution.py:475
  44.6 7.5 %all_to_all.16.parts_ref = bf16[4,64,256]{2,1,0:T(8,128)(2,1)S(1)} all-to-all(bf16[4,64,256]{2,1,0:T(8,128)(2,1)S(1)} %shard_map.89), channel_id=1, replica_groups=mesh['z'=16,'yh'=2,'yl'=2,'x'=4,'core'=2] {'yl','core'}, dimensions={0} | all-to-all | bytes 262144 | tf_op jit(solution)/shard_map/all_to_all | solution.py:646
  52.1 0.0 copy-start.2
  52.1 0.0 copy-start.3
  52.1 0.0 copy-start.4
  52.1 0.0 collective-permute-done.3.w_out_far_ref
  52.1 0.0 collective-permute-done.4.w_qkv_far_ref
  52.2 1.8 %shard_map.90 = bf16[4,16,3072]{2,1,0:T(8,128)(2,1)} custom-call(bf16[4,64,256]{2,1,0:T(8,128)(2,1)S(1)} %all_to_all.16.parts_ref, bf16[128,1536]{1,0:T(8,128)(2,1)S(1)} %copy-done.1, bf16[3,1536,128]{2,1,0:T(8,128)(2,1)S(1)} %bitcast.6, bf16[128,1536]{1,0:T(8,128)(2,1)S(1)} %collective-permute-done.3.w_out_far_ref, ...), custom_call_target="tpu_custom_call" | custom-call | tf_op jit(solution)/shard_map/pallas_call | solution.py:530
  53.9 4.3 %all-to-all-start.2 = ((bf16[4,16,3072]{2,1,0:T(8,128)(2,1)}), bf16[4,16,3072]{2,1,0:T(8,128)(2,1)S(1)}, u32[]{:S(2)}, u32[]{:S(2)}) async-start(bf16[4,16,3072]{2,1,0:T(8,128)(2,1)} %shard_map.90), calls=%async_computation.2 | async-start | bytes 786432 | tf_op jit(solution)/shard_map/all_to_all | solution.py:648
  58.2 0.0 copy-done.2
  58.2 0.0 copy-done.3
  58.2 0.0 copy-done.4
  58.2 0.8 %shard_map.87 = (bf16[2,16,1536]{2,1,0:T(8,128)(2,1)S(1)}, f32[4,16,1536]{2,1,0:T(8,128)S(1)}) custom-call(s32[32]{0:T(128)S(1)} %copy-done.5, bf16[128,1536]{1,0:T(8,128)(2,1)S(1)} %copy-done.2, bf16[128,1536]{1,0:T(8,128)(2,1)S(1)} %copy-done.3, bf16[3,32,1536]{2,1,0:T(8,128)(2,1)S(1)} %bitcast.8), custom_call_target="tpu_custom_call" | custom-call | tf_op jit(solution)/shard_map/pallas_call | solution.py:565
  59.0 6.9 %all-to-all-done.2.shares_ref = bf16[4,16,3072]{2,1,0:T(8,128)(2,1)S(1)} async-done(((bf16[4,16,3072]{2,1,0:T(8,128)(2,1)}), bf16[4,16,3072]{2,1,0:T(8,128)(2,1)S(1)}, u32[]{:S(2)}, u32[]{:S(2)}) %all-to-all-start.2) | async-done | bytes 393248 | tf_op jit(solution)/shard_map/all_to_all | solution.py:648
  65.9 0.7 %shard_map.91 = (bf16[16,1536]{1,0:T(8,128)(2,1)}, bf16[16,1536]{1,0:T(8,128)(2,1)}) custom-call(bf16[2,16,1536]{2,1,0:T(8,128)(2,1)S(1)} %get-tuple-element.22.rows_ref, f32[4,16,1536]{2,1,0:T(8,128)S(1)} %get-tuple-element.23.factors_ref, bf16[4,16,3072]{2,1,0:T(8,128)(2,1)S(1)} %all-to-all-done.2.shares_ref), custom_call_target="tpu_custom_call" | custom-call | tf_op jit(solution)/shard_map/pallas_call | solution.py:596
  (2 shorter events, 0.0 us)
Async XLA Ops:
  0.6 20.7 %copy-start.6 = (f32[2,64]{1,0:T(2,128)S(1)}, f32[2,64]{1,0:T(2,128)}, u32[]{:S(2)}) copy-start(f32[2,64]{1,0:T(2,128)} %param.11) | copy-start | bytes 1540
  0.6 28.3 %copy-start = (bf16[1536,3,128]{2,0,1:T(8,128)(2,1)S(1)}, bf16[1536,3,128]{2,0,1:T(8,128)(2,1)}, u32[]{:S(2)}) copy-start(bf16[1536,3,128]{2,0,1:T(8,128)(2,1)} %param.9) | copy-start | bytes 3538948
  0.7 30.2 %copy-start.1 = (bf16[128,1536]{1,0:T(8,128)(2,1)S(1)}, bf16[128,1536]{1,0:T(8,128)(2,1)}, u32[]{:S(2)}) copy-start(bf16[128,1536]{1,0:T(8,128)(2,1)} %w_out_ref.3) | copy-start | bytes 1179652
  0.7 32.6 %copy-start.5 = (s32[32]{0:T(128)S(1)}, s32[32]{0:T(128)}, u32[]{:S(2)}) copy-start(s32[32]{0:T(128)} %counts_ref.7) | copy-start | bytes 388
  13.1 20.2 %collective-permute-start.1 = (bf16[512,256]{1,0:T(8,128)(2,1)S(1)}, bf16[512,256]{1,0:T(8,128)(2,1)S(1)}, u32[]{:S(2)}, u32[]{:S(2)}) collective-permute-start(bf16[512,256]{1,0:T(8,128)(2,1)S(1)} %bitcast.9), channel_id=1, source_target_pairs={{0,32},{64,96},{128,160},{192,224},{256,288},{320,352},{384,416},{... | collective-permute-start | bytes 786440 | tf_op jit(solution)/shard_map/ppermute | solution.py:622
  19.4 13.9 %collective-permute-start.2 = (bf16[512,256]{1,0:T(8,128)(2,1)S(1)}, bf16[512,256]{1,0:T(8,128)(2,1)S(1)}, u32[]{:S(2)}, u32[]{:S(2)}) collective-permute-start(bf16[512,256]{1,0:T(8,128)(2,1)S(1)} %bitcast.10), channel_id=1, source_target_pairs={{480,0},{32,64},{96,128},{160,192},{224,256},{288,320},{352,384},{... | collective-permute-start | bytes 786440 | tf_op jit(solution)/shard_map/ppermute | solution.py:622
  21.3 17.7 %collective-permute-start = (bf16[256,256]{1,0:T(8,128)(2,1)S(1)}, bf16[256,256]{1,0:T(8,128)(2,1)S(1)}, u32[]{:S(2)}, u32[]{:S(2)}) collective-permute-start(bf16[256,256]{1,0:T(8,128)(2,1)S(1)} %bitcast.13), channel_id=1, source_target_pairs={{448,0},{465,1},{80,16},{65,17},{480,32},{497,33},{112,48},{97,49}... | collective-permute-start | bytes 393224 | tf_op jit(solution)/shard_map/ppermute | solution.py:633
  28.9 23.2 %collective-permute-start.4 = (bf16[3,1536,128]{2,1,0:T(8,128)(2,1)S(1)}, bf16[3,1536,128]{2,1,0:T(8,128)(2,1)S(1)}, u32[]{:S(2)}, u32[]{:S(2)}) collective-permute-start(bf16[3,1536,128]{2,1,0:T(8,128)(2,1)S(1)} %bitcast.5), channel_id=1, source_target_pairs={{0,1},{1,0},{2,3},{3,2},{4,5},{5,4},{6,7},{7,6},{8,9},{9,8},{10,11... | collective-permute-start | bytes 3538952 | tf_op jit(solution)/shard_map/ppermute | solution.py:643
  30.9 21.3 %collective-permute-start.3 = (bf16[128,1536]{1,0:T(8,128)(2,1)S(1)}, bf16[128,1536]{1,0:T(8,128)(2,1)S(1)}, u32[]{:S(2)}, u32[]{:S(2)}) collective-permute-start(bf16[128,1536]{1,0:T(8,128)(2,1)S(1)} %copy-done.1), channel_id=1, source_target_pairs={{0,1},{1,0},{2,3},{3,2},{4,5},{5,4},{6,7},{7,6},{8,9},{9,8},{10,11... | collective-permute-start | bytes 1179656 | tf_op jit(solution)/shard_map/ppermute | solution.py:643
  52.1 6.1 %copy-start.2 = (bf16[128,1536]{1,0:T(8,128)(2,1)S(1)}, bf16[128,1536]{1,0:T(8,128)(2,1)}, u32[]{:S(2)}) copy-start(bf16[128,1536]{1,0:T(8,128)(2,1)} %tokens_ref.2) | copy-start | bytes 1179652
  52.1 6.1 %copy-start.3 = (bf16[128,1536]{1,0:T(8,128)(2,1)S(1)}, bf16[128,1536]{1,0:T(8,128)(2,1)}, u32[]{:S(2)}) copy-start(bf16[128,1536]{1,0:T(8,128)(2,1)} %cotangent_ref.2) | copy-start | bytes 1179652
  52.1 6.1 %copy-start.4 = (bf16[32,3,1536]{2,0,1:T(8,128)(2,1)S(1)}, bf16[32,3,1536]{2,0,1:T(8,128)(2,1)}, u32[]{:S(2)}) copy-start(bf16[32,3,1536]{2,0,1:T(8,128)(2,1)} %param.12) | copy-start | bytes 884740
  53.9 12.0 %all-to-all-start.2 = ((bf16[4,16,3072]{2,1,0:T(8,128)(2,1)}), bf16[4,16,3072]{2,1,0:T(8,128)(2,1)S(1)}, u32[]{:S(2)}, u32[]{:S(2)}) async-start(bf16[4,16,3072]{2,1,0:T(8,128)(2,1)} %shard_map.90), calls=%async_computation.2 | async-start | bytes 786432 | tf_op jit(solution)/shard_map/all_to_all | solution.py:648

commit v2 on v1

--- a/solution.py
+++ b/solution.py
@@ -57,19 +57,58 @@
     return centred * inv_std, inv_std
 
 
+def w_out_of(weights_ref):
+    tiles = weights_ref.shape[1] // LANES
+    return jnp.concatenate(
+        [weights_ref[3, tile * LANES : (tile + 1) * LANES, :] for tile in range(tiles)], axis=1
+    )
+
+
 def enter_kernel(
-    counts_ref, tokens_ref, cotangent_ref, w_qkv_ref, w_out_ref, modulation_ref, out_ref
+    counts_ref,
+    tokens_hbm,
+    cotangent_hbm,
+    w_qkv_hbm,
+    w_out_hbm,
+    modulation_hbm,
+    out_ref,
+    weights_ref,
+    tokens_ref,
+    cotangent_ref,
+    modulation_ref,
+    sems,
 ):
+    pairs = [
+        (tokens_hbm, tokens_ref),
+        (modulation_hbm, modulation_ref),
+        (w_qkv_hbm, weights_ref.at[0:3]),
+        (cotangent_hbm, cotangent_ref),
+    ]
+    for tile in range(weights_ref.shape[1] // LANES):
+        at = slice(tile * LANES, (tile + 1) * LANES)
+        pairs.append((w_out_hbm.at[:, at], weights_ref.at[3, at, :]))
+    copies = [
+        pltpu.make_async_copy(source, target, sems.at[place])
+        for place, (source, target) in enumerate(pairs)
+    ]
+    for copy in copies:
+        copy.start()
     rows = tokens_ref.shape[0]
     first = block_index() * rows
+    copies[0].wait()
+    normed, _ = layer_norm(tokens_ref[...].astype(F32))
+    copies[1].wait()
     shift, scale, gate = modulation_rows(counts_ref, modulation_ref, first, rows)
-    normed, _ = layer_norm(tokens_ref[...].astype(F32))
     hidden = (normed * (1.0 + scale) + shift).astype(BF16)
-    weights = jnp.concatenate([w_qkv_ref[part] for part in range(3)], axis=1)
+    copies[2].wait()
+    weights = jnp.concatenate([weights_ref[part] for part in range(3)], axis=1)
     qkv = jnp.dot(hidden, weights, preferred_element_type=F32)
     q, k, v = (qkv[:, part * LANES : (part + 1) * LANES] for part in range(3))
+    copies[3].wait()
     d_mixed = (cotangent_ref[...].astype(F32) * gate).astype(BF16)
-    d_attn = rows_dot(d_mixed, w_out_ref[...])
+    for copy in copies[4:]:
+        copy.wait()
+    d_attn = rows_dot(d_mixed, w_out_of(weights_ref))
     low = lax.broadcasted_iota(jnp.int32, (rows, LANES), 1) < HEAD
 
     def beside(left, right):
@@ -83,11 +122,22 @@
 
 
 def enter(counts, tokens, cotangent, w_parts, w_out, modulation, quad):
+    rows, width = tokens.shape
+    whole = pl.BlockSpec(memory_space=pl.ANY)
     return pl.pallas_call(
         enter_kernel,
-        out_shape=jax.ShapeDtypeStruct((quad, tokens.shape[0], 2 * LANES), BF16),
-        in_specs=[SMEM] + [VMEM] * 5,
-        out_specs=VMEM,
+        out_shape=(
+            jax.ShapeDtypeStruct((quad, rows, 2 * LANES), BF16),
+            jax.ShapeDtypeStruct((4, width, LANES), BF16),
+        ),
+        in_specs=[SMEM] + [whole] * 5,
+        out_specs=(VMEM, VMEM),
+        scratch_shapes=[
+            pltpu.VMEM((rows, width), BF16),
+            pltpu.VMEM((rows, width), BF16),
+            pltpu.VMEM(modulation.shape, BF16),
+            pltpu.SemaphoreType.DMA((4 + width // LANES,)),
+        ],
         compiler_params=pltpu.CompilerParams(vmem_limit_bytes=ENTER_LIMIT),
     )(counts, tokens, cotangent, w_parts, w_out, modulation)
 
@@ -217,7 +267,18 @@
         so_ref[at, :] = scores
         highest = jnp.maximum(highest, rows_max(scores))
         go_ref[at, :] = rows_dot(vx_ref[at, :], d_own)
-    stats_ref[MAIN, :, :] = highest
+    highest = jnp.max(highest, axis=0, keepdims=True) * LOG2_E
+    total = jnp.zeros((8, CHUNK), F32)
+    grads = jnp.zeros((8, CHUNK), F32)
+    for piece in range(MAIN * CHUNK // TILE):
+        at = slice(piece * TILE, (piece + 1) * TILE)
+        weights = jnp.exp2(so_ref[at, :] * LOG2_E - highest)
+        so_ref[at, :] = weights
+        total = total + jnp.sum(by_eight(weights), axis=0)
+        grads = grads + jnp.sum(by_eight(weights * go_ref[at, :]), axis=0)
+    stats_ref[MAIN, 0:1, :] = highest
+    stats_ref[MAIN, 1:2, :] = jnp.sum(total, axis=0, keepdims=True)
+    stats_ref[MAIN, 2:3, :] = jnp.sum(grads, axis=0, keepdims=True)
 
     left_key = jnp.clip((left_from + CHUNK) // CHUNK - 1, 0, MAIN - REACH_CHUNKS)
     right_key = jnp.clip((right_to - 1) // CHUNK - (REACH_CHUNKS - 1), 0, MAIN - REACH_CHUNKS)
@@ -269,7 +330,7 @@
         out_specs=(VMEM,) * 10,
         scratch_shapes=[pltpu.VMEM((REACH_CHUNKS * CHUNK, CHUNK), F32)] * 2,
         cost_estimate=pl.CostEstimate(
-            flops=10000000000, bytes_accessed=1 << 20, transcendentals=1 << 20
+            flops=7000000000, bytes_accessed=1 << 20, transcendentals=1 << 20
         ),
         compiler_params=pltpu.CompilerParams(vmem_limit_bytes=VMEM_LIMIT),
     )(counts, gains, first, quad, second)
@@ -327,22 +388,28 @@
     scores = rows_dot(kf_ref[...], q_own)
     s_ref[0:CHUNK, :] = scores
     g_ref[0:CHUNK, :] = rows_dot(vf_ref[...], d_own)
-    highest = jnp.maximum(stats_ref[MAIN, :, :], rows_max(scores))
-    highest = jnp.max(highest, axis=0, keepdims=True) * LOG2_E
+    near_highest = stats_ref[MAIN, 0:1, :]
+    highest = jnp.max(rows_max(scores), axis=0, keepdims=True) * LOG2_E
+    highest = jnp.maximum(near_highest, highest)
+    shrink = jnp.exp2(near_highest - highest)
     zeros = jnp.zeros((8, CHUNK), F32)
-    total, grads = add_tiles(so_ref, go_ref, rows, highest, zeros, zeros)
-    total, grads = add_tiles(s_ref, g_ref, CHUNK, highest, total, grads)
-    scale = 1.0 / jnp.sum(total, axis=0, keepdims=True)
-    mean_grad = jnp.sum(grads, axis=0, keepdims=True) * scale
+    total, grads = add_tiles(s_ref, g_ref, CHUNK, highest, zeros, zeros)
+    total = jnp.sum(total, axis=0, keepdims=True) + stats_ref[MAIN, 1:2, :] * shrink
+    grads = jnp.sum(grads, axis=0, keepdims=True) + stats_ref[MAIN, 2:3, :] * shrink
+    scale = 1.0 / total
+    mean_grad = grads * scale
 
     def write_tile(scores, grads, highest, scale, mean_grad, to):
         probs = jnp.exp2(scores * LOG2_E - highest) * scale
         p_ref[to, :] = probs.astype(BF16)
         d_ref[to, :] = (probs * (grads - mean_grad)).astype(BF16)
 
+    near_scale = shrink * scale
     for piece in range(rows // TILE):
         at = slice(piece * TILE, (piece + 1) * TILE)
-        write_tile(so_ref[at, :], go_ref[at, :], highest, scale, mean_grad, at)
+        probs = so_ref[at, :] * near_scale
+        p_ref[at, :] = probs.astype(BF16)
+        d_ref[at, :] = (probs * (go_ref[at, :] - mean_grad)).astype(BF16)
     for piece in range(CHUNK // TILE):
         at = slice(piece * TILE, (piece + 1) * TILE)
         to = slice(rows + piece * TILE, rows + (piece + 1) * TILE)
@@ -485,15 +552,15 @@
         + [pltpu.VMEM((CHUNK, LANES), F32)] * 2
         + [pltpu.VMEM((CHUNK, 2 * LANES), BF16)],
         cost_estimate=pl.CostEstimate(
-            flops=10000000000, bytes_accessed=1 << 20, transcendentals=1 << 20
+            flops=7000000000, bytes_accessed=1 << 20, transcendentals=1 << 20
         ),
         compiler_params=pltpu.CompilerParams(vmem_limit_bytes=VMEM_LIMIT),
     )(counts, gains, far, quad, *near_parts)
 
 
-def project_kernel(parts_ref, w_out_ref, w_qkv_ref, w_out_far_ref, w_qkv_far_ref, out_ref):
+def project_kernel(parts_ref, weights_ref, weights_far_ref, out_ref):
     rows = parts_ref.shape[1]
-    width = w_out_ref.shape[1]
+    width = weights_ref.shape[1]
     share = out_ref.shape[1]
     core = lax.axis_index("core")
     low = lax.broadcasted_iota(jnp.int32, (rows, LANES), 1) < HEAD
@@ -513,10 +580,10 @@
     attn_far, grads_far = by_column(1 - core)
     mixed = jnp.dot(
         jnp.concatenate([attn, attn_far], axis=1),
-        jnp.concatenate([w_out_ref[...], w_out_far_ref[...]], axis=0),
+        jnp.concatenate([w_out_of(weights_ref), w_out_of(weights_far_ref)], axis=0),
         preferred_element_type=F32,
     ).astype(BF16)
-    weights = [ref[part] for ref in (w_qkv_ref, w_qkv_far_ref) for part in range(3)]
+    weights = [ref[part] for ref in (weights_ref, weights_far_ref) for part in range(3)]
     d_hidden = rows_dot(
         jnp.concatenate(grads + grads_far, axis=1), jnp.concatenate(weights, axis=1)
     ).astype(BF16)
@@ -526,16 +593,16 @@
         out_ref[place, :, width:] = d_hidden[at]
 
 
-def project(parts, w_out, w_parts, w_out_far, w_parts_far, x_count):
+def project(parts, weights, weights_far, x_count):
     return pl.pallas_call(
         project_kernel,
         out_shape=jax.ShapeDtypeStruct(
-            (x_count, parts.shape[1] // x_count, 2 * w_out.shape[1]), BF16
+            (x_count, parts.shape[1] // x_count, 2 * weights.shape[1]), BF16
         ),
-        in_specs=[VMEM] * 5,
+        in_specs=[VMEM] * 3,
         out_specs=VMEM,
         compiler_params=pltpu.CompilerParams(vmem_limit_bytes=VMEM_LIMIT),
-    )(parts, w_out, w_parts, w_out_far, w_parts_far)
+    )(parts, weights, weights_far)
 
 
 def ready_kernel(
@@ -613,7 +680,7 @@
     mod_parts = modulation.transpose(1, 0, 2)
     gains = jnp.pad(qk_gain, ((0, 6), (0, LANES - HEAD)))
 
-    heads = enter(image_counts, tokens, cotangent, w_parts, w_out, mod_parts, quad)
+    heads, weights = enter(image_counts, tokens, cotangent, w_parts, w_out, mod_parts, quad)
     mine = lax.all_to_all(heads, ("yh", "yl"), 0, 0)
     mine = mine.reshape(quad * tok_rows, 2 * LANES)
     evens = range(0, z_count, 2)
@@ -638,13 +705,11 @@
     )
     rows, factors = ready(image_counts, tokens_late, cotangent_late, mod_late, share)
     near_parts = attend_near(image_counts, gains, first, mine, second)
-    _, _, w_parts_late, w_out_late = lax.optimization_barrier((mine, mine, w_parts, w_out))
-    w_parts_far, w_out_far = (
-        lax.ppermute(w, "core", [(0, 1), (1, 0)]) for w in (w_parts_late, w_out_late)
-    )
+    _, weights_late = lax.optimization_barrier((mine, weights))
+    weights_far = lax.ppermute(weights_late, "core", [(0, 1), (1, 0)])
     parts = attend_far(image_counts, gains, far, mine, near_parts)
     parts = lax.all_to_all(parts, ("yl", "core"), 0, 0)
-    partial = project(parts, w_out, w_parts, w_out_far, w_parts_far, x_count)
+    partial = project(parts, weights, weights_far, x_count)
     shares = lax.all_to_all(partial, "x", 0, 0)
     return leave(rows, factors, shares)
 

time: 67.1 us -> 66.3 us (0.988)
  the two profiles are of different devices: /device:TPU:48 before, /device:TPU:8 now
where the time goes in v2:
time: 66.3 us; the launch traced here: 65.9 us
  blocking collectives  21.7 us (33%)
  starting transfers between devices  18.2 us (27%)
  Pallas kernels  15.4 us (23%)
  waiting for transfers between devices  9.85 us (15%)
  between operations  0.77 us (1%)
    all_to_all x1, blocking collectives, per_device(): mine = lax.all_to_all(heads, ('yh', 'yl'), 0, 0)  14.4 us
    ppermute x2, starting transfers between devices, per_device(): lax.ppermute(mine, 'z', pairs + [(j, i) for i, j in pairs])  10 us
    all_to_all x1, waiting for transfers between devices, per_device(): shares = lax.all_to_all(partial, 'x', 0, 0)  7.62 us
    all_to_all x1, blocking collectives, per_device(): parts = lax.all_to_all(parts, ('yl', 'core'), 0, 0)  7.25 us
    pallas_call x1, Pallas kernels, attend_near(): pl.pallas_call(near_kernel, out_shape=(head_rows,) * 4 + (jax.ShapeDtypeS...  4.8 us
    pallas_call x1, Pallas kernels, enter(): pl.pallas_call(enter_kernel, out_shape=(jax.ShapeDtypeStruct((quad, rows,...  4.56 us
    all_to_all x1, starting transfers between devices, per_device(): shares = lax.all_to_all(partial, 'x', 0, 0)  4.29 us
    pallas_call x1, Pallas kernels, attend_far(): pl.pallas_call(far_kernel, out_shape=jax.ShapeDtypeStruct((4, CHUNK // 4,...  2.77 us
  transfers between devices with their start and end apart: 5, of which 3 were waited for; matrix products, arithmetic and copies ran while one was open for 0% of the time, Pallas kernels for 13%

profile of v2, /device:TPU:8, one launch (start us, length us, event | category | flops | bytes accessed | tf_op | source)
XLA Modules:
  0.0 65.9 jit_solution(337075489486944488)
XLA Ops:
  0.6 0.0 copy-start.5
  0.6 0.0 copy-start.4
  0.7 4.6 %shard_map.86 = (bf16[4,128,256]{2,1,0:T(8,128)(2,1)}, bf16[4,1536,128]{2,1,0:T(8,128)(2,1)}) custom-call(s32[32]{0:T(128)} %counts_ref.7, bf16[128,1536]{1,0:T(8,128)(2,1)} %tokens_ref, bf16[128,1536]{1,0:T(8,128)(2,1)} %cotangent_ref, bf16[3,1536,128]{2,1,0:T(8,128)(2,1)} %bitcast.10, bf16[128,1536]{1,0:T(8,128)(2,1)} %w_out_hbm.1, ...), custom_call_target="tpu_custom_call" | custom-call | tf_op jit(solution)/shard_map/pallas_call | solution.py:127
  5.2 14.4 %all_to_all.15 = bf16[4,128,256]{2,1,0:T(8,128)(2,1)S(1)} all-to-all(bf16[4,128,256]{2,1,0:T(8,128)(2,1)} %get-tuple-element.20), channel_id=1, replica_groups=mesh['z'=16,'yh'=2,'yl'=2,'x'=4,'core'=2] {'yh','yl'}, dimensions={0} | all-to-all | bytes 524288 | tf_op jit(solution)/shard_map/all_to_all | solution.py:684
  19.7 1.9 %collective-permute-start.1 = (bf16[512,256]{1,0:T(8,128)(2,1)S(1)}, bf16[512,256]{1,0:T(8,128)(2,1)S(1)}, u32[]{:S(2)}, u32[]{:S(2)}) collective-permute-start(bf16[512,256]{1,0:T(8,128)(2,1)S(1)} %bitcast.6), channel_id=1, source_target_pairs={{0,32},{64,96},{128,160},{192,224},{256,288},{320,352},{384,416},{... | collective-permute-start | bytes 786440 | tf_op jit(solution)/shard_map/ppermute | solution.py:689
  21.6 8.1 %collective-permute-start.2 = (bf16[512,256]{1,0:T(8,128)(2,1)S(1)}, bf16[512,256]{1,0:T(8,128)(2,1)S(1)}, u32[]{:S(2)}, u32[]{:S(2)}) collective-permute-start(bf16[512,256]{1,0:T(8,128)(2,1)S(1)} %bitcast.7), channel_id=1, source_target_pairs={{480,0},{32,64},{96,128},{160,192},{224,256},{288,320},{352,384},{... | collective-permute-start | bytes 786440 | tf_op jit(solution)/shard_map/ppermute | solution.py:689
  29.7 0.0 copy-done.5
  29.7 1.9 %collective-permute-start.3 = (bf16[4,1536,128]{2,1,0:T(8,128)(2,1)}, bf16[4,1536,128]{2,1,0:T(8,128)(2,1)S(1)}, u32[]{:S(2)}, u32[]{:S(2)}) collective-permute-start(bf16[4,1536,128]{2,1,0:T(8,128)(2,1)} %get-tuple-element.37.weights_ref), channel_id=1, source_target_pairs={{0,1},{1,0},{2,3},{3,2},{4,5},{5,4},{6,7},{7,6},{8,9},{9,8},{10,11... | collective-permute-start | bytes 4718600 | tf_op jit(solution)/shard_map/ppermute | solution.py:709
  31.7 1.9 %collective-permute-start = (bf16[256,256]{1,0:T(8,128)(2,1)S(1)}, bf16[256,256]{1,0:T(8,128)(2,1)S(1)}, u32[]{:S(2)}, u32[]{:S(2)}) collective-permute-start(bf16[256,256]{1,0:T(8,128)(2,1)S(1)} %bitcast.11), channel_id=1, source_target_pairs={{448,0},{465,1},{80,16},{65,17},{480,32},{497,33},{112,48},{97,49}... | collective-permute-start | bytes 393224 | tf_op jit(solution)/shard_map/ppermute | solution.py:700
  33.6 0.0 collective-permute-done.1.first_ref
  33.6 0.8 %collective-permute-done.2.second_ref = bf16[512,256]{1,0:T(8,128)(2,1)S(1)} collective-permute-done((bf16[512,256]{1,0:T(8,128)(2,1)S(1)}, bf16[512,256]{1,0:T(8,128)(2,1)S(1)}, u32[]{:S(2)}, u32[]{:S(2)}) %collective-permute-start.2) | collective-permute-done | bytes 262176 | tf_op jit(solution)/shard_map/ppermute | solution.py:689
  34.4 0.0 copy-done.4
  34.4 4.8 %shard_map.88 = (bf16[1536,128]{1,0:T(8,128)(2,1)S(1)}, bf16[1536,128]{1,0:T(8,128)(2,1)S(1)}, bf16[1536,128]{1,0:T(8,128)(2,1)S(1)}, bf16[1536,128]{1,0:T(8,128...) custom-call(s32[32]{0:T(128)S(1)} %copy-done.4, ...), custom_call_target="tpu_custom_call" | custom-call | flops 7000000000 | bytes 1048576 | tf_op jit(solution)/shard_map/pallas_call | solution.py:324
  39.2 1.5 %collective-permute-done.far_ref = bf16[256,256]{1,0:T(8,128)(2,1)S(1)} collective-permute-done((bf16[256,256]{1,0:T(8,128)(2,1)S(1)}, bf16[256,256]{1,0:T(8,128)(2,1)S(1)}, u32[]{:S(2)}, u32[]{:S(2)}) %collective-permute-start) | collective-permute-done | bytes 131104 | tf_op jit(solution)/shard_map/ppermute | solution.py:700
  40.7 0.0 copy-start
  40.7 2.8 %shard_map.89 = bf16[4,64,256]{2,1,0:T(8,128)(2,1)S(1)} custom-call(s32[32]{0:T(128)S(1)} %copy-done.4, f32[8,128]{1,0:T(8,128)S(1)} %pad.4.gains_ref, bf16[256,256]{1,0:T(8,128)(2,1)S(1)} %collective-permute-done.far_ref, bf16[512,256]{1,0:T(8,128)(2,1)S(1)} %bitcast.9, bf16[1536,128]{1,0:T(8,128)(2,1)S(1)} %get-tuple-element.26.qx_ref, ...), custom_call_target="tpu_custom_call" | custom-call | flops 7000000000 | bytes 1048576 | tf_op jit(solution)/shard_map/pallas_call | solution.py:542
  43.4 7.2 %all_to_all.16.parts_ref = bf16[4,64,256]{2,1,0:T(8,128)(2,1)S(1)} all-to-all(bf16[4,64,256]{2,1,0:T(8,128)(2,1)S(1)} %shard_map.89), channel_id=1, replica_groups=mesh['z'=16,'yh'=2,'yl'=2,'x'=4,'core'=2] {'yl','core'}, dimensions={0} | all-to-all | bytes 262144 | tf_op jit(solution)/shard_map/all_to_all | solution.py:711
  50.7 0.0 copy-start.1
  50.7 0.0 copy-start.2
  50.7 0.0 copy-start.3
  50.7 0.0 collective-permute-done.3.weights_far_ref
  50.7 0.0 copy-done
  50.7 1.8 %shard_map.90 = bf16[4,16,3072]{2,1,0:T(8,128)(2,1)} custom-call(bf16[4,64,256]{2,1,0:T(8,128)(2,1)S(1)} %all_to_all.16.parts_ref, bf16[4,1536,128]{2,1,0:T(8,128)(2,1)S(1)} %copy-done, bf16[4,1536,128]{2,1,0:T(8,128)(2,1)S(1)} %collective-permute-done.3.weights_far_ref), custom_call_target="tpu_custom_call" | custom-call | tf_op jit(solution)/shard_map/pallas_call | solution.py:597
  52.5 4.3 %all-to-all-start.2 = ((bf16[4,16,3072]{2,1,0:T(8,128)(2,1)}), bf16[4,16,3072]{2,1,0:T(8,128)(2,1)S(1)}, u32[]{:S(2)}, u32[]{:S(2)}) async-start(bf16[4,16,3072]{2,1,0:T(8,128)(2,1)} %shard_map.90), calls=%async_computation.2 | async-start | bytes 786432 | tf_op jit(solution)/shard_map/all_to_all | solution.py:713
  56.8 0.0 copy-done.1
  56.8 0.0 copy-done.2
  56.8 0.0 copy-done.3
  56.8 0.8 %shard_map.87 = (bf16[2,16,1536]{2,1,0:T(8,128)(2,1)S(1)}, f32[4,16,1536]{2,1,0:T(8,128)S(1)}) custom-call(s32[32]{0:T(128)S(1)} %copy-done.4, bf16[128,1536]{1,0:T(8,128)(2,1)S(1)} %copy-done.1, bf16[128,1536]{1,0:T(8,128)(2,1)S(1)} %copy-done.2, bf16[3,32,1536]{2,1,0:T(8,128)(2,1)S(1)} %bitcast.5), custom_call_target="tpu_custom_call" | custom-call | tf_op jit(solution)/shard_map/pallas_call | solution.py:632
  57.5 7.6 %all-to-all-done.2.shares_ref = bf16[4,16,3072]{2,1,0:T(8,128)(2,1)S(1)} async-done(((bf16[4,16,3072]{2,1,0:T(8,128)(2,1)}), bf16[4,16,3072]{2,1,0:T(8,128)(2,1)S(1)}, u32[]{:S(2)}, u32[]{:S(2)}) %all-to-all-start.2) | async-done | bytes 393248 | tf_op jit(solution)/shard_map/all_to_all | solution.py:713
  65.2 0.7 %shard_map.91 = (bf16[16,1536]{1,0:T(8,128)(2,1)}, bf16[16,1536]{1,0:T(8,128)(2,1)}) custom-call(bf16[2,16,1536]{2,1,0:T(8,128)(2,1)S(1)} %get-tuple-element.24.rows_ref, f32[4,16,1536]{2,1,0:T(8,128)S(1)} %get-tuple-element.25.factors_ref, bf16[4,16,3072]{2,1,0:T(8,128)(2,1)S(1)} %all-to-all-done.2.shares_ref), custom_call_target="tpu_custom_call" | custom-call | tf_op jit(solution)/shard_map/pallas_call | solution.py:663
  (2 shorter events, 0.0 us)
Async XLA Ops:
  0.6 29.1 %copy-start.5 = (f32[2,64]{1,0:T(2,128)S(1)}, f32[2,64]{1,0:T(2,128)}, u32[]{:S(2)}) copy-start(f32[2,64]{1,0:T(2,128)} %param.11) | copy-start | bytes 1540
  0.6 33.7 %copy-start.4 = (s32[32]{0:T(128)S(1)}, s32[32]{0:T(128)}, u32[]{:S(2)}) copy-start(s32[32]{0:T(128)} %counts_ref.7) | copy-start | bytes 388
  19.7 14.0 %collective-permute-start.1 = (bf16[512,256]{1,0:T(8,128)(2,1)S(1)}, bf16[512,256]{1,0:T(8,128)(2,1)S(1)}, u32[]{:S(2)}, u32[]{:S(2)}) collective-permute-start(bf16[512,256]{1,0:T(8,128)(2,1)S(1)} %bitcast.6), channel_id=1, source_target_pairs={{0,32},{64,96},{128,160},{192,224},{256,288},{320,352},{384,416},{... | collective-permute-start | bytes 786440 | tf_op jit(solution)/shard_map/ppermute | solution.py:689
  21.6 12.8 %collective-permute-start.2 = (bf16[512,256]{1,0:T(8,128)(2,1)S(1)}, bf16[512,256]{1,0:T(8,128)(2,1)S(1)}, u32[]{:S(2)}, u32[]{:S(2)}) collective-permute-start(bf16[512,256]{1,0:T(8,128)(2,1)S(1)} %bitcast.7), channel_id=1, source_target_pairs={{480,0},{32,64},{96,128},{160,192},{224,256},{288,320},{352,384},{... | collective-permute-start | bytes 786440 | tf_op jit(solution)/shard_map/ppermute | solution.py:689
  29.7 21.0 %collective-permute-start.3 = (bf16[4,1536,128]{2,1,0:T(8,128)(2,1)}, bf16[4,1536,128]{2,1,0:T(8,128)(2,1)S(1)}, u32[]{:S(2)}, u32[]{:S(2)}) collective-permute-start(bf16[4,1536,128]{2,1,0:T(8,128)(2,1)} %get-tuple-element.37.weights_ref), channel_id=1, source_target_pairs={{0,1},{1,0},{2,3},{3,2},{4,5},{5,4},{6,7},{7,6},{8,9},{9,8},{10,11... | collective-permute-start | bytes 4718600 | tf_op jit(solution)/shard_map/ppermute | solution.py:709
  31.7 9.0 %collective-permute-start = (bf16[256,256]{1,0:T(8,128)(2,1)S(1)}, bf16[256,256]{1,0:T(8,128)(2,1)S(1)}, u32[]{:S(2)}, u32[]{:S(2)}) collective-permute-start(bf16[256,256]{1,0:T(8,128)(2,1)S(1)} %bitcast.11), channel_id=1, source_target_pairs={{448,0},{465,1},{80,16},{65,17},{480,32},{497,33},{112,48},{97,49}... | collective-permute-start | bytes 393224 | tf_op jit(solution)/shard_map/ppermute | solution.py:700
  40.7 10.0 %copy-start = (bf16[4,1536,128]{2,1,0:T(8,128)(2,1)S(1)}, bf16[4,1536,128]{2,1,0:T(8,128)(2,1)}, u32[]{:S(2)}) copy-start(bf16[4,1536,128]{2,1,0:T(8,128)(2,1)} %get-tuple-element.37.weights_ref) | copy-start | bytes 4718596
  50.7 6.1 %copy-start.1 = (bf16[128,1536]{1,0:T(8,128)(2,1)S(1)}, bf16[128,1536]{1,0:T(8,128)(2,1)}, u32[]{:S(2)}) copy-start(bf16[128,1536]{1,0:T(8,128)(2,1)} %tokens_ref) | copy-start | bytes 1179652
  50.7 6.1 %copy-start.2 = (bf16[128,1536]{1,0:T(8,128)(2,1)S(1)}, bf16[128,1536]{1,0:T(8,128)(2,1)}, u32[]{:S(2)}) copy-start(bf16[128,1536]{1,0:T(8,128)(2,1)} %cotangent_ref) | copy-start | bytes 1179652
  50.7 6.1 %copy-start.3 = (bf16[32,3,1536]{2,0,1:T(8,128)(2,1)S(1)}, bf16[32,3,1536]{2,0,1:T(8,128)(2,1)}, u32[]{:S(2)}) copy-start(bf16[32,3,1536]{2,0,1:T(8,128)(2,1)} %param.12) | copy-start | bytes 884740
  52.5 12.7 %all-to-all-start.2 = ((bf16[4,16,3072]{2,1,0:T(8,128)(2,1)}), bf16[4,16,3072]{2,1,0:T(8,128)(2,1)S(1)}, u32[]{:S(2)}, u32[]{:S(2)}) async-start(bf16[4,16,3072]{2,1,0:T(8,128)(2,1)} %shard_map.90), calls=%async_computation.2 | async-start | bytes 786432 | tf_op jit(solution)/shard_map/all_to_all | solution.py:713

commit v3 on v1

--- a/solution.py
+++ b/solution.py
@@ -55,6 +55,13 @@
     centred = values - average
     inv_std = lax.rsqrt(jnp.mean(centred * centred, axis=-1, keepdims=True) + EPS)
     return centred * inv_std, inv_std
+
+
+def w_out_of(weights_ref):
+    tiles = weights_ref.shape[1] // LANES
+    return jnp.concatenate(
+        [weights_ref[3, tile * LANES : (tile + 1) * LANES, :] for tile in range(tiles)], axis=1
+    )
 
 
 def enter_kernel(
@@ -90,6 +97,41 @@
         out_specs=VMEM,
         compiler_params=pltpu.CompilerParams(vmem_limit_bytes=ENTER_LIMIT),
     )(counts, tokens, cotangent, w_parts, w_out, modulation)
+
+
+def pack_kernel(w_qkv_ref, w_out_ref, weights_ref, sems):
+    pairs = [(w_qkv_ref, weights_ref.at[0:3])]
+    for tile in range(weights_ref.shape[1] // LANES):
+        at = slice(tile * LANES, (tile + 1) * LANES)
+        pairs.append((w_out_ref.at[:, at], weights_ref.at[3, at, :]))
+    copies = [
+        pltpu.make_async_copy(source, target, sems.at[place])
+        for place, (source, target) in enumerate(pairs)
+    ]
+    for copy in copies:
+        copy.start()
+    for copy in copies:
+        copy.wait()
+
+
+def pack(w_parts, w_out):
+    width = w_out.shape[1]
+    whole = pl.BlockSpec(memory_space=pl.ANY)
+    return pl.pallas_call(
+        pack_kernel,
+        out_shape=jax.ShapeDtypeStruct((4, width, LANES), BF16),
+        in_specs=[whole] * 2,
+        out_specs=VMEM,
+        scratch_shapes=[pltpu.SemaphoreType.DMA((1 + width // LANES,))],
+        compiler_params=pltpu.CompilerParams(vmem_limit_bytes=8 * 1024 * 1024),
+    )(w_parts, w_out)
+
+
+def w_out_of(weights_ref):
+    tiles = weights_ref.shape[1] // LANES
+    return jnp.concatenate(
+        [weights_ref[3, tile * LANES : (tile + 1) * LANES, :] for tile in range(tiles)], axis=1
+    )
 
 
 LOG2_E = math.log2(math.e)
@@ -217,7 +259,18 @@
         so_ref[at, :] = scores
         highest = jnp.maximum(highest, rows_max(scores))
         go_ref[at, :] = rows_dot(vx_ref[at, :], d_own)
-    stats_ref[MAIN, :, :] = highest
+    highest = jnp.max(highest, axis=0, keepdims=True) * LOG2_E
+    total = jnp.zeros((8, CHUNK), F32)
+    grads = jnp.zeros((8, CHUNK), F32)
+    for piece in range(MAIN * CHUNK // TILE):
+        at = slice(piece * TILE, (piece + 1) * TILE)
+        weights = jnp.exp2(so_ref[at, :] * LOG2_E - highest)
+        so_ref[at, :] = weights
+        total = total + jnp.sum(by_eight(weights), axis=0)
+        grads = grads + jnp.sum(by_eight(weights * go_ref[at, :]), axis=0)
+    stats_ref[MAIN, 0:1, :] = highest
+    stats_ref[MAIN, 1:2, :] = jnp.sum(total, axis=0, keepdims=True)
+    stats_ref[MAIN, 2:3, :] = jnp.sum(grads, axis=0, keepdims=True)
 
     left_key = jnp.clip((left_from + CHUNK) // CHUNK - 1, 0, MAIN - REACH_CHUNKS)
     right_key = jnp.clip((right_to - 1) // CHUNK - (REACH_CHUNKS - 1), 0, MAIN - REACH_CHUNKS)
@@ -269,7 +322,7 @@
         out_specs=(VMEM,) * 10,
         scratch_shapes=[pltpu.VMEM((REACH_CHUNKS * CHUNK, CHUNK), F32)] * 2,
         cost_estimate=pl.CostEstimate(
-            flops=10000000000, bytes_accessed=1 << 20, transcendentals=1 << 20
+            flops=7000000000, bytes_accessed=1 << 20, transcendentals=1 << 20
         ),
         compiler_params=pltpu.CompilerParams(vmem_limit_bytes=VMEM_LIMIT),
     )(counts, gains, first, quad, second)
@@ -327,22 +380,28 @@
     scores = rows_dot(kf_ref[...], q_own)
     s_ref[0:CHUNK, :] = scores
     g_ref[0:CHUNK, :] = rows_dot(vf_ref[...], d_own)
-    highest = jnp.maximum(stats_ref[MAIN, :, :], rows_max(scores))
-    highest = jnp.max(highest, axis=0, keepdims=True) * LOG2_E
+    near_highest = stats_ref[MAIN, 0:1, :]
+    highest = jnp.max(rows_max(scores), axis=0, keepdims=True) * LOG2_E
+    highest = jnp.maximum(near_highest, highest)
+    shrink = jnp.exp2(near_highest - highest)
     zeros = jnp.zeros((8, CHUNK), F32)
-    total, grads = add_tiles(so_ref, go_ref, rows, highest, zeros, zeros)
-    total, grads = add_tiles(s_ref, g_ref, CHUNK, highest, total, grads)
-    scale = 1.0 / jnp.sum(total, axis=0, keepdims=True)
-    mean_grad = jnp.sum(grads, axis=0, keepdims=True) * scale
+    total, grads = add_tiles(s_ref, g_ref, CHUNK, highest, zeros, zeros)
+    total = jnp.sum(total, axis=0, keepdims=True) + stats_ref[MAIN, 1:2, :] * shrink
+    grads = jnp.sum(grads, axis=0, keepdims=True) + stats_ref[MAIN, 2:3, :] * shrink
+    scale = 1.0 / total
+    mean_grad = grads * scale
 
     def write_tile(scores, grads, highest, scale, mean_grad, to):
         probs = jnp.exp2(scores * LOG2_E - highest) * scale
         p_ref[to, :] = probs.astype(BF16)
         d_ref[to, :] = (probs * (grads - mean_grad)).astype(BF16)
 
+    near_scale = shrink * scale
     for piece in range(rows // TILE):
         at = slice(piece * TILE, (piece + 1) * TILE)
-        write_tile(so_ref[at, :], go_ref[at, :], highest, scale, mean_grad, at)
+        probs = so_ref[at, :] * near_scale
+        p_ref[at, :] = probs.astype(BF16)
+        d_ref[at, :] = (probs * (go_ref[at, :] - mean_grad)).astype(BF16)
     for piece in range(CHUNK // TILE):
         at = slice(piece * TILE, (piece + 1) * TILE)
         to = slice(rows + piece * TILE, rows + (piece + 1) * TILE)
@@ -485,15 +544,15 @@
         + [pltpu.VMEM((CHUNK, LANES), F32)] * 2
         + [pltpu.VMEM((CHUNK, 2 * LANES), BF16)],
         cost_estimate=pl.CostEstimate(
-            flops=10000000000, bytes_accessed=1 << 20, transcendentals=1 << 20
+            flops=7000000000, bytes_accessed=1 << 20, transcendentals=1 << 20
         ),
         compiler_params=pltpu.CompilerParams(vmem_limit_bytes=VMEM_LIMIT),
     )(counts, gains, far, quad, *near_parts)
 
 
-def project_kernel(parts_ref, w_out_ref, w_qkv_ref, w_out_far_ref, w_qkv_far_ref, out_ref):
+def project_kernel(parts_ref, weights_ref, weights_far_ref, out_ref):
     rows = parts_ref.shape[1]
-    width = w_out_ref.shape[1]
+    width = weights_ref.shape[1]
     share = out_ref.shape[1]
     core = lax.axis_index("core")
     low = lax.broadcasted_iota(jnp.int32, (rows, LANES), 1) < HEAD
@@ -513,10 +572,10 @@
     attn_far, grads_far = by_column(1 - core)
     mixed = jnp.dot(
         jnp.concatenate([attn, attn_far], axis=1),
-        jnp.concatenate([w_out_ref[...], w_out_far_ref[...]], axis=0),
+        jnp.concatenate([w_out_of(weights_ref), w_out_of(weights_far_ref)], axis=0),
         preferred_element_type=F32,
     ).astype(BF16)
-    weights = [ref[part] for ref in (w_qkv_ref, w_qkv_far_ref) for part in range(3)]
+    weights = [ref[part] for ref in (weights_ref, weights_far_ref) for part in range(3)]
     d_hidden = rows_dot(
         jnp.concatenate(grads + grads_far, axis=1), jnp.concatenate(weights, axis=1)
     ).astype(BF16)
@@ -526,16 +585,16 @@
         out_ref[place, :, width:] = d_hidden[at]
 
 
-def project(parts, w_out, w_parts, w_out_far, w_parts_far, x_count):
+def project(parts, weights, weights_far, x_count):
     return pl.pallas_call(
         project_kernel,
         out_shape=jax.ShapeDtypeStruct(
-            (x_count, parts.shape[1] // x_count, 2 * w_out.shape[1]), BF16
+            (x_count, parts.shape[1] // x_count, 2 * weights.shape[1]), BF16
         ),
-        in_specs=[VMEM] * 5,
+        in_specs=[VMEM] * 3,
         out_specs=VMEM,
         compiler_params=pltpu.CompilerParams(vmem_limit_bytes=VMEM_LIMIT),
-    )(parts, w_out, w_parts, w_out_far, w_parts_far)
+    )(parts, weights, weights_far)
 
 
 def ready_kernel(
@@ -638,13 +697,12 @@
     )
     rows, factors = ready(image_counts, tokens_late, cotangent_late, mod_late, share)
     near_parts = attend_near(image_counts, gains, first, mine, second)
-    _, _, w_parts_late, w_out_late = lax.optimization_barrier((mine, mine, w_parts, w_out))
-    w_parts_far, w_out_far = (
-        lax.ppermute(w, "core", [(0, 1), (1, 0)]) for w in (w_parts_late, w_out_late)
-    )
+    _, w_parts_late, w_out_late = lax.optimization_barrier((mine, w_parts, w_out))
+    weights = pack(w_parts_late, w_out_late)
+    weights_far = lax.ppermute(weights, "core", [(0, 1), (1, 0)])
     parts = attend_far(image_counts, gains, far, mine, near_parts)
     parts = lax.all_to_all(parts, ("yl", "core"), 0, 0)
-    partial = project(parts, w_out, w_parts, w_out_far, w_parts_far, x_count)
+    partial = project(parts, weights, weights_far, x_count)
     shares = lax.all_to_all(partial, "x", 0, 0)
     return leave(rows, factors, shares)
 

time: 67.1 us -> 65.8 us (0.981)
  the two profiles are of different devices: /device:TPU:48 before, /device:TPU:8 now
where the time goes in v3:
time: 65.8 us; the launch traced here: 65.4 us
  blocking collectives  21.7 us (33%)
  starting transfers between devices  18.2 us (28%)
  Pallas kernels  14.8 us (22%)
  waiting for transfers between devices  9.9 us (15%)
  between operations  0.79 us (1%)
    all_to_all x1, blocking collectives, per_device(): mine = lax.all_to_all(heads, ('yh', 'yl'), 0, 0)  14.4 us
    ppermute x2, starting transfers between devices, per_device(): lax.ppermute(mine, 'z', pairs + [(j, i) for i, j in pairs])  10 us
    all_to_all x1, waiting for transfers between devices, per_device(): shares = lax.all_to_all(partial, 'x', 0, 0)  7.62 us
    all_to_all x1, blocking collectives, per_device(): parts = lax.all_to_all(parts, ('yl', 'core'), 0, 0)  7.26 us
    pallas_call x1, Pallas kernels, attend_near(): pl.pallas_call(near_kernel, out_shape=(head_rows,) * 4 + (jax.ShapeDtypeS...  4.75 us
    all_to_all x1, starting transfers between devices, per_device(): shares = lax.all_to_all(partial, 'x', 0, 0)  4.29 us
    pallas_call x1, Pallas kernels, enter(): pl.pallas_call(enter_kernel, out_shape=jax.ShapeDtypeStruct((quad, tokens...  3.62 us
    pallas_call x1, Pallas kernels, attend_far(): pl.pallas_call(far_kernel, out_shape=jax.ShapeDtypeStruct((4, CHUNK // 4,...  2.72 us
  transfers between devices with their start and end apart: 5, of which 3 were waited for; matrix products, arithmetic and copies ran while one was open for 0% of the time, Pallas kernels for 13%

profile of v3, /device:TPU:8, one launch (start us, length us, event | category | flops | bytes accessed | tf_op | source)
XLA Modules:
  0.0 65.4 jit_solution(13090339457007702588)
XLA Ops:
  0.6 0.0 copy-start.6
  0.6 0.0 copy-start
  0.7 0.0 copy-start.1
  0.7 3.6 %shard_map.86 = bf16[4,128,256]{2,1,0:T(8,128)(2,1)} custom-call(s32[32]{0:T(128)} %counts_ref.7, bf16[128,1536]{1,0:T(8,128)(2,1)} %tokens_ref.2, bf16[128,1536]{1,0:T(8,128)(2,1)} %cotangent_ref.2, bf16[3,1536,128]{2,1,0:T(8,128)(2,1)} %bitcast.4, bf16[128,1536]{1,0:T(8,128)(2,1)} %w_out_ref.2, bf16[3,32,1536]{2,1,0:T(8,128)(2,1)} %bitcast.6), custom_call_target="tpu_custom_call" | custom-call | tf_op jit(solution)/shard_map/pallas_call | solution.py:93
  4.3 14.4 %all_to_all.15 = bf16[4,128,256]{2,1,0:T(8,128)(2,1)S(1)} all-to-all(bf16[4,128,256]{2,1,0:T(8,128)(2,1)} %shard_map.86), channel_id=1, replica_groups=mesh['z'=16,'yh'=2,'yl'=2,'x'=4,'core'=2] {'yh','yl'}, dimensions={0} | all-to-all | bytes 524288 | tf_op jit(solution)/shard_map/all_to_all | solution.py:676
  18.7 1.9 %collective-permute-start.1 = (bf16[512,256]{1,0:T(8,128)(2,1)S(1)}, bf16[512,256]{1,0:T(8,128)(2,1)S(1)}, u32[]{:S(2)}, u32[]{:S(2)}) collective-permute-start(bf16[512,256]{1,0:T(8,128)(2,1)S(1)} %bitcast.8), channel_id=1, source_target_pairs={{0,32},{64,96},{128,160},{192,224},{256,288},{320,352},{384,416},{... | collective-permute-start | bytes 786440 | tf_op jit(solution)/shard_map/ppermute | solution.py:681
  20.6 8.1 %collective-permute-start.2 = (bf16[512,256]{1,0:T(8,128)(2,1)S(1)}, bf16[512,256]{1,0:T(8,128)(2,1)S(1)}, u32[]{:S(2)}, u32[]{:S(2)}) collective-permute-start(bf16[512,256]{1,0:T(8,128)(2,1)S(1)} %bitcast.9), channel_id=1, source_target_pairs={{480,0},{32,64},{96,128},{160,192},{224,256},{288,320},{352,384},{... | collective-permute-start | bytes 786440 | tf_op jit(solution)/shard_map/ppermute | solution.py:681
  28.7 0.0 copy-done.6
  28.8 0.0 copy-done
  28.8 0.0 copy-done.1
  28.8 0.0 copy-start.5
  28.8 0.5 shard_map.90.weights_ref
  29.3 1.9 %collective-permute-start.3 = (bf16[4,1536,128]{2,1,0:T(8,128)(2,1)S(1)}, bf16[4,1536,128]{2,1,0:T(8,128)(2,1)S(1)}, u32[]{:S(2)}, u32[]{:S(2)}) collective-permute-start(bf16[4,1536,128]{2,1,0:T(8,128)(2,1)S(1)} %shard_map.90.weights_ref), channel_id=1, source_target_pairs={{0,1},{1,0},{2,3},{3,2},{4,5},{5,4},{6,7},{7,6},{8,9},{9,8},{10,11... | collective-permute-start | bytes 4718600 | tf_op jit(solution)/shard_map/ppermute | solution.py:702
  31.2 1.9 %collective-permute-start = (bf16[256,256]{1,0:T(8,128)(2,1)S(1)}, bf16[256,256]{1,0:T(8,128)(2,1)S(1)}, u32[]{:S(2)}, u32[]{:S(2)}) collective-permute-start(bf16[256,256]{1,0:T(8,128)(2,1)S(1)} %bitcast.12), channel_id=1, source_target_pairs={{448,0},{465,1},{80,16},{65,17},{480,32},{497,33},{112,48},{97,49}... | collective-permute-start | bytes 393224 | tf_op jit(solution)/shard_map/ppermute | solution.py:692
  33.2 0.0 collective-permute-done.1.first_ref
  33.2 0.3 collective-permute-done.2.second_ref
  33.4 0.0 copy-done.5
  33.4 4.7 %shard_map.88 = (bf16[1536,128]{1,0:T(8,128)(2,1)S(1)}, bf16[1536,128]{1,0:T(8,128)(2,1)S(1)}, bf16[1536,128]{1,0:T(8,128)(2,1)S(1)}, bf16[1536,128]{1,0:T(8,128...) custom-call(s32[32]{0:T(128)S(1)} %copy-done.5, ...), custom_call_target="tpu_custom_call" | custom-call | flops 7000000000 | bytes 1048576 | tf_op jit(solution)/shard_map/pallas_call | solution.py:316
  38.2 2.0 %collective-permute-done.far_ref = bf16[256,256]{1,0:T(8,128)(2,1)S(1)} collective-permute-done((bf16[256,256]{1,0:T(8,128)(2,1)S(1)}, bf16[256,256]{1,0:T(8,128)(2,1)S(1)}, u32[]{:S(2)}, u32[]{:S(2)}) %collective-permute-start) | collective-permute-done | bytes 131104 | tf_op jit(solution)/shard_map/ppermute | solution.py:692
  40.2 2.7 %shard_map.89 = bf16[4,64,256]{2,1,0:T(8,128)(2,1)S(1)} custom-call(s32[32]{0:T(128)S(1)} %copy-done.5, f32[8,128]{1,0:T(8,128)S(1)} %pad.4.gains_ref, bf16[256,256]{1,0:T(8,128)(2,1)S(1)} %collective-permute-done.far_ref, bf16[512,256]{1,0:T(8,128)(2,1)S(1)} %bitcast.11, bf16[1536,128]{1,0:T(8,128)(2,1)S(1)} %get-tuple-element.24.qx_ref, ...), custom_call_target="tpu_custom_call" | custom-call | flops 7000000000 | bytes 1048576 | tf_op jit(solution)/shard_map/pallas_call | solution.py:534
  42.9 7.3 %all_to_all.16.parts_ref = bf16[4,64,256]{2,1,0:T(8,128)(2,1)S(1)} all-to-all(bf16[4,64,256]{2,1,0:T(8,128)(2,1)S(1)} %shard_map.89), channel_id=1, replica_groups=mesh['z'=16,'yh'=2,'yl'=2,'x'=4,'core'=2] {'yl','core'}, dimensions={0} | all-to-all | bytes 262144 | tf_op jit(solution)/shard_map/all_to_all | solution.py:704
  50.2 0.0 copy-start.2
  50.2 0.0 copy-start.3
  50.2 0.0 copy-start.4
  50.2 0.0 collective-permute-done.3.weights_far_ref
  50.2 1.8 %shard_map.91 = bf16[4,16,3072]{2,1,0:T(8,128)(2,1)} custom-call(bf16[4,64,256]{2,1,0:T(8,128)(2,1)S(1)} %all_to_all.16.parts_ref, bf16[4,1536,128]{2,1,0:T(8,128)(2,1)S(1)} %shard_map.90.weights_ref, bf16[4,1536,128]{2,1,0:T(8,128)(2,1)S(1)} %collective-permute-done.3.weights_far_ref), custom_call_target="tpu_custom_call" | custom-call | tf_op jit(solution)/shard_map/pallas_call | solution.py:589
  52.0 4.3 %all-to-all-start.2 = ((bf16[4,16,3072]{2,1,0:T(8,128)(2,1)}), bf16[4,16,3072]{2,1,0:T(8,128)(2,1)S(1)}, u32[]{:S(2)}, u32[]{:S(2)}) async-start(bf16[4,16,3072]{2,1,0:T(8,128)(2,1)} %shard_map.91), calls=%async_computation.2 | async-start | bytes 786432 | tf_op jit(solution)/shard_map/all_to_all | solution.py:706
  56.2 0.0 copy-done.2
  56.3 0.0 copy-done.3
  56.3 0.0 copy-done.4
  56.3 0.8 %shard_map.87 = (bf16[2,16,1536]{2,1,0:T(8,128)(2,1)S(1)}, f32[4,16,1536]{2,1,0:T(8,128)S(1)}) custom-call(s32[32]{0:T(128)S(1)} %copy-done.5, bf16[128,1536]{1,0:T(8,128)(2,1)S(1)} %copy-done.2, bf16[128,1536]{1,0:T(8,128)(2,1)S(1)} %copy-done.3, bf16[3,32,1536]{2,1,0:T(8,128)(2,1)S(1)} %bitcast.7), custom_call_target="tpu_custom_call" | custom-call | tf_op jit(solution)/shard_map/pallas_call | solution.py:624
  57.0 7.6 %all-to-all-done.2.shares_ref = bf16[4,16,3072]{2,1,0:T(8,128)(2,1)S(1)} async-done(((bf16[4,16,3072]{2,1,0:T(8,128)(2,1)}), bf16[4,16,3072]{2,1,0:T(8,128)(2,1)S(1)}, u32[]{:S(2)}, u32[]{:S(2)}) %all-to-all-start.2) | async-done | bytes 393248 | tf_op jit(solution)/shard_map/all_to_all | solution.py:706
  64.7 0.7 %shard_map.92 = (bf16[16,1536]{1,0:T(8,128)(2,1)}, bf16[16,1536]{1,0:T(8,128)(2,1)}) custom-call(bf16[2,16,1536]{2,1,0:T(8,128)(2,1)S(1)} %get-tuple-element.22.rows_ref, f32[4,16,1536]{2,1,0:T(8,128)S(1)} %get-tuple-element.23.factors_ref, bf16[4,16,3072]{2,1,0:T(8,128)(2,1)S(1)} %all-to-all-done.2.shares_ref), custom_call_target="tpu_custom_call" | custom-call | tf_op jit(solution)/shard_map/pallas_call | solution.py:655
  (2 shorter events, 0.0 us)
Async XLA Ops:
  0.6 28.1 %copy-start.6 = (f32[2,64]{1,0:T(2,128)S(1)}, f32[2,64]{1,0:T(2,128)}, u32[]{:S(2)}) copy-start(f32[2,64]{1,0:T(2,128)} %param.11) | copy-start | bytes 1540
  0.6 28.1 %copy-start = (bf16[1536,3,128]{2,0,1:T(8,128)(2,1)S(1)}, bf16[1536,3,128]{2,0,1:T(8,128)(2,1)}, u32[]{:S(2)}) copy-start(bf16[1536,3,128]{2,0,1:T(8,128)(2,1)} %param.9) | copy-start | bytes 3538948
  0.7 28.1 %copy-start.1 = (bf16[128,1536]{1,0:T(8,128)(2,1)S(1)}, bf16[128,1536]{1,0:T(8,128)(2,1)}, u32[]{:S(2)}) copy-start(bf16[128,1536]{1,0:T(8,128)(2,1)} %w_out_ref.2) | copy-start | bytes 1179652
  18.7 14.5 %collective-permute-start.1 = (bf16[512,256]{1,0:T(8,128)(2,1)S(1)}, bf16[512,256]{1,0:T(8,128)(2,1)S(1)}, u32[]{:S(2)}, u32[]{:S(2)}) collective-permute-start(bf16[512,256]{1,0:T(8,128)(2,1)S(1)} %bitcast.8), channel_id=1, source_target_pairs={{0,32},{64,96},{128,160},{192,224},{256,288},{320,352},{384,416},{... | collective-permute-start | bytes 786440 | tf_op jit(solution)/shard_map/ppermute | solution.py:681
  20.6 12.8 %collective-permute-start.2 = (bf16[512,256]{1,0:T(8,128)(2,1)S(1)}, bf16[512,256]{1,0:T(8,128)(2,1)S(1)}, u32[]{:S(2)}, u32[]{:S(2)}) collective-permute-start(bf16[512,256]{1,0:T(8,128)(2,1)S(1)} %bitcast.9), channel_id=1, source_target_pairs={{480,0},{32,64},{96,128},{160,192},{224,256},{288,320},{352,384},{... | collective-permute-start | bytes 786440 | tf_op jit(solution)/shard_map/ppermute | solution.py:681
  28.8 4.6 %copy-start.5 = (s32[32]{0:T(128)S(1)}, s32[32]{0:T(128)}, u32[]{:S(2)}) copy-start(s32[32]{0:T(128)} %counts_ref.7) | copy-start | bytes 388
  29.3 20.9 %collective-permute-start.3 = (bf16[4,1536,128]{2,1,0:T(8,128)(2,1)S(1)}, bf16[4,1536,128]{2,1,0:T(8,128)(2,1)S(1)}, u32[]{:S(2)}, u32[]{:S(2)}) collective-permute-start(bf16[4,1536,128]{2,1,0:T(8,128)(2,1)S(1)} %shard_map.90.weights_ref), channel_id=1, source_target_pairs={{0,1},{1,0},{2,3},{3,2},{4,5},{5,4},{6,7},{7,6},{8,9},{9,8},{10,11... | collective-permute-start | bytes 4718600 | tf_op jit(solution)/shard_map/ppermute | solution.py:702
  31.2 9.0 %collective-permute-start = (bf16[256,256]{1,0:T(8,128)(2,1)S(1)}, bf16[256,256]{1,0:T(8,128)(2,1)S(1)}, u32[]{:S(2)}, u32[]{:S(2)}) collective-permute-start(bf16[256,256]{1,0:T(8,128)(2,1)S(1)} %bitcast.12), channel_id=1, source_target_pairs={{448,0},{465,1},{80,16},{65,17},{480,32},{497,33},{112,48},{97,49}... | collective-permute-start | bytes 393224 | tf_op jit(solution)/shard_map/ppermute | solution.py:692
  50.2 6.1 %copy-start.2 = (bf16[128,1536]{1,0:T(8,128)(2,1)S(1)}, bf16[128,1536]{1,0:T(8,128)(2,1)}, u32[]{:S(2)}) copy-start(bf16[128,1536]{1,0:T(8,128)(2,1)} %tokens_ref.2) | copy-start | bytes 1179652
  50.2 6.1 %copy-start.3 = (bf16[128,1536]{1,0:T(8,128)(2,1)S(1)}, bf16[128,1536]{1,0:T(8,128)(2,1)}, u32[]{:S(2)}) copy-start(bf16[128,1536]{1,0:T(8,128)(2,1)} %cotangent_ref.2) | copy-start | bytes 1179652
  50.2 6.1 %copy-start.4 = (bf16[32,3,1536]{2,0,1:T(8,128)(2,1)S(1)}, bf16[32,3,1536]{2,0,1:T(8,128)(2,1)}, u32[]{:S(2)}) copy-start(bf16[32,3,1536]{2,0,1:T(8,128)(2,1)} %param.12) | copy-start | bytes 884740
  52.0 12.7 %all-to-all-start.2 = ((bf16[4,16,3072]{2,1,0:T(8,128)(2,1)}), bf16[4,16,3072]{2,1,0:T(8,128)(2,1)S(1)}, u32[]{:S(2)}, u32[]{:S(2)}) async-start(bf16[4,16,3072]{2,1,0:T(8,128)(2,1)} %shard_map.91), calls=%async_computation.2 | async-start | bytes 786432 | tf_op jit(solution)/shard_map/all_to_all | solution.py:706

commit v4 on v3

--- a/solution.py
+++ b/solution.py
@@ -57,26 +57,49 @@
     return centred * inv_std, inv_std
 
 
-def w_out_of(weights_ref):
-    tiles = weights_ref.shape[1] // LANES
-    return jnp.concatenate(
-        [weights_ref[3, tile * LANES : (tile + 1) * LANES, :] for tile in range(tiles)], axis=1
-    )
-
-
 def enter_kernel(
-    counts_ref, tokens_ref, cotangent_ref, w_qkv_ref, w_out_ref, modulation_ref, out_ref
+    counts_ref,
+    tokens_hbm,
+    cotangent_hbm,
+    w_qkv_hbm,
+    w_out_hbm,
+    modulation_hbm,
+    out_ref,
+    tokens_ref,
+    cotangent_ref,
+    w_qkv_ref,
+    w_out_ref,
+    modulation_ref,
+    sems,
 ):
+    pairs = [
+        (tokens_hbm, tokens_ref),
+        (modulation_hbm, modulation_ref),
+        (cotangent_hbm, cotangent_ref),
+        (w_out_hbm, w_out_ref),
+        (w_qkv_hbm, w_qkv_ref),
+    ]
+    copies = [
+        pltpu.make_async_copy(source, target, sems.at[place])
+        for place, (source, target) in enumerate(pairs)
+    ]
+    for copy in copies:
+        copy.start()
     rows = tokens_ref.shape[0]
     first = block_index() * rows
+    copies[0].wait()
+    normed, _ = layer_norm(tokens_ref[...].astype(F32))
+    copies[1].wait()
     shift, scale, gate = modulation_rows(counts_ref, modulation_ref, first, rows)
-    normed, _ = layer_norm(tokens_ref[...].astype(F32))
     hidden = (normed * (1.0 + scale) + shift).astype(BF16)
+    copies[2].wait()
+    d_mixed = (cotangent_ref[...].astype(F32) * gate).astype(BF16)
+    copies[3].wait()
+    d_attn = rows_dot(d_mixed, w_out_ref[...])
+    copies[4].wait()
     weights = jnp.concatenate([w_qkv_ref[part] for part in range(3)], axis=1)
     qkv = jnp.dot(hidden, weights, preferred_element_type=F32)
     q, k, v = (qkv[:, part * LANES : (part + 1) * LANES] for part in range(3))
-    d_mixed = (cotangent_ref[...].astype(F32) * gate).astype(BF16)
-    d_attn = rows_dot(d_mixed, w_out_ref[...])
     low = lax.broadcasted_iota(jnp.int32, (rows, LANES), 1) < HEAD
 
     def beside(left, right):
@@ -90,13 +113,17 @@
 
 
 def enter(counts, tokens, cotangent, w_parts, w_out, modulation, quad):
+    whole = pl.BlockSpec(memory_space=pl.ANY)
+    operands = (tokens, cotangent, w_parts, w_out, modulation)
     return pl.pallas_call(
         enter_kernel,
         out_shape=jax.ShapeDtypeStruct((quad, tokens.shape[0], 2 * LANES), BF16),
-        in_specs=[SMEM] + [VMEM] * 5,
+        in_specs=[SMEM] + [whole] * 5,
         out_specs=VMEM,
+        scratch_shapes=[pltpu.VMEM(operand.shape, BF16) for operand in operands]
+        + [pltpu.SemaphoreType.DMA((5,))],
         compiler_params=pltpu.CompilerParams(vmem_limit_bytes=ENTER_LIMIT),
-    )(counts, tokens, cotangent, w_parts, w_out, modulation)
+    )(counts, *operands)
 
 
 def pack_kernel(w_qkv_ref, w_out_ref, weights_ref, sems):
@@ -322,7 +349,7 @@
         out_specs=(VMEM,) * 10,
         scratch_shapes=[pltpu.VMEM((REACH_CHUNKS * CHUNK, CHUNK), F32)] * 2,
         cost_estimate=pl.CostEstimate(
-            flops=7000000000, bytes_accessed=1 << 20, transcendentals=1 << 20
+            flops=9000000000, bytes_accessed=1 << 20, transcendentals=1 << 20
         ),
         compiler_params=pltpu.CompilerParams(vmem_limit_bytes=VMEM_LIMIT),
     )(counts, gains, first, quad, second)
@@ -544,7 +571,7 @@
         + [pltpu.VMEM((CHUNK, LANES), F32)] * 2
         + [pltpu.VMEM((CHUNK, 2 * LANES), BF16)],
         cost_estimate=pl.CostEstimate(
-            flops=7000000000, bytes_accessed=1 << 20, transcendentals=1 << 20
+            flops=9000000000, bytes_accessed=1 << 20, transcendentals=1 << 20
         ),
         compiler_params=pltpu.CompilerParams(vmem_limit_bytes=VMEM_LIMIT),
     )(counts, gains, far, quad, *near_parts)

time: 65.8 us -> 64.9 us (0.986)
    ppermute x2, waiting for transfers between devices: 0.27 us -> 2.33 us  [per_device(): lax.ppermute(mine, 'z', pairs + [(j, i) for i, j in pairs])]
    ppermute x1, waiting for transfers between devices: 2.01 us -> 0.01 us  [per_device(): lax.ppermute(far_half, ('z', 'yh', 'core'), [(far_source(i), i) for i in...]
    pallas_call x1, Pallas kernels: 3.62 us -> 4.28 us  [enter(): pl.pallas_call(enter_kernel, out_shape=jax.ShapeDtypeStruct((quad, tokens...]
    pallas_call x1, Pallas kernels: 4.75 us -> 4.08 us  [attend_near(): pl.pallas_call(near_kernel, out_shape=(head_rows,) * 4 + (jax.ShapeDtypeS...]
  transfers between devices with their start and end apart: 5 -> 5, of which waited for: 3 -> 2; matrix products, arithmetic and copies ran while one was open for 0% -> 0% of each run, Pallas kernels for 13% -> 12%
where the time goes in v4:
time: 64.9 us; the launch traced here: 64.5 us
  blocking collectives  21.2 us (33%)
  starting transfers between devices  18.1 us (28%)
  Pallas kernels  14.6 us (22%)
  waiting for transfers between devices  9.69 us (15%)
  between operations  0.81 us (1%)
    all_to_all x1, blocking collectives, per_device(): mine = lax.all_to_all(heads, ('yh', 'yl'), 0, 0)  14.4 us
    ppermute x2, starting transfers between devices, per_device(): lax.ppermute(mine, 'z', pairs + [(j, i) for i, j in pairs])  10 us
    all_to_all x1, waiting for transfers between devices, per_device(): shares = lax.all_to_all(partial, 'x', 0, 0)  7.35 us
    all_to_all x1, blocking collectives, per_device(): parts = lax.all_to_all(parts, ('yl', 'core'), 0, 0)  6.74 us
    all_to_all x1, starting transfers between devices, per_device(): shares = lax.all_to_all(partial, 'x', 0, 0)  4.3 us
    pallas_call x1, Pallas kernels, enter(): pl.pallas_call(enter_kernel, out_shape=jax.ShapeDtypeStruct((quad, tokens...  4.28 us
    pallas_call x1, Pallas kernels, attend_near(): pl.pallas_call(near_kernel, out_shape=(head_rows,) * 4 + (jax.ShapeDtypeS...  4.08 us
    pallas_call x1, Pallas kernels, attend_far(): pl.pallas_call(far_kernel, out_shape=jax.ShapeDtypeStruct((4, CHUNK // 4,...  2.52 us
  transfers between devices with their start and end apart: 5, of which 2 were waited for; matrix products, arithmetic and copies ran while one was open for 0% of the time, Pallas kernels for 12%

profile of v4, /device:TPU:8, one launch (start us, length us, event | category | flops | bytes accessed | tf_op | source)
XLA Modules:
  0.0 64.5 jit_solution(10727288978897981123)
XLA Ops:
  0.6 0.0 copy-start.6
  0.6 0.0 copy-start
  0.7 0.0 copy-start.1
  0.7 4.3 %shard_map.86 = bf16[4,128,256]{2,1,0:T(8,128)(2,1)} custom-call(s32[32]{0:T(128)} %counts_ref.7, bf16[128,1536]{1,0:T(8,128)(2,1)} %tokens_ref, bf16[128,1536]{1,0:T(8,128)(2,1)} %cotangent_ref, bf16[3,1536,128]{2,1,0:T(8,128)(2,1)} %bitcast.4, bf16[128,1536]{1,0:T(8,128)(2,1)} %w_out_ref, bf16[3,32,1536]{2,1,0:T(8,128)(2,1)} %bitcast.6), custom_call_target="tpu_custom_call" | custom-call | tf_op jit(solution)/shard_map/pallas_call | solution.py:118
  5.0 14.4 %all_to_all.15 = bf16[4,128,256]{2,1,0:T(8,128)(2,1)S(1)} all-to-all(bf16[4,128,256]{2,1,0:T(8,128)(2,1)} %shard_map.86), channel_id=1, replica_groups=mesh['z'=16,'yh'=2,'yl'=2,'x'=4,'core'=2] {'yh','yl'}, dimensions={0} | all-to-all | bytes 524288 | tf_op jit(solution)/shard_map/all_to_all | solution.py:703
  19.4 1.9 %collective-permute-start.1 = (bf16[512,256]{1,0:T(8,128)(2,1)S(1)}, bf16[512,256]{1,0:T(8,128)(2,1)S(1)}, u32[]{:S(2)}, u32[]{:S(2)}) collective-permute-start(bf16[512,256]{1,0:T(8,128)(2,1)S(1)} %bitcast.8), channel_id=1, source_target_pairs={{0,32},{64,96},{128,160},{192,224},{256,288},{320,352},{384,416},{... | collective-permute-start | bytes 786440 | tf_op jit(solution)/shard_map/ppermute | solution.py:708
  21.3 8.1 %collective-permute-start.2 = (bf16[512,256]{1,0:T(8,128)(2,1)S(1)}, bf16[512,256]{1,0:T(8,128)(2,1)S(1)}, u32[]{:S(2)}, u32[]{:S(2)}) collective-permute-start(bf16[512,256]{1,0:T(8,128)(2,1)S(1)} %bitcast.9), channel_id=1, source_target_pairs={{480,0},{32,64},{96,128},{160,192},{224,256},{288,320},{352,384},{... | collective-permute-start | bytes 786440 | tf_op jit(solution)/shard_map/ppermute | solution.py:708
  29.4 0.0 copy-done.6
  29.5 0.0 copy-start.5
  29.5 1.9 %collective-permute-start = (bf16[256,256]{1,0:T(8,128)(2,1)S(1)}, bf16[256,256]{1,0:T(8,128)(2,1)S(1)}, u32[]{:S(2)}, u32[]{:S(2)}) collective-permute-start(bf16[256,256]{1,0:T(8,128)(2,1)S(1)} %bitcast.12), channel_id=1, source_target_pairs={{448,0},{465,1},{80,16},{65,17},{480,32},{497,33},{112,48},{97,49}... | collective-permute-start | bytes 393224 | tf_op jit(solution)/shard_map/ppermute | solution.py:719
  31.4 0.0 copy-done
  31.4 0.0 copy-done.1
  31.4 0.5 shard_map.90.weights_ref
  31.9 1.9 %collective-permute-start.3 = (bf16[4,1536,128]{2,1,0:T(8,128)(2,1)S(1)}, bf16[4,1536,128]{2,1,0:T(8,128)(2,1)S(1)}, u32[]{:S(2)}, u32[]{:S(2)}) collective-permute-start(bf16[4,1536,128]{2,1,0:T(8,128)(2,1)S(1)} %shard_map.90.weights_ref), channel_id=1, source_target_pairs={{0,1},{1,0},{2,3},{3,2},{4,5},{5,4},{6,7},{7,6},{8,9},{9,8},{10,11... | collective-permute-start | bytes 4718600 | tf_op jit(solution)/shard_map/ppermute | solution.py:729
  33.8 0.0 collective-permute-done.1.first_ref
  33.8 2.3 %collective-permute-done.2.second_ref = bf16[512,256]{1,0:T(8,128)(2,1)S(1)} collective-permute-done((bf16[512,256]{1,0:T(8,128)(2,1)S(1)}, bf16[512,256]{1,0:T(8,128)(2,1)S(1)}, u32[]{:S(2)}, u32[]{:S(2)}) %collective-permute-start.2) | collective-permute-done | bytes 262176 | tf_op jit(solution)/shard_map/ppermute | solution.py:708
  36.2 0.0 copy-done.5
  36.2 4.1 %shard_map.88 = (bf16[1536,128]{1,0:T(8,128)(2,1)S(1)}, bf16[1536,128]{1,0:T(8,128)(2,1)S(1)}, bf16[1536,128]{1,0:T(8,128)(2,1)S(1)}, bf16[1536,128]{1,0:T(8,128...) custom-call(s32[32]{0:T(128)S(1)} %copy-done.5, ...), custom_call_target="tpu_custom_call" | custom-call | flops 8999999488 | bytes 1048576 | tf_op jit(solution)/shard_map/pallas_call | solution.py:343
  40.3 0.0 collective-permute-done.far_ref
  40.3 2.5 %shard_map.89 = bf16[4,64,256]{2,1,0:T(8,128)(2,1)S(1)} custom-call(s32[32]{0:T(128)S(1)} %copy-done.5, f32[8,128]{1,0:T(8,128)S(1)} %pad.4.gains_ref, bf16[256,256]{1,0:T(8,128)(2,1)S(1)} %collective-permute-done.far_ref, bf16[512,256]{1,0:T(8,128)(2,1)S(1)} %bitcast.11, bf16[1536,128]{1,0:T(8,128)(2,1)S(1)} %get-tuple-element.24.qx_ref, ...), custom_call_target="tpu_custom_call" | custom-call | flops 8999999488 | bytes 1048576 | tf_op jit(solution)/shard_map/pallas_call | solution.py:561
  42.8 6.7 %all_to_all.16.parts_ref = bf16[4,64,256]{2,1,0:T(8,128)(2,1)S(1)} all-to-all(bf16[4,64,256]{2,1,0:T(8,128)(2,1)S(1)} %shard_map.89), channel_id=1, replica_groups=mesh['z'=16,'yh'=2,'yl'=2,'x'=4,'core'=2] {'yl','core'}, dimensions={0} | all-to-all | bytes 262144 | tf_op jit(solution)/shard_map/all_to_all | solution.py:731
  49.5 0.0 copy-start.2
  49.5 0.0 copy-start.3
  49.5 0.0 copy-start.4
  49.5 0.0 collective-permute-done.3.weights_far_ref
  49.5 1.8 %shard_map.91 = bf16[4,16,3072]{2,1,0:T(8,128)(2,1)} custom-call(bf16[4,64,256]{2,1,0:T(8,128)(2,1)S(1)} %all_to_all.16.parts_ref, bf16[4,1536,128]{2,1,0:T(8,128)(2,1)S(1)} %shard_map.90.weights_ref, bf16[4,1536,128]{2,1,0:T(8,128)(2,1)S(1)} %collective-permute-done.3.weights_far_ref), custom_call_target="tpu_custom_call" | custom-call | tf_op jit(solution)/shard_map/pallas_call | solution.py:616
  51.3 4.3 %all-to-all-start.2 = ((bf16[4,16,3072]{2,1,0:T(8,128)(2,1)}), bf16[4,16,3072]{2,1,0:T(8,128)(2,1)S(1)}, u32[]{:S(2)}, u32[]{:S(2)}) async-start(bf16[4,16,3072]{2,1,0:T(8,128)(2,1)} %shard_map.91), calls=%async_computation.2 | async-start | bytes 786432 | tf_op jit(solution)/shard_map/all_to_all | solution.py:733
  55.6 0.0 copy-done.2
  55.6 0.0 copy-done.3
  55.6 0.0 copy-done.4
  55.6 0.8 %shard_map.87 = (bf16[2,16,1536]{2,1,0:T(8,128)(2,1)S(1)}, f32[4,16,1536]{2,1,0:T(8,128)S(1)}) custom-call(s32[32]{0:T(128)S(1)} %copy-done.5, bf16[128,1536]{1,0:T(8,128)(2,1)S(1)} %copy-done.2, bf16[128,1536]{1,0:T(8,128)(2,1)S(1)} %copy-done.3, bf16[3,32,1536]{2,1,0:T(8,128)(2,1)S(1)} %bitcast.7), custom_call_target="tpu_custom_call" | custom-call | tf_op jit(solution)/shard_map/pallas_call | solution.py:651
  56.4 7.3 %all-to-all-done.2.shares_ref = bf16[4,16,3072]{2,1,0:T(8,128)(2,1)S(1)} async-done(((bf16[4,16,3072]{2,1,0:T(8,128)(2,1)}), bf16[4,16,3072]{2,1,0:T(8,128)(2,1)S(1)}, u32[]{:S(2)}, u32[]{:S(2)}) %all-to-all-start.2) | async-done | bytes 393248 | tf_op jit(solution)/shard_map/all_to_all | solution.py:733
  63.7 0.7 %shard_map.92 = (bf16[16,1536]{1,0:T(8,128)(2,1)}, bf16[16,1536]{1,0:T(8,128)(2,1)}) custom-call(bf16[2,16,1536]{2,1,0:T(8,128)(2,1)S(1)} %get-tuple-element.22.rows_ref, f32[4,16,1536]{2,1,0:T(8,128)S(1)} %get-tuple-element.23.factors_ref, bf16[4,16,3072]{2,1,0:T(8,128)(2,1)S(1)} %all-to-all-done.2.shares_ref), custom_call_target="tpu_custom_call" | custom-call | tf_op jit(solution)/shard_map/pallas_call | solution.py:682
  (2 shorter events, 0.0 us)
Async XLA Ops:
  0.6 28.8 %copy-start.6 = (f32[2,64]{1,0:T(2,128)S(1)}, f32[2,64]{1,0:T(2,128)}, u32[]{:S(2)}) copy-start(f32[2,64]{1,0:T(2,128)} %param.11) | copy-start | bytes 1540
  0.6 30.8 %copy-start = (bf16[1536,3,128]{2,0,1:T(8,128)(2,1)S(1)}, bf16[1536,3,128]{2,0,1:T(8,128)(2,1)}, u32[]{:S(2)}) copy-start(bf16[1536,3,128]{2,0,1:T(8,128)(2,1)} %param.9) | copy-start | bytes 3538948
  0.7 30.8 %copy-start.1 = (bf16[128,1536]{1,0:T(8,128)(2,1)S(1)}, bf16[128,1536]{1,0:T(8,128)(2,1)}, u32[]{:S(2)}) copy-start(bf16[128,1536]{1,0:T(8,128)(2,1)} %w_out_ref) | copy-start | bytes 1179652
  19.4 14.4 %collective-permute-start.1 = (bf16[512,256]{1,0:T(8,128)(2,1)S(1)}, bf16[512,256]{1,0:T(8,128)(2,1)S(1)}, u32[]{:S(2)}, u32[]{:S(2)}) collective-permute-start(bf16[512,256]{1,0:T(8,128)(2,1)S(1)} %bitcast.8), channel_id=1, source_target_pairs={{0,32},{64,96},{128,160},{192,224},{256,288},{320,352},{384,416},{... | collective-permute-start | bytes 786440 | tf_op jit(solution)/shard_map/ppermute | solution.py:708
  21.3 14.9 %collective-permute-start.2 = (bf16[512,256]{1,0:T(8,128)(2,1)S(1)}, bf16[512,256]{1,0:T(8,128)(2,1)S(1)}, u32[]{:S(2)}, u32[]{:S(2)}) collective-permute-start(bf16[512,256]{1,0:T(8,128)(2,1)S(1)} %bitcast.9), channel_id=1, source_target_pairs={{480,0},{32,64},{96,128},{160,192},{224,256},{288,320},{352,384},{... | collective-permute-start | bytes 786440 | tf_op jit(solution)/shard_map/ppermute | solution.py:708
  29.5 6.7 %copy-start.5 = (s32[32]{0:T(128)S(1)}, s32[32]{0:T(128)}, u32[]{:S(2)}) copy-start(s32[32]{0:T(128)} %counts_ref.7) | copy-start | bytes 388
  29.5 10.8 %collective-permute-start = (bf16[256,256]{1,0:T(8,128)(2,1)S(1)}, bf16[256,256]{1,0:T(8,128)(2,1)S(1)}, u32[]{:S(2)}, u32[]{:S(2)}) collective-permute-start(bf16[256,256]{1,0:T(8,128)(2,1)S(1)} %bitcast.12), channel_id=1, source_target_pairs={{448,0},{465,1},{80,16},{65,17},{480,32},{497,33},{112,48},{97,49}... | collective-permute-start | bytes 393224 | tf_op jit(solution)/shard_map/ppermute | solution.py:719
  31.9 17.6 %collective-permute-start.3 = (bf16[4,1536,128]{2,1,0:T(8,128)(2,1)S(1)}, bf16[4,1536,128]{2,1,0:T(8,128)(2,1)S(1)}, u32[]{:S(2)}, u32[]{:S(2)}) collective-permute-start(bf16[4,1536,128]{2,1,0:T(8,128)(2,1)S(1)} %shard_map.90.weights_ref), channel_id=1, source_target_pairs={{0,1},{1,0},{2,3},{3,2},{4,5},{5,4},{6,7},{7,6},{8,9},{9,8},{10,11... | collective-permute-start | bytes 4718600 | tf_op jit(solution)/shard_map/ppermute | solution.py:729
  49.5 6.1 %copy-start.2 = (bf16[128,1536]{1,0:T(8,128)(2,1)S(1)}, bf16[128,1536]{1,0:T(8,128)(2,1)}, u32[]{:S(2)}) copy-start(bf16[128,1536]{1,0:T(8,128)(2,1)} %tokens_ref) | copy-start | bytes 1179652
  49.5 6.1 %copy-start.3 = (bf16[128,1536]{1,0:T(8,128)(2,1)S(1)}, bf16[128,1536]{1,0:T(8,128)(2,1)}, u32[]{:S(2)}) copy-start(bf16[128,1536]{1,0:T(8,128)(2,1)} %cotangent_ref) | copy-start | bytes 1179652
  49.5 6.1 %copy-start.4 = (bf16[32,3,1536]{2,0,1:T(8,128)(2,1)S(1)}, bf16[32,3,1536]{2,0,1:T(8,128)(2,1)}, u32[]{:S(2)}) copy-start(bf16[32,3,1536]{2,0,1:T(8,128)(2,1)} %param.12) | copy-start | bytes 884740
  51.3 12.4 %all-to-all-start.2 = ((bf16[4,16,3072]{2,1,0:T(8,128)(2,1)}), bf16[4,16,3072]{2,1,0:T(8,128)(2,1)S(1)}, u32[]{:S(2)}, u32[]{:S(2)}) async-start(bf16[4,16,3072]{2,1,0:T(8,128)(2,1)} %shard_map.91), calls=%async_computation.2 | async-start | bytes 786432 | tf_op jit(solution)/shard_map/all_to_all | solution.py:733

commit v5 on v3

--- a/solution.py
+++ b/solution.py
@@ -55,13 +55,6 @@
     centred = values - average
     inv_std = lax.rsqrt(jnp.mean(centred * centred, axis=-1, keepdims=True) + EPS)
     return centred * inv_std, inv_std
-
-
-def w_out_of(weights_ref):
-    tiles = weights_ref.shape[1] // LANES
-    return jnp.concatenate(
-        [weights_ref[3, tile * LANES : (tile + 1) * LANES, :] for tile in range(tiles)], axis=1
-    )
 
 
 def enter_kernel(
@@ -285,14 +278,13 @@
             key = jnp.where(begin < own_at, left_key, right_key) * CHUNK
             q_block = qx_ref[at, :]
             d_block = dx_ref[at, :]
+            keys_at = pl.ds(pl.multiple_of(key, CHUNK), REACH_CHUNKS * CHUNK)
+            s_ref[...] = rows_dot(kx_ref[keys_at, :], q_block)
+            g_ref[...] = rows_dot(vx_ref[keys_at, :], d_block)
             highest = jnp.full((8, CHUNK), -jnp.inf, F32)
-            for piece in range(REACH_CHUNKS):
-                keys_at = pl.ds(pl.multiple_of(key + piece * CHUNK, CHUNK), CHUNK)
-                here = slice(piece * CHUNK, (piece + 1) * CHUNK)
-                scores = rows_dot(kx_ref[keys_at, :], q_block)
-                s_ref[here, :] = scores
-                highest = jnp.maximum(highest, rows_max(scores))
-                g_ref[here, :] = rows_dot(vx_ref[keys_at, :], d_block)
+            for piece in range(REACH_CHUNKS * CHUNK // TILE):
+                here = slice(piece * TILE, (piece + 1) * TILE)
+                highest = jnp.maximum(highest, rows_max(s_ref[here, :]))
             highest = jnp.max(highest, axis=0, keepdims=True) * LOG2_E
             zeros = jnp.zeros((8, CHUNK), F32)
             total, grads = add_tiles(s_ref, g_ref, REACH_CHUNKS * CHUNK, highest, zeros, zeros)
@@ -696,6 +688,7 @@
         (mine, tokens, cotangent, mod_parts)
     )
     rows, factors = ready(image_counts, tokens_late, cotangent_late, mod_late, share)
+    first, rows, factors = lax.optimization_barrier((first, rows, factors))
     near_parts = attend_near(image_counts, gains, first, mine, second)
     _, w_parts_late, w_out_late = lax.optimization_barrier((mine, w_parts, w_out))
     weights = pack(w_parts_late, w_out_late)

time: 65.8 us -> 66.6 us (1.012)
  the two profiles are of different devices: /device:TPU:8 before, /device:TPU:64 now
where the time goes in v5:
time: 66.6 us; the launch traced here: 66.2 us
  blocking collectives  33.2 us (50%)
  Pallas kernels  17.6 us (26%)
  starting transfers between devices  14 us (21%)
  between operations  0.85 us (1%)
    all_to_all x1, blocking collectives, per_device(): shares = lax.all_to_all(partial, 'x', 0, 0)  11.8 us
    all_to_all x1, blocking collectives, per_device(): mine = lax.all_to_all(heads, ('yh', 'yl'), 0, 0)  11.1 us
    all_to_all x1, blocking collectives, per_device(): parts = lax.all_to_all(parts, ('yl', 'core'), 0, 0)  10.2 us
    ppermute x2, starting transfers between devices, per_device(): lax.ppermute(mine, 'z', pairs + [(j, i) for i, j in pairs])  8.31 us
    pallas_call x1, Pallas kernels, attend_near(): pl.pallas_call(near_kernel, out_shape=(head_rows,) * 4 + (jax.ShapeDtypeS...  6.17 us
    pallas_call x1, Pallas kernels, attend_far(): pl.pallas_call(far_kernel, out_shape=jax.ShapeDtypeStruct((4, CHUNK // 4,...  4.81 us
    ppermute x1, starting transfers between devices, per_device(): lax.ppermute(far_half, ('z', 'yh', 'core'), [(far_source(i), i) for i in...  3.82 us
    pallas_call x1, Pallas kernels, enter(): pl.pallas_call(enter_kernel, out_shape=jax.ShapeDtypeStruct((quad, tokens...  3.62 us
  transfers between devices with their start and end apart: 4, of which 1 were waited for; matrix products, arithmetic and copies ran while one was open for 0% of the time, Pallas kernels for 18%

profile of v5, /device:TPU:64, one launch (start us, length us, event | category | flops | bytes accessed | tf_op | source)
XLA Modules:
  0.0 66.2 jit_solution(6359280037563709776)
XLA Ops:
  0.6 0.0 copy-start.6
  0.6 0.0 copy-start
  0.7 0.0 copy-start.1
  0.7 3.6 %shard_map.86 = bf16[4,128,256]{2,1,0:T(8,128)(2,1)} custom-call(s32[32]{0:T(128)} %counts_ref.7, bf16[128,1536]{1,0:T(8,128)(2,1)} %tokens_ref.2, bf16[128,1536]{1,0:T(8,128)(2,1)} %cotangent_ref.2, bf16[3,1536,128]{2,1,0:T(8,128)(2,1)} %bitcast.4, bf16[128,1536]{1,0:T(8,128)(2,1)} %w_out_ref.2, bf16[3,32,1536]{2,1,0:T(8,128)(2,1)} %bitcast.6), custom_call_target="tpu_custom_call" | custom-call | tf_op jit(solution)/shard_map/pallas_call | solution.py:86
  4.3 11.1 %all_to_all.15 = bf16[4,128,256]{2,1,0:T(8,128)(2,1)S(1)} all-to-all(bf16[4,128,256]{2,1,0:T(8,128)(2,1)} %shard_map.86), channel_id=1, replica_groups=mesh['z'=16,'yh'=2,'yl'=2,'x'=4,'core'=2] {'yh','yl'}, dimensions={0} | all-to-all | bytes 524288 | tf_op jit(solution)/shard_map/all_to_all | solution.py:668
  15.4 3.8 %collective-permute-start = (bf16[512,256]{1,0:T(8,128)(2,1)S(1)}, bf16[512,256]{1,0:T(8,128)(2,1)S(1)}, u32[]{:S(2)}, u32[]{:S(2)}) collective-permute-start(bf16[512,256]{1,0:T(8,128)(2,1)S(1)} %bitcast.8), channel_id=1, source_target_pairs={{0,32},{64,96},{128,160},{192,224},{256,288},{320,352},{384,416},{... | collective-permute-start | bytes 786440 | tf_op jit(solution)/shard_map/ppermute | solution.py:673
  19.2 4.5 %collective-permute-start.2 = (bf16[512,256]{1,0:T(8,128)(2,1)S(1)}, bf16[512,256]{1,0:T(8,128)(2,1)S(1)}, u32[]{:S(2)}, u32[]{:S(2)}) collective-permute-start(bf16[512,256]{1,0:T(8,128)(2,1)S(1)} %bitcast.9), channel_id=1, source_target_pairs={{480,0},{32,64},{96,128},{160,192},{224,256},{288,320},{352,384},{... | collective-permute-start | bytes 786440 | tf_op jit(solution)/shard_map/ppermute | solution.py:673
  23.8 0.0 copy-done.6
  23.8 0.0 copy-done
  23.8 0.0 copy-done.1
  23.8 0.0 copy-start.2
  23.8 0.0 copy-start.3
  23.8 0.0 copy-start.4
  23.8 0.0 copy-start.5
  23.9 0.5 shard_map.90.weights_ref
  24.3 1.9 %collective-permute-start.3 = (bf16[4,1536,128]{2,1,0:T(8,128)(2,1)S(1)}, bf16[4,1536,128]{2,1,0:T(8,128)(2,1)S(1)}, u32[]{:S(2)}, u32[]{:S(2)}) collective-permute-start(bf16[4,1536,128]{2,1,0:T(8,128)(2,1)S(1)} %shard_map.90.weights_ref), channel_id=1, source_target_pairs={{0,1},{1,0},{2,3},{3,2},{4,5},{5,4},{6,7},{7,6},{8,9},{9,8},{10,11... | collective-permute-start | bytes 4718600 | tf_op jit(solution)/shard_map/ppermute | solution.py:695
  26.3 3.8 %collective-permute-start.1 = (bf16[256,256]{1,0:T(8,128)(2,1)S(1)}, bf16[256,256]{1,0:T(8,128)(2,1)S(1)}, u32[]{:S(2)}, u32[]{:S(2)}) collective-permute-start(bf16[256,256]{1,0:T(8,128)(2,1)S(1)} %bitcast.12), channel_id=1, source_target_pairs={{448,0},{465,1},{80,16},{65,17},{480,32},{497,33},{112,48},{97,49}... | collective-permute-start | bytes 393224 | tf_op jit(solution)/shard_map/ppermute | solution.py:684
  30.1 0.0 copy-done.2
  30.1 0.0 copy-done.3
  30.1 0.0 copy-done.4
  30.1 0.0 copy-done.5
  30.1 0.8 %shard_map.87 = (bf16[2,16,1536]{2,1,0:T(8,128)(2,1)S(1)}, f32[4,16,1536]{2,1,0:T(8,128)S(1)}) custom-call(s32[32]{0:T(128)S(1)} %copy-done.5, bf16[128,1536]{1,0:T(8,128)(2,1)S(1)} %copy-done.2, bf16[128,1536]{1,0:T(8,128)(2,1)S(1)} %copy-done.3, bf16[3,32,1536]{2,1,0:T(8,128)(2,1)S(1)} %bitcast.7), custom_call_target="tpu_custom_call" | custom-call | tf_op jit(solution)/shard_map/pallas_call | solution.py:616
  30.9 0.0 collective-permute-done.first_ref
  30.9 0.0 collective-permute-done.2.second_ref
  30.9 6.2 %shard_map.88 = (bf16[1536,128]{1,0:T(8,128)(2,1)S(1)}, bf16[1536,128]{1,0:T(8,128)(2,1)S(1)}, bf16[1536,128]{1,0:T(8,128)(2,1)S(1)}, bf16[1536,128]{1,0:T(8,128...) custom-call(s32[32]{0:T(128)S(1)} %copy-done.5, ...), custom_call_target="tpu_custom_call" | custom-call | flops 7000000000 | bytes 1048576 | tf_op jit(solution)/shard_map/pallas_call | solution.py:308
  37.1 0.5 collective-permute-done.1.far_ref
  37.6 4.8 %shard_map.89 = bf16[4,64,256]{2,1,0:T(8,128)(2,1)S(1)} custom-call(s32[32]{0:T(128)S(1)} %copy-done.5, f32[8,128]{1,0:T(8,128)S(1)} %pad.4.gains_ref, bf16[256,256]{1,0:T(8,128)(2,1)S(1)} %collective-permute-done.1.far_ref, bf16[512,256]{1,0:T(8,128)(2,1)S(1)} %bitcast.11, bf16[1536,128]{1,0:T(8,128)(2,1)S(1)} %get-tuple-element.30.qx_ref, ...), custom_call_target="tpu_custom_call" | custom-call | flops 7000000000 | bytes 1048576 | tf_op jit(solution)/shard_map/pallas_call | solution.py:526
  42.4 10.2 %all_to_all.16.parts_ref = bf16[4,64,256]{2,1,0:T(8,128)(2,1)S(1)} all-to-all(bf16[4,64,256]{2,1,0:T(8,128)(2,1)S(1)} %shard_map.89), channel_id=1, replica_groups=mesh['z'=16,'yh'=2,'yl'=2,'x'=4,'core'=2] {'yl','core'}, dimensions={0} | all-to-all | bytes 262144 | tf_op jit(solution)/shard_map/all_to_all | solution.py:697
  52.7 0.0 collective-permute-done.3.weights_far_ref
  52.7 1.0 %shard_map.91 = bf16[4,16,3072]{2,1,0:T(8,128)(2,1)S(1)} custom-call(bf16[4,64,256]{2,1,0:T(8,128)(2,1)S(1)} %all_to_all.16.parts_ref, bf16[4,1536,128]{2,1,0:T(8,128)(2,1)S(1)} %shard_map.90.weights_ref, bf16[4,1536,128]{2,1,0:T(8,128)(2,1)S(1)} %collective-permute-done.3.weights_far_ref), custom_call_target="tpu_custom_call" | custom-call | tf_op jit(solution)/shard_map/pallas_call | solution.py:581
  53.7 11.8 %all_to_all.17.shares_ref = bf16[4,16,3072]{2,1,0:T(8,128)(2,1)S(1)} all-to-all(bf16[4,16,3072]{2,1,0:T(8,128)(2,1)S(1)} %shard_map.91), channel_id=1, replica_groups=mesh['z'=16,'yh'=2,'yl'=2,'x'=4,'core'=2] {'x'}, dimensions={0} | all-to-all | bytes 786432 | tf_op jit(solution)/shard_map/all_to_all | solution.py:699
  65.5 0.7 %shard_map.92 = (bf16[16,1536]{1,0:T(8,128)(2,1)}, bf16[16,1536]{1,0:T(8,128)(2,1)}) custom-call(bf16[2,16,1536]{2,1,0:T(8,128)(2,1)S(1)} %get-tuple-element.27.rows_ref, f32[4,16,1536]{2,1,0:T(8,128)S(1)} %get-tuple-element.28.factors_ref, bf16[4,16,3072]{2,1,0:T(8,128)(2,1)S(1)} %all_to_all.17.shares_ref), custom_call_target="tpu_custom_call" | custom-call | tf_op jit(solution)/shard_map/pallas_call | solution.py:647
  (2 shorter events, 0.0 us)
Async XLA Ops:
  0.6 23.1 %copy-start.6 = (f32[2,64]{1,0:T(2,128)S(1)}, f32[2,64]{1,0:T(2,128)}, u32[]{:S(2)}) copy-start(f32[2,64]{1,0:T(2,128)} %param.11) | copy-start | bytes 1540
  0.6 23.1 %copy-start = (bf16[1536,3,128]{2,0,1:T(8,128)(2,1)S(1)}, bf16[1536,3,128]{2,0,1:T(8,128)(2,1)}, u32[]{:S(2)}) copy-start(bf16[1536,3,128]{2,0,1:T(8,128)(2,1)} %param.9) | copy-start | bytes 3538948
  0.7 23.1 %copy-start.1 = (bf16[128,1536]{1,0:T(8,128)(2,1)S(1)}, bf16[128,1536]{1,0:T(8,128)(2,1)}, u32[]{:S(2)}) copy-start(bf16[128,1536]{1,0:T(8,128)(2,1)} %w_out_ref.2) | copy-start | bytes 1179652
  15.4 15.5 %collective-permute-start = (bf16[512,256]{1,0:T(8,128)(2,1)S(1)}, bf16[512,256]{1,0:T(8,128)(2,1)S(1)}, u32[]{:S(2)}, u32[]{:S(2)}) collective-permute-start(bf16[512,256]{1,0:T(8,128)(2,1)S(1)} %bitcast.8), channel_id=1, source_target_pairs={{0,32},{64,96},{128,160},{192,224},{256,288},{320,352},{384,416},{... | collective-permute-start | bytes 786440 | tf_op jit(solution)/shard_map/ppermute | solution.py:673
  19.2 11.7 %collective-permute-start.2 = (bf16[512,256]{1,0:T(8,128)(2,1)S(1)}, bf16[512,256]{1,0:T(8,128)(2,1)S(1)}, u32[]{:S(2)}, u32[]{:S(2)}) collective-permute-start(bf16[512,256]{1,0:T(8,128)(2,1)S(1)} %bitcast.9), channel_id=1, source_target_pairs={{480,0},{32,64},{96,128},{160,192},{224,256},{288,320},{352,384},{... | collective-permute-start | bytes 786440 | tf_op jit(solution)/shard_map/ppermute | solution.py:673
  23.8 6.3 %copy-start.2 = (bf16[128,1536]{1,0:T(8,128)(2,1)S(1)}, bf16[128,1536]{1,0:T(8,128)(2,1)}, u32[]{:S(2)}) copy-start(bf16[128,1536]{1,0:T(8,128)(2,1)} %tokens_ref.2) | copy-start | bytes 1179652
  23.8 6.3 %copy-start.3 = (bf16[128,1536]{1,0:T(8,128)(2,1)S(1)}, bf16[128,1536]{1,0:T(8,128)(2,1)}, u32[]{:S(2)}) copy-start(bf16[128,1536]{1,0:T(8,128)(2,1)} %cotangent_ref.2) | copy-start | bytes 1179652
  23.8 6.3 %copy-start.4 = (bf16[32,3,1536]{2,0,1:T(8,128)(2,1)S(1)}, bf16[32,3,1536]{2,0,1:T(8,128)(2,1)}, u32[]{:S(2)}) copy-start(bf16[32,3,1536]{2,0,1:T(8,128)(2,1)} %param.12) | copy-start | bytes 884740
  23.8 6.3 %copy-start.5 = (s32[32]{0:T(128)S(1)}, s32[32]{0:T(128)}, u32[]{:S(2)}) copy-start(s32[32]{0:T(128)} %counts_ref.7) | copy-start | bytes 388
  24.3 28.4 %collective-permute-start.3 = (bf16[4,1536,128]{2,1,0:T(8,128)(2,1)S(1)}, bf16[4,1536,128]{2,1,0:T(8,128)(2,1)S(1)}, u32[]{:S(2)}, u32[]{:S(2)}) collective-permute-start(bf16[4,1536,128]{2,1,0:T(8,128)(2,1)S(1)} %shard_map.90.weights_ref), channel_id=1, source_target_pairs={{0,1},{1,0},{2,3},{3,2},{4,5},{5,4},{6,7},{7,6},{8,9},{9,8},{10,11... | collective-permute-start | bytes 4718600 | tf_op jit(solution)/shard_map/ppermute | solution.py:695
  26.3 11.4 %collective-permute-start.1 = (bf16[256,256]{1,0:T(8,128)(2,1)S(1)}, bf16[256,256]{1,0:T(8,128)(2,1)S(1)}, u32[]{:S(2)}, u32[]{:S(2)}) collective-permute-start(bf16[256,256]{1,0:T(8,128)(2,1)S(1)} %bitcast.12), channel_id=1, source_target_pairs={{448,0},{465,1},{80,16},{65,17},{480,32},{497,33},{112,48},{97,49}... | collective-permute-start | bytes 393224 | tf_op jit(solution)/shard_map/ppermute | solution.py:684

commit v6 on v5

--- a/solution.py
+++ b/solution.py
@@ -204,6 +204,32 @@
 
 def rows_max(values):
     return jnp.max(by_eight(values), axis=0)
+
+
+def running_sums(k_ref, v_ref, key, chunks, q_block, d_block, s_ref, g_ref):
+    highest = jnp.full((8, CHUNK), -jnp.inf, F32)
+    total = jnp.zeros((8, CHUNK), F32)
+    grads = jnp.zeros((8, CHUNK), F32)
+    for piece in range(chunks):
+        keys_at = pl.ds(pl.multiple_of(key + piece * CHUNK, CHUNK), CHUNK)
+        here = slice(piece * CHUNK, (piece + 1) * CHUNK)
+        scores = rows_dot(k_ref[keys_at, :], q_block)
+        s_ref[here, :] = scores
+        g_ref[here, :] = rows_dot(v_ref[keys_at, :], d_block)
+        higher = jnp.maximum(highest, rows_max(scores) * LOG2_E)
+        shrink = jnp.exp2(highest - higher)
+        total = total * shrink
+        grads = grads * shrink
+        highest = higher
+        for tile in range(CHUNK // TILE):
+            at = slice(piece * CHUNK + tile * TILE, piece * CHUNK + (tile + 1) * TILE)
+            weights = jnp.exp2(by_eight(s_ref[at, :]) * LOG2_E - highest[None])
+            total = total + jnp.sum(weights, axis=0)
+            grads = grads + jnp.sum(weights * by_eight(g_ref[at, :]), axis=0)
+    top = jnp.max(highest, axis=0, keepdims=True)
+    shrink = jnp.exp2(highest - top)
+    total = jnp.sum(total * shrink, axis=0, keepdims=True)
+    return top, total, jnp.sum(grads * shrink, axis=0, keepdims=True)
 
 
 def near_kernel(
@@ -278,19 +304,12 @@
             key = jnp.where(begin < own_at, left_key, right_key) * CHUNK
             q_block = qx_ref[at, :]
             d_block = dx_ref[at, :]
-            keys_at = pl.ds(pl.multiple_of(key, CHUNK), REACH_CHUNKS * CHUNK)
-            s_ref[...] = rows_dot(kx_ref[keys_at, :], q_block)
-            g_ref[...] = rows_dot(vx_ref[keys_at, :], d_block)
-            highest = jnp.full((8, CHUNK), -jnp.inf, F32)
-            for piece in range(REACH_CHUNKS * CHUNK // TILE):
-                here = slice(piece * TILE, (piece + 1) * TILE)
-                highest = jnp.maximum(highest, rows_max(s_ref[here, :]))
-            highest = jnp.max(highest, axis=0, keepdims=True) * LOG2_E
-            zeros = jnp.zeros((8, CHUNK), F32)
-            total, grads = add_tiles(s_ref, g_ref, REACH_CHUNKS * CHUNK, highest, zeros, zeros)
+            highest, total, grads = running_sums(
+                kx_ref, vx_ref, key, REACH_CHUNKS, q_block, d_block, s_ref, g_ref
+            )
             stats_ref[slot, 0:1, :] = highest
-            stats_ref[slot, 1:2, :] = jnp.sum(total, axis=0, keepdims=True)
-            stats_ref[slot, 2:3, :] = jnp.sum(grads, axis=0, keepdims=True)
+            stats_ref[slot, 1:2, :] = total
+            stats_ref[slot, 2:3, :] = grads
             near_at = pl.ds(pl.multiple_of(own_at - key, CHUNK), CHUNK)
             sn_ref[slot, :, :] = s_ref[near_at, :]
             gn_ref[slot, :, :] = g_ref[near_at, :]
@@ -314,7 +333,7 @@
         out_specs=(VMEM,) * 10,
         scratch_shapes=[pltpu.VMEM((REACH_CHUNKS * CHUNK, CHUNK), F32)] * 2,
         cost_estimate=pl.CostEstimate(
-            flops=7000000000, bytes_accessed=1 << 20, transcendentals=1 << 20
+            flops=9000000000, bytes_accessed=1 << 20, transcendentals=1 << 20
         ),
         compiler_params=pltpu.CompilerParams(vmem_limit_bytes=VMEM_LIMIT),
     )(counts, gains, first, quad, second)
@@ -536,7 +555,7 @@
         + [pltpu.VMEM((CHUNK, LANES), F32)] * 2
         + [pltpu.VMEM((CHUNK, 2 * LANES), BF16)],
         cost_estimate=pl.CostEstimate(
-            flops=7000000000, bytes_accessed=1 << 20, transcendentals=1 << 20
+            flops=9000000000, bytes_accessed=1 << 20, transcendentals=1 << 20
         ),
         compiler_params=pltpu.CompilerParams(vmem_limit_bytes=VMEM_LIMIT),
     )(counts, gains, far, quad, *near_parts)

time: 66.6 us -> 63.7 us (0.956)
  the two profiles are of different devices: /device:TPU:64 before, /device:TPU:8 now
where the time goes in v6:
time: 63.7 us; the launch traced here: 63.3 us
  blocking collectives  33.4 us (52%)
  starting transfers between devices  14 us (22%)
  Pallas kernels  13.6 us (21%)
  waiting for transfers between devices  1.35 us (2%)
  between operations  0.85 us (1%)
    all_to_all x1, blocking collectives, per_device(): mine = lax.all_to_all(heads, ('yh', 'yl'), 0, 0)  14.4 us
    all_to_all x1, blocking collectives, per_device(): shares = lax.all_to_all(partial, 'x', 0, 0)  12.2 us
    ppermute x2, starting transfers between devices, per_device(): lax.ppermute(mine, 'z', pairs + [(j, i) for i, j in pairs])  10 us
    all_to_all x1, blocking collectives, per_device(): parts = lax.all_to_all(parts, ('yl', 'core'), 0, 0)  6.73 us
    pallas_call x1, Pallas kernels, attend_near(): pl.pallas_call(near_kernel, out_shape=(head_rows,) * 4 + (jax.ShapeDtypeS...  4.25 us
    pallas_call x1, Pallas kernels, enter(): pl.pallas_call(enter_kernel, out_shape=jax.ShapeDtypeStruct((quad, tokens...  3.62 us
    pallas_call x1, Pallas kernels, attend_far(): pl.pallas_call(far_kernel, out_shape=jax.ShapeDtypeStruct((4, CHUNK // 4,...  2.78 us
    ppermute x1, starting transfers between devices, per_device(): lax.ppermute(far_half, ('z', 'yh', 'core'), [(far_source(i), i) for i in...  2.05 us
  transfers between devices with their start and end apart: 4, of which 1 were waited for; matrix products, arithmetic and copies ran while one was open for 0% of the time, Pallas kernels for 13%

profile of v6, /device:TPU:8, one launch (start us, length us, event | category | flops | bytes accessed | tf_op | source)
XLA Modules:
  0.0 63.3 jit_solution(9495634899703406582)
XLA Ops:
  0.6 0.0 copy-start.6
  0.6 0.0 copy-start
  0.7 0.0 copy-start.1
  0.7 3.6 %shard_map.86 = bf16[4,128,256]{2,1,0:T(8,128)(2,1)} custom-call(s32[32]{0:T(128)} %counts_ref.7, bf16[128,1536]{1,0:T(8,128)(2,1)} %tokens_ref.2, bf16[128,1536]{1,0:T(8,128)(2,1)} %cotangent_ref.2, bf16[3,1536,128]{2,1,0:T(8,128)(2,1)} %bitcast.4, bf16[128,1536]{1,0:T(8,128)(2,1)} %w_out_ref.2, bf16[3,32,1536]{2,1,0:T(8,128)(2,1)} %bitcast.6), custom_call_target="tpu_custom_call" | custom-call | tf_op jit(solution)/shard_map/pallas_call | solution.py:86
  4.3 14.4 %all_to_all.15 = bf16[4,128,256]{2,1,0:T(8,128)(2,1)S(1)} all-to-all(bf16[4,128,256]{2,1,0:T(8,128)(2,1)} %shard_map.86), channel_id=1, replica_groups=mesh['z'=16,'yh'=2,'yl'=2,'x'=4,'core'=2] {'yh','yl'}, dimensions={0} | all-to-all | bytes 524288 | tf_op jit(solution)/shard_map/all_to_all | solution.py:687
  18.7 1.9 %collective-permute-start = (bf16[512,256]{1,0:T(8,128)(2,1)S(1)}, bf16[512,256]{1,0:T(8,128)(2,1)S(1)}, u32[]{:S(2)}, u32[]{:S(2)}) collective-permute-start(bf16[512,256]{1,0:T(8,128)(2,1)S(1)} %bitcast.8), channel_id=1, source_target_pairs={{0,32},{64,96},{128,160},{192,224},{256,288},{320,352},{384,416},{... | collective-permute-start | bytes 786440 | tf_op jit(solution)/shard_map/ppermute | solution.py:692
  20.6 8.1 %collective-permute-start.2 = (bf16[512,256]{1,0:T(8,128)(2,1)S(1)}, bf16[512,256]{1,0:T(8,128)(2,1)S(1)}, u32[]{:S(2)}, u32[]{:S(2)}) collective-permute-start(bf16[512,256]{1,0:T(8,128)(2,1)S(1)} %bitcast.9), channel_id=1, source_target_pairs={{480,0},{32,64},{96,128},{160,192},{224,256},{288,320},{352,384},{... | collective-permute-start | bytes 786440 | tf_op jit(solution)/shard_map/ppermute | solution.py:692
  28.7 0.0 copy-done.6
  28.8 0.0 copy-start.2
  28.8 0.0 copy-start.3
  28.8 0.0 copy-start.4
  28.8 0.0 copy-start.5
  28.8 2.1 %collective-permute-start.1 = (bf16[256,256]{1,0:T(8,128)(2,1)S(1)}, bf16[256,256]{1,0:T(8,128)(2,1)S(1)}, u32[]{:S(2)}, u32[]{:S(2)}) collective-permute-start(bf16[256,256]{1,0:T(8,128)(2,1)S(1)} %bitcast.12), channel_id=1, source_target_pairs={{448,0},{465,1},{80,16},{65,17},{480,32},{497,33},{112,48},{97,49}... | collective-permute-start | bytes 393224 | tf_op jit(solution)/shard_map/ppermute | solution.py:703
  30.9 0.0 copy-done
  30.9 0.0 copy-done.1
  30.9 0.5 shard_map.90.weights_ref
  31.4 1.9 %collective-permute-start.3 = (bf16[4,1536,128]{2,1,0:T(8,128)(2,1)S(1)}, bf16[4,1536,128]{2,1,0:T(8,128)(2,1)S(1)}, u32[]{:S(2)}, u32[]{:S(2)}) collective-permute-start(bf16[4,1536,128]{2,1,0:T(8,128)(2,1)S(1)} %shard_map.90.weights_ref), channel_id=1, source_target_pairs={{0,1},{1,0},{2,3},{3,2},{4,5},{5,4},{6,7},{7,6},{8,9},{9,8},{10,11... | collective-permute-start | bytes 4718600 | tf_op jit(solution)/shard_map/ppermute | solution.py:714
  33.3 0.0 copy-done.2
  33.3 0.0 copy-done.3
  33.3 0.0 copy-done.4
  33.3 0.0 copy-done.5
  33.4 0.8 %shard_map.87 = (bf16[2,16,1536]{2,1,0:T(8,128)(2,1)S(1)}, f32[4,16,1536]{2,1,0:T(8,128)S(1)}) custom-call(s32[32]{0:T(128)S(1)} %copy-done.5, bf16[128,1536]{1,0:T(8,128)(2,1)S(1)} %copy-done.2, bf16[128,1536]{1,0:T(8,128)(2,1)S(1)} %copy-done.3, bf16[3,32,1536]{2,1,0:T(8,128)(2,1)S(1)} %bitcast.7), custom_call_target="tpu_custom_call" | custom-call | tf_op jit(solution)/shard_map/pallas_call | solution.py:635
  34.1 0.0 collective-permute-done.first_ref
  34.1 1.3 %collective-permute-done.2.second_ref = bf16[512,256]{1,0:T(8,128)(2,1)S(1)} collective-permute-done((bf16[512,256]{1,0:T(8,128)(2,1)S(1)}, bf16[512,256]{1,0:T(8,128)(2,1)S(1)}, u32[]{:S(2)}, u32[]{:S(2)}) %collective-permute-start.2) | collective-permute-done | bytes 262176 | tf_op jit(solution)/shard_map/ppermute | solution.py:692
  35.5 4.2 %shard_map.88 = (bf16[1536,128]{1,0:T(8,128)(2,1)S(1)}, bf16[1536,128]{1,0:T(8,128)(2,1)S(1)}, bf16[1536,128]{1,0:T(8,128)(2,1)S(1)}, bf16[1536,128]{1,0:T(8,128...) custom-call(s32[32]{0:T(128)S(1)} %copy-done.5, ...), custom_call_target="tpu_custom_call" | custom-call | flops 8999999488 | bytes 1048576 | tf_op jit(solution)/shard_map/pallas_call | solution.py:327
  39.7 0.0 collective-permute-done.1.far_ref
  39.8 2.8 %shard_map.89 = bf16[4,64,256]{2,1,0:T(8,128)(2,1)S(1)} custom-call(s32[32]{0:T(128)S(1)} %copy-done.5, f32[8,128]{1,0:T(8,128)S(1)} %pad.4.gains_ref, bf16[256,256]{1,0:T(8,128)(2,1)S(1)} %collective-permute-done.1.far_ref, bf16[512,256]{1,0:T(8,128)(2,1)S(1)} %bitcast.11, bf16[1536,128]{1,0:T(8,128)(2,1)S(1)} %get-tuple-element.30.qx_ref, ...), custom_call_target="tpu_custom_call" | custom-call | flops 8999999488 | bytes 1048576 | tf_op jit(solution)/shard_map/pallas_call | solution.py:545
  42.5 6.7 %all_to_all.16.parts_ref = bf16[4,64,256]{2,1,0:T(8,128)(2,1)S(1)} all-to-all(bf16[4,64,256]{2,1,0:T(8,128)(2,1)S(1)} %shard_map.89), channel_id=1, replica_groups=mesh['z'=16,'yh'=2,'yl'=2,'x'=4,'core'=2] {'yl','core'}, dimensions={0} | all-to-all | bytes 262144 | tf_op jit(solution)/shard_map/all_to_all | solution.py:716
  49.3 0.0 collective-permute-done.3.weights_far_ref
  49.3 1.0 %shard_map.91 = bf16[4,16,3072]{2,1,0:T(8,128)(2,1)S(1)} custom-call(bf16[4,64,256]{2,1,0:T(8,128)(2,1)S(1)} %all_to_all.16.parts_ref, bf16[4,1536,128]{2,1,0:T(8,128)(2,1)S(1)} %shard_map.90.weights_ref, bf16[4,1536,128]{2,1,0:T(8,128)(2,1)S(1)} %collective-permute-done.3.weights_far_ref), custom_call_target="tpu_custom_call" | custom-call | tf_op jit(solution)/shard_map/pallas_call | solution.py:600
  50.3 12.2 %all_to_all.17.shares_ref = bf16[4,16,3072]{2,1,0:T(8,128)(2,1)S(1)} all-to-all(bf16[4,16,3072]{2,1,0:T(8,128)(2,1)S(1)} %shard_map.91), channel_id=1, replica_groups=mesh['z'=16,'yh'=2,'yl'=2,'x'=4,'core'=2] {'x'}, dimensions={0} | all-to-all | bytes 786432 | tf_op jit(solution)/shard_map/all_to_all | solution.py:718
  62.5 0.7 %shard_map.92 = (bf16[16,1536]{1,0:T(8,128)(2,1)}, bf16[16,1536]{1,0:T(8,128)(2,1)}) custom-call(bf16[2,16,1536]{2,1,0:T(8,128)(2,1)S(1)} %get-tuple-element.27.rows_ref, f32[4,16,1536]{2,1,0:T(8,128)S(1)} %get-tuple-element.28.factors_ref, bf16[4,16,3072]{2,1,0:T(8,128)(2,1)S(1)} %all_to_all.17.shares_ref), custom_call_target="tpu_custom_call" | custom-call | tf_op jit(solution)/shard_map/pallas_call | solution.py:666
  (2 shorter events, 0.0 us)
Async XLA Ops:
  0.6 28.1 %copy-start.6 = (f32[2,64]{1,0:T(2,128)S(1)}, f32[2,64]{1,0:T(2,128)}, u32[]{:S(2)}) copy-start(f32[2,64]{1,0:T(2,128)} %param.11) | copy-start | bytes 1540
  0.6 30.3 %copy-start = (bf16[1536,3,128]{2,0,1:T(8,128)(2,1)S(1)}, bf16[1536,3,128]{2,0,1:T(8,128)(2,1)}, u32[]{:S(2)}) copy-start(bf16[1536,3,128]{2,0,1:T(8,128)(2,1)} %param.9) | copy-start | bytes 3538948
  0.7 30.3 %copy-start.1 = (bf16[128,1536]{1,0:T(8,128)(2,1)S(1)}, bf16[128,1536]{1,0:T(8,128)(2,1)}, u32[]{:S(2)}) copy-start(bf16[128,1536]{1,0:T(8,128)(2,1)} %w_out_ref.2) | copy-start | bytes 1179652
  18.7 15.4 %collective-permute-start = (bf16[512,256]{1,0:T(8,128)(2,1)S(1)}, bf16[512,256]{1,0:T(8,128)(2,1)S(1)}, u32[]{:S(2)}, u32[]{:S(2)}) collective-permute-start(bf16[512,256]{1,0:T(8,128)(2,1)S(1)} %bitcast.8), channel_id=1, source_target_pairs={{0,32},{64,96},{128,160},{192,224},{256,288},{320,352},{384,416},{... | collective-permute-start | bytes 786440 | tf_op jit(solution)/shard_map/ppermute | solution.py:692
  20.6 14.9 %collective-permute-start.2 = (bf16[512,256]{1,0:T(8,128)(2,1)S(1)}, bf16[512,256]{1,0:T(8,128)(2,1)S(1)}, u32[]{:S(2)}, u32[]{:S(2)}) collective-permute-start(bf16[512,256]{1,0:T(8,128)(2,1)S(1)} %bitcast.9), channel_id=1, source_target_pairs={{480,0},{32,64},{96,128},{160,192},{224,256},{288,320},{352,384},{... | collective-permute-start | bytes 786440 | tf_op jit(solution)/shard_map/ppermute | solution.py:692
  28.8 4.5 %copy-start.2 = (bf16[128,1536]{1,0:T(8,128)(2,1)S(1)}, bf16[128,1536]{1,0:T(8,128)(2,1)}, u32[]{:S(2)}) copy-start(bf16[128,1536]{1,0:T(8,128)(2,1)} %tokens_ref.2) | copy-start | bytes 1179652
  28.8 4.5 %copy-start.3 = (bf16[128,1536]{1,0:T(8,128)(2,1)S(1)}, bf16[128,1536]{1,0:T(8,128)(2,1)}, u32[]{:S(2)}) copy-start(bf16[128,1536]{1,0:T(8,128)(2,1)} %cotangent_ref.2) | copy-start | bytes 1179652
  28.8 4.5 %copy-start.4 = (bf16[32,3,1536]{2,0,1:T(8,128)(2,1)S(1)}, bf16[32,3,1536]{2,0,1:T(8,128)(2,1)}, u32[]{:S(2)}) copy-start(bf16[32,3,1536]{2,0,1:T(8,128)(2,1)} %param.12) | copy-start | bytes 884740
  28.8 4.5 %copy-start.5 = (s32[32]{0:T(128)S(1)}, s32[32]{0:T(128)}, u32[]{:S(2)}) copy-start(s32[32]{0:T(128)} %counts_ref.7) | copy-start | bytes 388
  28.8 10.9 %collective-permute-start.1 = (bf16[256,256]{1,0:T(8,128)(2,1)S(1)}, bf16[256,256]{1,0:T(8,128)(2,1)S(1)}, u32[]{:S(2)}, u32[]{:S(2)}) collective-permute-start(bf16[256,256]{1,0:T(8,128)(2,1)S(1)} %bitcast.12), channel_id=1, source_target_pairs={{448,0},{465,1},{80,16},{65,17},{480,32},{497,33},{112,48},{97,49}... | collective-permute-start | bytes 393224 | tf_op jit(solution)/shard_map/ppermute | solution.py:703
  31.4 17.9 %collective-permute-start.3 = (bf16[4,1536,128]{2,1,0:T(8,128)(2,1)S(1)}, bf16[4,1536,128]{2,1,0:T(8,128)(2,1)S(1)}, u32[]{:S(2)}, u32[]{:S(2)}) collective-permute-start(bf16[4,1536,128]{2,1,0:T(8,128)(2,1)S(1)} %shard_map.90.weights_ref), channel_id=1, source_target_pairs={{0,1},{1,0},{2,3},{3,2},{4,5},{5,4},{6,7},{7,6},{8,9},{9,8},{10,11... | collective-permute-start | bytes 4718600 | tf_op jit(solution)/shard_map/ppermute | solution.py:714

commit v7 on v6

--- a/solution.py
+++ b/solution.py
@@ -206,16 +206,20 @@
     return jnp.max(by_eight(values), axis=0)
 
 
-def running_sums(k_ref, v_ref, key, chunks, q_block, d_block, s_ref, g_ref):
+def chunks_from(key, count, *refs):
+    rows = [pl.ds(pl.multiple_of(key + i * CHUNK, CHUNK), CHUNK) for i in range(count)]
+    return [tuple(ref.at[at, :] for ref in refs) for at in rows]
+
+
+def running_sums(pieces, q_block, d_block, s_ref, g_ref):
     highest = jnp.full((8, CHUNK), -jnp.inf, F32)
     total = jnp.zeros((8, CHUNK), F32)
     grads = jnp.zeros((8, CHUNK), F32)
-    for piece in range(chunks):
-        keys_at = pl.ds(pl.multiple_of(key + piece * CHUNK, CHUNK), CHUNK)
+    for piece, (keys_ref, values_ref) in enumerate(pieces):
         here = slice(piece * CHUNK, (piece + 1) * CHUNK)
-        scores = rows_dot(k_ref[keys_at, :], q_block)
+        scores = rows_dot(keys_ref[...], q_block)
         s_ref[here, :] = scores
-        g_ref[here, :] = rows_dot(v_ref[keys_at, :], d_block)
+        g_ref[here, :] = rows_dot(values_ref[...], d_block)
         higher = jnp.maximum(highest, rows_max(scores) * LOG2_E)
         shrink = jnp.exp2(highest - higher)
         total = total * shrink
@@ -304,9 +308,8 @@
             key = jnp.where(begin < own_at, left_key, right_key) * CHUNK
             q_block = qx_ref[at, :]
             d_block = dx_ref[at, :]
-            highest, total, grads = running_sums(
-                kx_ref, vx_ref, key, REACH_CHUNKS, q_block, d_block, s_ref, g_ref
-            )
+            pieces = chunks_from(key, REACH_CHUNKS, kx_ref, vx_ref)
+            highest, total, grads = running_sums(pieces, q_block, d_block, s_ref, g_ref)
             stats_ref[slot, 0:1, :] = highest
             stats_ref[slot, 1:2, :] = total
             stats_ref[slot, 2:3, :] = grads
@@ -364,9 +367,12 @@
     g_ref,
     p_ref,
     d_ref,
+    pn_ref,
+    dn_ref,
     sums_ref,
     dk_ref,
     dv_ref,
+    own_out_ref,
     done_ref,
 ):
     half, own_at, starts, ends, left_from, right_to = window_facts(counts_ref)
@@ -402,11 +408,6 @@
     scale = 1.0 / total
     mean_grad = grads * scale
 
-    def write_tile(scores, grads, highest, scale, mean_grad, to):
-        probs = jnp.exp2(scores * LOG2_E - highest) * scale
-        p_ref[to, :] = probs.astype(BF16)
-        d_ref[to, :] = (probs * (grads - mean_grad)).astype(BF16)
-
     near_scale = shrink * scale
     for piece in range(rows // TILE):
         at = slice(piece * TILE, (piece + 1) * TILE)
@@ -416,9 +417,11 @@
     for piece in range(CHUNK // TILE):
         at = slice(piece * TILE, (piece + 1) * TILE)
         to = slice(rows + piece * TILE, rows + (piece + 1) * TILE)
-        write_tile(s_ref[at, :], g_ref[at, :], highest, scale, mean_grad, to)
-    dk_ref[...] = jnp.dot(d_ref[own_rows, :], q_own, preferred_element_type=F32)
-    dv_ref[...] = jnp.dot(p_ref[own_rows, :], d_own, preferred_element_type=F32)
+        probs = jnp.exp2(s_ref[at, :] * LOG2_E - highest) * scale
+        p_ref[to, :] = probs.astype(BF16)
+        d_ref[to, :] = (probs * (g_ref[at, :] - mean_grad)).astype(BF16)
+    pn_ref[:, own_rows] = p_ref[own_rows, :]
+    dn_ref[:, own_rows] = d_ref[own_rows, :]
 
     def times_window(values_ref):
         main = jnp.dot(kv_ref[...], values_ref[0:rows, :], preferred_element_type=F32)
@@ -427,95 +430,68 @@
         )
 
     upper = lax.broadcasted_iota(jnp.int32, (LANES, CHUNK), 0) < HEAD
-    own_out = jnp.where(upper, times_window(d_ref) * INV_ROOT, times_window(p_ref)).T
+    own_out_ref[...] = jnp.where(
+        upper, times_window(d_ref) * INV_ROOT, times_window(p_ref)
+    ).T
 
     query_lane = lax.broadcasted_iota(jnp.int32, (1, CHUNK), 1)
     reaches_far = jnp.where(half == 0, left_from < 0, right_to > rows)
-
-    def add_gradients(tiles, begin, q_block, d_block, highest, total, grads):
-        place = query_lane + begin
+    sums_ref[...] = stats_ref[...]
+    dk_ref[...] = jnp.zeros_like(dk_ref)
+    dv_ref[...] = jnp.zeros_like(dv_ref)
+
+    @pl.when(reaches_far)
+    def _():
+        for step in range(2):
+            slot = half * (MAIN - 2) + step
+            at = pl.ds(pl.multiple_of(slot * CHUNK, CHUNK), CHUNK)
+            space = pl.ds((REACH_CHUNKS + step) * CHUNK, CHUNK)
+            highest, total, grads = running_sums(
+                [(kf_ref, vf_ref)], qx_ref[at, :], dx_ref[at, :], s_ref.at[space], g_ref.at[space]
+            )
+            before = sums_ref[slot, 0:1, :]
+            higher = jnp.maximum(before, highest)
+            old = jnp.exp2(before - higher)
+            new = jnp.exp2(highest - higher)
+            sums_ref[slot, 0:1, :] = higher
+            sums_ref[slot, 1:2, :] = sums_ref[slot, 1:2, :] * old + total * new
+            sums_ref[slot, 2:3, :] = sums_ref[slot, 2:3, :] * old + grads * new
+
+        q_block = qf_ref[...]
+        d_block = df_ref[...]
+        key = half * (MAIN // 2) * CHUNK
+        pieces = chunks_from(key, REACH_CHUNKS - 1, kx_ref, vx_ref) + [(kf_ref, vf_ref)]
+        highest, total, grads = running_sums(pieces, q_block, d_block, s_ref, g_ref)
+        place = query_lane + far_at
         scale = jnp.where((place >= left_from) & (place < right_to), 1.0 / total, 0.0)
         mean_grad = grads * scale
         for piece in range(CHUNK // TILE):
-            scores, given = tiles(piece)
             at = slice(piece * TILE, (piece + 1) * TILE)
-            write_tile(scores, given, highest, scale, mean_grad, at)
-        dk_ref[...] += jnp.dot(d_ref[0:CHUNK, :], q_block, preferred_element_type=F32)
-        dv_ref[...] += jnp.dot(p_ref[0:CHUNK, :], d_block, preferred_element_type=F32)
-
-    def one_chunk(step, carry):
+            near_at = pl.ds(pl.multiple_of(own_at - key + piece * TILE, TILE), TILE)
+            probs = jnp.exp2(s_ref[near_at, :] * LOG2_E - highest) * scale
+            p_ref[at, :] = probs.astype(BF16)
+            d_ref[at, :] = (probs * (g_ref[near_at, :] - mean_grad)).astype(BF16)
+        dk_ref[...] = jnp.dot(d_ref[0:CHUNK, :], q_block, preferred_element_type=F32)
+        dv_ref[...] = jnp.dot(p_ref[0:CHUNK, :], d_block, preferred_element_type=F32)
+
+    for step in range(MAIN - 1):
         slot = step + jnp.where(step >= 2 + half, 1, 0)
         begin = slot * CHUNK
-
-        @pl.when((begin < right_to) & (begin + CHUNK > left_from))
-        def _():
-            at = pl.ds(pl.multiple_of(begin, CHUNK), CHUNK)
-            q_block = qx_ref[at, :]
-            d_block = dx_ref[at, :]
-            sums_ref[...] = stats_ref[slot, :, :]
-            same_side = (begin < own_at) == (half == 0)
-
-            @pl.when(reaches_far & same_side)
-            def _():
-                scores = rows_dot(kf_ref[...], q_block)
-                s_ref[0:CHUNK, :] = scores
-                g_ref[0:CHUNK, :] = rows_dot(vf_ref[...], d_block)
-                before = sums_ref[0:1, :]
-                highest = jnp.max(rows_max(scores), axis=0, keepdims=True) * LOG2_E
-                highest = jnp.maximum(before, highest)
-                total, grads = add_tiles(s_ref, g_ref, CHUNK, highest, zeros, zeros)
-                shrink = jnp.exp2(before - highest)
-                sums_ref[0:1, :] = highest
-                total = jnp.sum(total, axis=0, keepdims=True)
-                grads = jnp.sum(grads, axis=0, keepdims=True)
-                sums_ref[1:2, :] = sums_ref[1:2, :] * shrink + total
-                sums_ref[2:3, :] = sums_ref[2:3, :] * shrink + grads
-
-            def tiles(piece):
-                at = slice(piece * TILE, (piece + 1) * TILE)
-                return sn_ref[slot, at, :], gn_ref[slot, at, :]
-
-            add_gradients(
-                tiles, begin, q_block, d_block, sums_ref[0:1, :], sums_ref[1:2, :], sums_ref[2:3, :]
-            )
-
-        return carry
-
-    lax.fori_loop(0, MAIN - 1, one_chunk, 0)
-
-    @pl.when(reaches_far)
-    def _():
-        q_block = qf_ref[...]
-        d_block = df_ref[...]
-        key = half * (MAIN // 2) * CHUNK
-        highest = jnp.full((8, CHUNK), -jnp.inf, F32)
-        for piece in range(REACH_CHUNKS):
-            here = slice(piece * CHUNK, (piece + 1) * CHUNK)
-            if piece < REACH_CHUNKS - 1:
-                keys_at = pl.ds(pl.multiple_of(key + piece * CHUNK, CHUNK), CHUNK)
-                keys, values = kx_ref[keys_at, :], vx_ref[keys_at, :]
-            else:
-                keys, values = kf_ref[...], vf_ref[...]
-            scores = rows_dot(keys, q_block)
-            s_ref[here, :] = scores
-            highest = jnp.maximum(highest, rows_max(scores))
-            g_ref[here, :] = rows_dot(values, d_block)
-        highest = jnp.max(highest, axis=0, keepdims=True) * LOG2_E
-        total, grads = add_tiles(s_ref, g_ref, REACH_CHUNKS * CHUNK, highest, zeros, zeros)
-
-        def tiles(piece):
-            at = pl.ds(pl.multiple_of(own_at - key + piece * TILE, TILE), TILE)
-            return s_ref[at, :], g_ref[at, :]
-
-        add_gradients(
-            tiles,
-            far_at,
-            q_block,
-            d_block,
-            highest,
-            jnp.sum(total, axis=0, keepdims=True),
-            jnp.sum(grads, axis=0, keepdims=True),
-        )
+        chunk_at = pl.ds(pl.multiple_of(begin, CHUNK), CHUNK)
+        place = query_lane + begin
+        valid = (place >= left_from) & (place < right_to)
+        highest = sums_ref[slot, 0:1, :]
+        scale = 1.0 / sums_ref[slot, 1:2, :]
+        mean_grad = sums_ref[slot, 2:3, :] * scale
+        for piece in range(CHUNK // TILE):
+            at = slice(piece * TILE, (piece + 1) * TILE)
+            probs = jnp.exp2(sn_ref[slot, at, :] * LOG2_E - highest) * scale
+            d_scores = probs * (gn_ref[slot, at, :] - mean_grad)
+            pn_ref[at, chunk_at] = jnp.where(valid, probs, 0.0).astype(BF16)
+            dn_ref[at, chunk_at] = jnp.where(valid, d_scores, 0.0).astype(BF16)
+    d_key = dk_ref[...] + jnp.dot(dn_ref[...], qx_ref[...], preferred_element_type=F32)
+    d_value = dv_ref[...] + jnp.dot(pn_ref[...], dx_ref[...], preferred_element_type=F32)
+    own_out = own_out_ref[...]
 
     def norm_grad(raw, gain, d_norm):
         inverse = lax.rsqrt(lower_mean(raw * raw) + EPS)
@@ -528,9 +504,9 @@
     raw_q = quad_ref[own_in_quad, 0:LANES].astype(F32)
     raw_k = quad_ref[own_in_quad, LANES:].astype(F32)
     d_q = norm_grad(raw_q, gains_ref[0:1, :], own_out)
-    d_k = norm_grad(raw_k, gains_ref[1:2, :], dk_ref[...])
+    d_k = norm_grad(raw_k, gains_ref[1:2, :], d_key)
     done_ref[:, 0:LANES] = jnp.where(low, d_q, own_out).astype(BF16)
-    done_ref[:, LANES:] = jnp.where(low, d_k, dv_ref[...]).astype(BF16)
+    done_ref[:, LANES:] = jnp.where(low, d_k, d_value).astype(BF16)
     share = 16
     for member in range(out_ref.shape[0]):
         block, core = member // 2, member % 2
@@ -549,10 +525,11 @@
         out_specs=VMEM,
         scratch_shapes=[pltpu.VMEM((CHUNK, LANES), BF16)] * 4
         + [pltpu.VMEM((LANES, CHUNK), BF16)]
-        + [pltpu.VMEM((REACH_CHUNKS * CHUNK, CHUNK), F32)] * 2
+        + [pltpu.VMEM(((REACH_CHUNKS + 2) * CHUNK, CHUNK), F32)] * 2
         + [pltpu.VMEM(((MAIN + 1) * CHUNK, CHUNK), BF16)] * 2
-        + [pltpu.VMEM((8, CHUNK), F32)]
-        + [pltpu.VMEM((CHUNK, LANES), F32)] * 2
+        + [pltpu.VMEM((CHUNK, MAIN * CHUNK), BF16)] * 2
+        + [pltpu.VMEM((MAIN + 1, 8, CHUNK), F32)]
+        + [pltpu.VMEM((CHUNK, LANES), F32)] * 3
         + [pltpu.VMEM((CHUNK, 2 * LANES), BF16)],
         cost_estimate=pl.CostEstimate(
             flops=9000000000, bytes_accessed=1 << 20, transcendentals=1 << 20

time: 63.7 us -> 63.7 us (level)
  the two profiles are of different devices: /device:TPU:8 before, /device:TPU:16 now
where the time goes in v7:
time: 63.7 us; the launch traced here: 63.3 us
  blocking collectives  32.5 us (51%)
  starting transfers between devices  15.4 us (24%)
  Pallas kernels  14.5 us (23%)
  between operations  0.85 us (1%)
    all_to_all x1, blocking collectives, per_device(): mine = lax.all_to_all(heads, ('yh', 'yl'), 0, 0)  13.1 us
    all_to_all x1, blocking collectives, per_device(): shares = lax.all_to_all(partial, 'x', 0, 0)  11.8 us
    ppermute x2, starting transfers between devices, per_device(): lax.ppermute(mine, 'z', pairs + [(j, i) for i, j in pairs])  10 us
    all_to_all x1, blocking collectives, per_device(): parts = lax.all_to_all(parts, ('yl', 'core'), 0, 0)  7.62 us
    pallas_call x1, Pallas kernels, attend_near(): pl.pallas_call(near_kernel, out_shape=(head_rows,) * 4 + (jax.ShapeDtypeS...  4.26 us
    pallas_call x1, Pallas kernels, enter(): pl.pallas_call(enter_kernel, out_shape=jax.ShapeDtypeStruct((quad, tokens...  3.62 us
    pallas_call x1, Pallas kernels, attend_far(): pl.pallas_call(far_kernel, out_shape=jax.ShapeDtypeStruct((4, CHUNK // 4,...  3.62 us
    ppermute x1, starting transfers between devices, per_device(): lax.ppermute(far_half, ('z', 'yh', 'core'), [(far_source(i), i) for i in...  3.49 us
  transfers between devices with their start and end apart: 4, of which 0 were waited for; matrix products, arithmetic and copies ran while one was open for 0% of the time, Pallas kernels for 14%

profile of v7, /device:TPU:16, one launch (start us, length us, event | category | flops | bytes accessed | tf_op | source)
XLA Modules:
  0.0 63.3 jit_solution(10566289043257942811)
XLA Ops:
  0.6 0.0 copy-start.6
  0.6 0.0 copy-start
  0.7 0.0 copy-start.1
  0.7 3.6 %shard_map.86 = bf16[4,128,256]{2,1,0:T(8,128)(2,1)} custom-call(s32[32]{0:T(128)} %counts_ref.7, bf16[128,1536]{1,0:T(8,128)(2,1)} %tokens_ref.2, bf16[128,1536]{1,0:T(8,128)(2,1)} %cotangent_ref.2, bf16[3,1536,128]{2,1,0:T(8,128)(2,1)} %bitcast.4, bf16[128,1536]{1,0:T(8,128)(2,1)} %w_out_ref.2, bf16[3,32,1536]{2,1,0:T(8,128)(2,1)} %bitcast.6), custom_call_target="tpu_custom_call" | custom-call | tf_op jit(solution)/shard_map/pallas_call | solution.py:86
  4.3 13.1 %all_to_all.15 = bf16[4,128,256]{2,1,0:T(8,128)(2,1)S(1)} all-to-all(bf16[4,128,256]{2,1,0:T(8,128)(2,1)} %shard_map.86), channel_id=1, replica_groups=mesh['z'=16,'yh'=2,'yl'=2,'x'=4,'core'=2] {'yh','yl'}, dimensions={0} | all-to-all | bytes 524288 | tf_op jit(solution)/shard_map/all_to_all | solution.py:664
  17.3 1.9 %collective-permute-start = (bf16[512,256]{1,0:T(8,128)(2,1)S(1)}, bf16[512,256]{1,0:T(8,128)(2,1)S(1)}, u32[]{:S(2)}, u32[]{:S(2)}) collective-permute-start(bf16[512,256]{1,0:T(8,128)(2,1)S(1)} %bitcast.8), channel_id=1, source_target_pairs={{0,32},{64,96},{128,160},{192,224},{256,288},{320,352},{384,416},{... | collective-permute-start | bytes 786440 | tf_op jit(solution)/shard_map/ppermute | solution.py:669
  19.3 8.1 %collective-permute-start.2 = (bf16[512,256]{1,0:T(8,128)(2,1)S(1)}, bf16[512,256]{1,0:T(8,128)(2,1)S(1)}, u32[]{:S(2)}, u32[]{:S(2)}) collective-permute-start(bf16[512,256]{1,0:T(8,128)(2,1)S(1)} %bitcast.9), channel_id=1, source_target_pairs={{480,0},{32,64},{96,128},{160,192},{224,256},{288,320},{352,384},{... | collective-permute-start | bytes 786440 | tf_op jit(solution)/shard_map/ppermute | solution.py:669
  27.4 0.0 copy-done.6
  27.4 0.0 copy-start.2
  27.4 0.0 copy-start.3
  27.5 0.0 copy-start.4
  27.5 0.0 copy-start.5
  27.5 3.5 %collective-permute-start.1 = (bf16[256,256]{1,0:T(8,128)(2,1)S(1)}, bf16[256,256]{1,0:T(8,128)(2,1)S(1)}, u32[]{:S(2)}, u32[]{:S(2)}) collective-permute-start(bf16[256,256]{1,0:T(8,128)(2,1)S(1)} %bitcast.12), channel_id=1, source_target_pairs={{448,0},{465,1},{80,16},{65,17},{480,32},{497,33},{112,48},{97,49}... | collective-permute-start | bytes 393224 | tf_op jit(solution)/shard_map/ppermute | solution.py:680
  31.0 0.0 copy-done
  31.0 0.0 copy-done.1
  31.0 0.5 shard_map.90.weights_ref
  31.5 1.9 %collective-permute-start.3 = (bf16[4,1536,128]{2,1,0:T(8,128)(2,1)S(1)}, bf16[4,1536,128]{2,1,0:T(8,128)(2,1)S(1)}, u32[]{:S(2)}, u32[]{:S(2)}) collective-permute-start(bf16[4,1536,128]{2,1,0:T(8,128)(2,1)S(1)} %shard_map.90.weights_ref), channel_id=1, source_target_pairs={{0,1},{1,0},{2,3},{3,2},{4,5},{5,4},{6,7},{7,6},{8,9},{9,8},{10,11... | collective-permute-start | bytes 4718600 | tf_op jit(solution)/shard_map/ppermute | solution.py:691
  33.4 0.0 copy-done.2
  33.4 0.0 copy-done.3
  33.4 0.0 copy-done.4
  33.4 0.0 copy-done.5
  33.4 0.8 %shard_map.87 = (bf16[2,16,1536]{2,1,0:T(8,128)(2,1)S(1)}, f32[4,16,1536]{2,1,0:T(8,128)S(1)}) custom-call(s32[32]{0:T(128)S(1)} %copy-done.5, bf16[128,1536]{1,0:T(8,128)(2,1)S(1)} %copy-done.2, bf16[128,1536]{1,0:T(8,128)(2,1)S(1)} %copy-done.3, bf16[3,32,1536]{2,1,0:T(8,128)(2,1)S(1)} %bitcast.7), custom_call_target="tpu_custom_call" | custom-call | tf_op jit(solution)/shard_map/pallas_call | solution.py:612
  34.2 0.0 collective-permute-done.first_ref
  34.2 0.0 collective-permute-done.2.second_ref
  34.2 4.3 %shard_map.88 = (bf16[1536,128]{1,0:T(8,128)(2,1)S(1)}, bf16[1536,128]{1,0:T(8,128)(2,1)S(1)}, bf16[1536,128]{1,0:T(8,128)(2,1)S(1)}, bf16[1536,128]{1,0:T(8,128...) custom-call(s32[32]{0:T(128)S(1)} %copy-done.5, ...), custom_call_target="tpu_custom_call" | custom-call | flops 8999999488 | bytes 1048576 | tf_op jit(solution)/shard_map/pallas_call | solution.py:330
  38.5 0.0 collective-permute-done.1.far_ref
  38.5 3.6 %shard_map.89 = bf16[4,64,256]{2,1,0:T(8,128)(2,1)S(1)} custom-call(s32[32]{0:T(128)S(1)} %copy-done.5, f32[8,128]{1,0:T(8,128)S(1)} %pad.4.gains_ref, bf16[256,256]{1,0:T(8,128)(2,1)S(1)} %collective-permute-done.1.far_ref, bf16[512,256]{1,0:T(8,128)(2,1)S(1)} %bitcast.11, bf16[1536,128]{1,0:T(8,128)(2,1)S(1)} %get-tuple-element.30.qx_ref, ...), custom_call_target="tpu_custom_call" | custom-call | flops 8999999488 | bytes 1048576 | tf_op jit(solution)/shard_map/pallas_call | solution.py:521
  42.1 7.6 %all_to_all.16.parts_ref = bf16[4,64,256]{2,1,0:T(8,128)(2,1)S(1)} all-to-all(bf16[4,64,256]{2,1,0:T(8,128)(2,1)S(1)} %shard_map.89), channel_id=1, replica_groups=mesh['z'=16,'yh'=2,'yl'=2,'x'=4,'core'=2] {'yl','core'}, dimensions={0} | all-to-all | bytes 262144 | tf_op jit(solution)/shard_map/all_to_all | solution.py:693
  49.8 0.0 collective-permute-done.3.weights_far_ref
  49.8 1.0 %shard_map.91 = bf16[4,16,3072]{2,1,0:T(8,128)(2,1)S(1)} custom-call(bf16[4,64,256]{2,1,0:T(8,128)(2,1)S(1)} %all_to_all.16.parts_ref, bf16[4,1536,128]{2,1,0:T(8,128)(2,1)S(1)} %shard_map.90.weights_ref, bf16[4,1536,128]{2,1,0:T(8,128)(2,1)S(1)} %collective-permute-done.3.weights_far_ref), custom_call_target="tpu_custom_call" | custom-call | tf_op jit(solution)/shard_map/pallas_call | solution.py:577
  50.8 11.8 %all_to_all.17.shares_ref = bf16[4,16,3072]{2,1,0:T(8,128)(2,1)S(1)} all-to-all(bf16[4,16,3072]{2,1,0:T(8,128)(2,1)S(1)} %shard_map.91), channel_id=1, replica_groups=mesh['z'=16,'yh'=2,'yl'=2,'x'=4,'core'=2] {'x'}, dimensions={0} | all-to-all | bytes 786432 | tf_op jit(solution)/shard_map/all_to_all | solution.py:695
  62.6 0.7 %shard_map.92 = (bf16[16,1536]{1,0:T(8,128)(2,1)}, bf16[16,1536]{1,0:T(8,128)(2,1)}) custom-call(bf16[2,16,1536]{2,1,0:T(8,128)(2,1)S(1)} %get-tuple-element.27.rows_ref, f32[4,16,1536]{2,1,0:T(8,128)S(1)} %get-tuple-element.28.factors_ref, bf16[4,16,3072]{2,1,0:T(8,128)(2,1)S(1)} %all_to_all.17.shares_ref), custom_call_target="tpu_custom_call" | custom-call | tf_op jit(solution)/shard_map/pallas_call | solution.py:643
  (2 shorter events, 0.0 us)
Async XLA Ops:
  0.6 26.8 %copy-start.6 = (f32[2,64]{1,0:T(2,128)S(1)}, f32[2,64]{1,0:T(2,128)}, u32[]{:S(2)}) copy-start(f32[2,64]{1,0:T(2,128)} %param.11) | copy-start | bytes 1540
  0.6 30.3 %copy-start = (bf16[1536,3,128]{2,0,1:T(8,128)(2,1)S(1)}, bf16[1536,3,128]{2,0,1:T(8,128)(2,1)}, u32[]{:S(2)}) copy-start(bf16[1536,3,128]{2,0,1:T(8,128)(2,1)} %param.9) | copy-start | bytes 3538948
  0.7 30.3 %copy-start.1 = (bf16[128,1536]{1,0:T(8,128)(2,1)S(1)}, bf16[128,1536]{1,0:T(8,128)(2,1)}, u32[]{:S(2)}) copy-start(bf16[128,1536]{1,0:T(8,128)(2,1)} %w_out_ref.2) | copy-start | bytes 1179652
  17.3 16.9 %collective-permute-start = (bf16[512,256]{1,0:T(8,128)(2,1)S(1)}, bf16[512,256]{1,0:T(8,128)(2,1)S(1)}, u32[]{:S(2)}, u32[]{:S(2)}) collective-permute-start(bf16[512,256]{1,0:T(8,128)(2,1)S(1)} %bitcast.8), channel_id=1, source_target_pairs={{0,32},{64,96},{128,160},{192,224},{256,288},{320,352},{384,416},{... | collective-permute-start | bytes 786440 | tf_op jit(solution)/shard_map/ppermute | solution.py:669
  19.3 15.0 %collective-permute-start.2 = (bf16[512,256]{1,0:T(8,128)(2,1)S(1)}, bf16[512,256]{1,0:T(8,128)(2,1)S(1)}, u32[]{:S(2)}, u32[]{:S(2)}) collective-permute-start(bf16[512,256]{1,0:T(8,128)(2,1)S(1)} %bitcast.9), channel_id=1, source_target_pairs={{480,0},{32,64},{96,128},{160,192},{224,256},{288,320},{352,384},{... | collective-permute-start | bytes 786440 | tf_op jit(solution)/shard_map/ppermute | solution.py:669
  27.4 6.0 %copy-start.2 = (bf16[128,1536]{1,0:T(8,128)(2,1)S(1)}, bf16[128,1536]{1,0:T(8,128)(2,1)}, u32[]{:S(2)}) copy-start(bf16[128,1536]{1,0:T(8,128)(2,1)} %tokens_ref.2) | copy-start | bytes 1179652
  27.4 6.0 %copy-start.3 = (bf16[128,1536]{1,0:T(8,128)(2,1)S(1)}, bf16[128,1536]{1,0:T(8,128)(2,1)}, u32[]{:S(2)}) copy-start(bf16[128,1536]{1,0:T(8,128)(2,1)} %cotangent_ref.2) | copy-start | bytes 1179652
  27.5 6.0 %copy-start.4 = (bf16[32,3,1536]{2,0,1:T(8,128)(2,1)S(1)}, bf16[32,3,1536]{2,0,1:T(8,128)(2,1)}, u32[]{:S(2)}) copy-start(bf16[32,3,1536]{2,0,1:T(8,128)(2,1)} %param.12) | copy-start | bytes 884740
  27.5 6.0 %copy-start.5 = (s32[32]{0:T(128)S(1)}, s32[32]{0:T(128)}, u32[]{:S(2)}) copy-start(s32[32]{0:T(128)} %counts_ref.7) | copy-start | bytes 388
  27.5 11.0 %collective-permute-start.1 = (bf16[256,256]{1,0:T(8,128)(2,1)S(1)}, bf16[256,256]{1,0:T(8,128)(2,1)S(1)}, u32[]{:S(2)}, u32[]{:S(2)}) collective-permute-start(bf16[256,256]{1,0:T(8,128)(2,1)S(1)} %bitcast.12), channel_id=1, source_target_pairs={{448,0},{465,1},{80,16},{65,17},{480,32},{497,33},{112,48},{97,49}... | collective-permute-start | bytes 393224 | tf_op jit(solution)/shard_map/ppermute | solution.py:680
  31.5 18.3 %collective-permute-start.3 = (bf16[4,1536,128]{2,1,0:T(8,128)(2,1)S(1)}, bf16[4,1536,128]{2,1,0:T(8,128)(2,1)S(1)}, u32[]{:S(2)}, u32[]{:S(2)}) collective-permute-start(bf16[4,1536,128]{2,1,0:T(8,128)(2,1)S(1)} %shard_map.90.weights_ref), channel_id=1, source_target_pairs={{0,1},{1,0},{2,3},{3,2},{4,5},{5,4},{6,7},{7,6},{8,9},{9,8},{10,11... | collective-permute-start | bytes 4718600 | tf_op jit(solution)/shard_map/ppermute | solution.py:691

commit v8 on v7

--- a/solution.py
+++ b/solution.py
@@ -661,7 +661,13 @@
     gains = jnp.pad(qk_gain, ((0, 6), (0, LANES - HEAD)))
 
     heads = enter(image_counts, tokens, cotangent, w_parts, w_out, mod_parts, quad)
+    _, tokens_late, cotangent_late, mod_late, w_parts_late, w_out_late = (
+        lax.optimization_barrier((heads, tokens, cotangent, mod_parts, w_parts, w_out))
+    )
+    rows, factors = ready(image_counts, tokens_late, cotangent_late, mod_late, share)
+    weights = pack(w_parts_late, w_out_late)
     mine = lax.all_to_all(heads, ("yh", "yl"), 0, 0)
+    mine, rows, factors, weights = lax.optimization_barrier((mine, rows, factors, weights))
     mine = mine.reshape(quad * tok_rows, 2 * LANES)
     evens = range(0, z_count, 2)
     swaps = [(i, i + 1) for i in evens], [((i - 1) % z_count, i) for i in evens]
@@ -680,14 +686,7 @@
     far = lax.ppermute(
         far_half, ("z", "yh", "core"), [(far_source(i), i) for i in range(halves)]
     )
-    _, tokens_late, cotangent_late, mod_late = lax.optimization_barrier(
-        (mine, tokens, cotangent, mod_parts)
-    )
-    rows, factors = ready(image_counts, tokens_late, cotangent_late, mod_late, share)
-    first, rows, factors = lax.optimization_barrier((first, rows, factors))
     near_parts = attend_near(image_counts, gains, first, mine, second)
-    _, w_parts_late, w_out_late = lax.optimization_barrier((mine, w_parts, w_out))
-    weights = pack(w_parts_late, w_out_late)
     weights_far = lax.ppermute(weights, "core", [(0, 1), (1, 0)])
     parts = attend_far(image_counts, gains, far, mine, near_parts)
     parts = lax.all_to_all(parts, ("yl", "core"), 0, 0)

time: 63.7 us -> 62.7 us (0.984)
  blocking collectives: 32.5 us -> 19.6 us
  starting transfers between devices: 15.4 us -> 24.4 us
  waiting for transfers between devices: 0.01 us -> 2.35 us
  local copies, waits for them, and re-layouts: 0.04 us -> 0.72 us
    all_to_all x1 -> x0, blocking collectives: 13.1 us -> none  [per_device(): mine = lax.all_to_all(heads, ('yh', 'yl'), 0, 0)]
    all_to_all x0 -> x1, starting transfers between devices: none -> 9.08 us  [per_device(): mine = lax.all_to_all(heads, ('yh', 'yl'), 0, 0)]
    all_to_all x0 -> x1, waiting for transfers between devices: none -> 1.72 us  [per_device(): mine = lax.all_to_all(heads, ('yh', 'yl'), 0, 0)]
    unnamed x14, local copies, waits for them, and re-layouts: 0.04 us -> 0.72 us
  transfers between devices with their start and end apart: 4 -> 5, of which waited for: 0 -> 2; matrix products, arithmetic and copies ran while one was open for 0% -> 0% of each run, Pallas kernels for 14% -> 15%
where the time goes in v8:
time: 62.7 us; the launch traced here: 62.3 us
  starting transfers between devices  24.4 us (39%)
  blocking collectives  19.6 us (31%)
  Pallas kernels  14.5 us (23%)
  waiting for transfers between devices  2.35 us (4%)
  between operations  0.8 us (1%)
  local copies, waits for them, and re-layouts  0.72 us (1%)
    all_to_all x1, blocking collectives, per_device(): shares = lax.all_to_all(partial, 'x', 0, 0)  11.8 us
    ppermute x2, starting transfers between devices, per_device(): lax.ppermute(mine, 'z', pairs + [(j, i) for i, j in pairs])  10 us
    all_to_all x1, starting transfers between devices, per_device(): mine = lax.all_to_all(heads, ('yh', 'yl'), 0, 0)  9.08 us
    all_to_all x1, blocking collectives, per_device(): parts = lax.all_to_all(parts, ('yl', 'core'), 0, 0)  7.76 us
    pallas_call x1, Pallas kernels, attend_near(): pl.pallas_call(near_kernel, out_shape=(head_rows,) * 4 + (jax.ShapeDtypeS...  4.26 us
    pallas_call x1, Pallas kernels, enter(): pl.pallas_call(enter_kernel, out_shape=jax.ShapeDtypeStruct((quad, tokens...  3.62 us
    pallas_call x1, Pallas kernels, attend_far(): pl.pallas_call(far_kernel, out_shape=jax.ShapeDtypeStruct((4, CHUNK // 4,...  3.62 us
    ppermute x1, starting transfers between devices, per_device(): lax.ppermute(far_half, ('z', 'yh', 'core'), [(far_source(i), i) for i in...  3.36 us
  transfers between devices with their start and end apart: 5, of which 2 were waited for; matrix products, arithmetic and copies ran while one was open for 0% of the time, Pallas kernels for 15%

profile of v8, /device:TPU:16, one launch (start us, length us, event | category | flops | bytes accessed | tf_op | source)
XLA Modules:
  0.0 62.3 jit_solution(12959572314832964128)
XLA Ops:
  0.6 0.0 copy-start
  0.6 0.0 copy-start.1
  0.6 3.6 %shard_map.86 = bf16[4,128,256]{2,1,0:T(8,128)(2,1)} custom-call(s32[32]{0:T(128)} %counts_ref.7, bf16[128,1536]{1,0:T(8,128)(2,1)} %tokens_ref.2, bf16[128,1536]{1,0:T(8,128)(2,1)} %cotangent_ref.2, bf16[3,1536,128]{2,1,0:T(8,128)(2,1)} %bitcast.4, bf16[128,1536]{1,0:T(8,128)(2,1)} %w_out_ref.2, bf16[3,32,1536]{2,1,0:T(8,128)(2,1)} %bitcast.6), custom_call_target="tpu_custom_call" | custom-call | tf_op jit(solution)/shard_map/pallas_call | solution.py:86
  4.3 9.1 %all-to-all-start = ((bf16[4,128,256]{2,1,0:T(8,128)(2,1)}), bf16[4,128,256]{2,1,0:T(8,128)(2,1)S(1)}, u32[]{:S(2)}, u32[]{:S(2)}) async-start(bf16[4,128,256]{2,1,0:T(8,128)(2,1)} %shard_map.86), calls=%async_computation | async-start | bytes 524288 | tf_op jit(solution)/shard_map/all_to_all | solution.py:669
  13.4 0.0 copy-done
  13.4 0.0 copy-done.1
  13.4 0.0 copy-start.2
  13.4 0.0 copy-start.3
  13.4 0.0 copy-start.4
  13.4 0.0 copy-start.5
  13.4 0.0 copy-start.6
  13.4 0.5 shard_map.88.weights_ref
  13.9 0.5 copy-done.2
  14.4 0.1 copy-done.3
  14.5 0.1 copy-done.4
  14.6 0.0 copy-done.5
  14.6 0.8 %shard_map.87 = (bf16[2,16,1536]{2,1,0:T(8,128)(2,1)S(1)}, f32[4,16,1536]{2,1,0:T(8,128)S(1)}) custom-call(s32[32]{0:T(128)S(1)} %copy-done.5, bf16[128,1536]{1,0:T(8,128)(2,1)S(1)} %copy-done.2, bf16[128,1536]{1,0:T(8,128)(2,1)S(1)} %copy-done.3, bf16[3,32,1536]{2,1,0:T(8,128)(2,1)S(1)} %bitcast.7), custom_call_target="tpu_custom_call" | custom-call | tf_op jit(solution)/shard_map/pallas_call | solution.py:612
  15.3 1.7 %all-to-all-done = bf16[4,128,256]{2,1,0:T(8,128)(2,1)S(1)} async-done(((bf16[4,128,256]{2,1,0:T(8,128)(2,1)}), bf16[4,128,256]{2,1,0:T(8,128)(2,1)S(1)}, u32[]{:S(2)}, u32[]{:S(2)}) %all-to-all-start) | async-done | bytes 262176 | tf_op jit(solution)/shard_map/all_to_all | solution.py:669
  17.1 1.9 %collective-permute-start.1 = (bf16[512,256]{1,0:T(8,128)(2,1)S(1)}, bf16[512,256]{1,0:T(8,128)(2,1)S(1)}, u32[]{:S(2)}, u32[]{:S(2)}) collective-permute-start(bf16[512,256]{1,0:T(8,128)(2,1)S(1)} %bitcast.8), channel_id=1, source_target_pairs={{0,32},{64,96},{128,160},{192,224},{256,288},{320,352},{384,416},{... | collective-permute-start | bytes 786440 | tf_op jit(solution)/shard_map/ppermute | solution.py:675
  19.0 8.1 %collective-permute-start.2 = (bf16[512,256]{1,0:T(8,128)(2,1)S(1)}, bf16[512,256]{1,0:T(8,128)(2,1)S(1)}, u32[]{:S(2)}, u32[]{:S(2)}) collective-permute-start(bf16[512,256]{1,0:T(8,128)(2,1)S(1)} %bitcast.9), channel_id=1, source_target_pairs={{480,0},{32,64},{96,128},{160,192},{224,256},{288,320},{352,384},{... | collective-permute-start | bytes 786440 | tf_op jit(solution)/shard_map/ppermute | solution.py:675
  27.1 0.0 copy-done.6
  27.2 3.4 %collective-permute-start = (bf16[256,256]{1,0:T(8,128)(2,1)S(1)}, bf16[256,256]{1,0:T(8,128)(2,1)S(1)}, u32[]{:S(2)}, u32[]{:S(2)}) collective-permute-start(bf16[256,256]{1,0:T(8,128)(2,1)S(1)} %bitcast.12), channel_id=1, source_target_pairs={{448,0},{465,1},{80,16},{65,17},{480,32},{497,33},{112,48},{97,49}... | collective-permute-start | bytes 393224 | tf_op jit(solution)/shard_map/ppermute | solution.py:686
  30.5 1.9 %collective-permute-start.3 = (bf16[4,1536,128]{2,1,0:T(8,128)(2,1)S(1)}, bf16[4,1536,128]{2,1,0:T(8,128)(2,1)S(1)}, u32[]{:S(2)}, u32[]{:S(2)}) collective-permute-start(bf16[4,1536,128]{2,1,0:T(8,128)(2,1)S(1)} %shard_map.88.weights_ref), channel_id=1, source_target_pairs={{0,1},{1,0},{2,3},{3,2},{4,5},{5,4},{6,7},{7,6},{8,9},{9,8},{10,11... | collective-permute-start | bytes 4718600 | tf_op jit(solution)/shard_map/ppermute | solution.py:690
  32.5 0.0 collective-permute-done.1.first_ref
  32.5 0.6 collective-permute-done.2.second_ref
  33.1 4.3 %shard_map.89 = (bf16[1536,128]{1,0:T(8,128)(2,1)S(1)}, bf16[1536,128]{1,0:T(8,128)(2,1)S(1)}, bf16[1536,128]{1,0:T(8,128)(2,1)S(1)}, bf16[1536,128]{1,0:T(8,128...) custom-call(s32[32]{0:T(128)S(1)} %copy-done.5, ...), custom_call_target="tpu_custom_call" | custom-call | flops 8999999488 | bytes 1048576 | tf_op jit(solution)/shard_map/pallas_call | solution.py:330
  37.4 0.0 collective-permute-done.far_ref
  37.4 3.6 %shard_map.90 = bf16[4,64,256]{2,1,0:T(8,128)(2,1)S(1)} custom-call(s32[32]{0:T(128)S(1)} %copy-done.5, f32[8,128]{1,0:T(8,128)S(1)} %pad.4.gains_ref, bf16[256,256]{1,0:T(8,128)(2,1)S(1)} %collective-permute-done.far_ref, bf16[512,256]{1,0:T(8,128)(2,1)S(1)} %bitcast.11, bf16[1536,128]{1,0:T(8,128)(2,1)S(1)} %get-tuple-element.33.qx_ref, ...), custom_call_target="tpu_custom_call" | custom-call | flops 8999999488 | bytes 1048576 | tf_op jit(solution)/shard_map/pallas_call | solution.py:521
  41.0 7.8 %all_to_all.15.parts_ref = bf16[4,64,256]{2,1,0:T(8,128)(2,1)S(1)} all-to-all(bf16[4,64,256]{2,1,0:T(8,128)(2,1)S(1)} %shard_map.90), channel_id=1, replica_groups=mesh['z'=16,'yh'=2,'yl'=2,'x'=4,'core'=2] {'yl','core'}, dimensions={0} | all-to-all | bytes 262144 | tf_op jit(solution)/shard_map/all_to_all | solution.py:692
  48.8 0.0 collective-permute-done.3.weights_far_ref
  48.8 1.0 %shard_map.91 = bf16[4,16,3072]{2,1,0:T(8,128)(2,1)S(1)} custom-call(bf16[4,64,256]{2,1,0:T(8,128)(2,1)S(1)} %all_to_all.15.parts_ref, bf16[4,1536,128]{2,1,0:T(8,128)(2,1)S(1)} %shard_map.88.weights_ref, bf16[4,1536,128]{2,1,0:T(8,128)(2,1)S(1)} %collective-permute-done.3.weights_far_ref), custom_call_target="tpu_custom_call" | custom-call | tf_op jit(solution)/shard_map/pallas_call | solution.py:577
  49.8 11.8 %all_to_all.16.shares_ref = bf16[4,16,3072]{2,1,0:T(8,128)(2,1)S(1)} all-to-all(bf16[4,16,3072]{2,1,0:T(8,128)(2,1)S(1)} %shard_map.91), channel_id=1, replica_groups=mesh['z'=16,'yh'=2,'yl'=2,'x'=4,'core'=2] {'x'}, dimensions={0} | all-to-all | bytes 786432 | tf_op jit(solution)/shard_map/all_to_all | solution.py:694
  61.6 0.7 %shard_map.92 = (bf16[16,1536]{1,0:T(8,128)(2,1)}, bf16[16,1536]{1,0:T(8,128)(2,1)}) custom-call(bf16[2,16,1536]{2,1,0:T(8,128)(2,1)S(1)} %get-tuple-element.30.rows_ref, f32[4,16,1536]{2,1,0:T(8,128)S(1)} %get-tuple-element.31.factors_ref, bf16[4,16,3072]{2,1,0:T(8,128)(2,1)S(1)} %all_to_all.16.shares_ref), custom_call_target="tpu_custom_call" | custom-call | tf_op jit(solution)/shard_map/pallas_call | solution.py:643
  (2 shorter events, 0.0 us)
Async XLA Ops:
  0.6 12.7 %copy-start = (bf16[1536,3,128]{2,0,1:T(8,128)(2,1)S(1)}, bf16[1536,3,128]{2,0,1:T(8,128)(2,1)}, u32[]{:S(2)}) copy-start(bf16[1536,3,128]{2,0,1:T(8,128)(2,1)} %param.9) | copy-start | bytes 3538948
  0.6 12.7 %copy-start.1 = (bf16[128,1536]{1,0:T(8,128)(2,1)S(1)}, bf16[128,1536]{1,0:T(8,128)(2,1)}, u32[]{:S(2)}) copy-start(bf16[128,1536]{1,0:T(8,128)(2,1)} %w_out_ref.2) | copy-start | bytes 1179652
  4.3 12.8 %all-to-all-start = ((bf16[4,128,256]{2,1,0:T(8,128)(2,1)}), bf16[4,128,256]{2,1,0:T(8,128)(2,1)S(1)}, u32[]{:S(2)}, u32[]{:S(2)}) async-start(bf16[4,128,256]{2,1,0:T(8,128)(2,1)} %shard_map.86), calls=%async_computation | async-start | bytes 524288 | tf_op jit(solution)/shard_map/all_to_all | solution.py:669
  13.4 1.0 %copy-start.2 = (bf16[128,1536]{1,0:T(8,128)(2,1)S(1)}, bf16[128,1536]{1,0:T(8,128)(2,1)}, u32[]{:S(2)}) copy-start(bf16[128,1536]{1,0:T(8,128)(2,1)} %tokens_ref.2) | copy-start | bytes 1179652
  13.4 1.1 %copy-start.3 = (bf16[128,1536]{1,0:T(8,128)(2,1)S(1)}, bf16[128,1536]{1,0:T(8,128)(2,1)}, u32[]{:S(2)}) copy-start(bf16[128,1536]{1,0:T(8,128)(2,1)} %cotangent_ref.2) | copy-start | bytes 1179652
  13.4 1.2 %copy-start.4 = (bf16[32,3,1536]{2,0,1:T(8,128)(2,1)S(1)}, bf16[32,3,1536]{2,0,1:T(8,128)(2,1)}, u32[]{:S(2)}) copy-start(bf16[32,3,1536]{2,0,1:T(8,128)(2,1)} %param.12) | copy-start | bytes 884740
  13.4 1.2 %copy-start.5 = (s32[32]{0:T(128)S(1)}, s32[32]{0:T(128)}, u32[]{:S(2)}) copy-start(s32[32]{0:T(128)} %counts_ref.7) | copy-start | bytes 388
  13.4 13.7 %copy-start.6 = (f32[2,64]{1,0:T(2,128)S(1)}, f32[2,64]{1,0:T(2,128)}, u32[]{:S(2)}) copy-start(f32[2,64]{1,0:T(2,128)} %param.11) | copy-start | bytes 1540
  17.1 15.4 %collective-permute-start.1 = (bf16[512,256]{1,0:T(8,128)(2,1)S(1)}, bf16[512,256]{1,0:T(8,128)(2,1)S(1)}, u32[]{:S(2)}, u32[]{:S(2)}) collective-permute-start(bf16[512,256]{1,0:T(8,128)(2,1)S(1)} %bitcast.8), channel_id=1, source_target_pairs={{0,32},{64,96},{128,160},{192,224},{256,288},{320,352},{384,416},{... | collective-permute-start | bytes 786440 | tf_op jit(solution)/shard_map/ppermute | solution.py:675
  19.0 14.1 %collective-permute-start.2 = (bf16[512,256]{1,0:T(8,128)(2,1)S(1)}, bf16[512,256]{1,0:T(8,128)(2,1)S(1)}, u32[]{:S(2)}, u32[]{:S(2)}) collective-permute-start(bf16[512,256]{1,0:T(8,128)(2,1)S(1)} %bitcast.9), channel_id=1, source_target_pairs={{480,0},{32,64},{96,128},{160,192},{224,256},{288,320},{352,384},{... | collective-permute-start | bytes 786440 | tf_op jit(solution)/shard_map/ppermute | solution.py:675
  27.2 10.2 %collective-permute-start = (bf16[256,256]{1,0:T(8,128)(2,1)S(1)}, bf16[256,256]{1,0:T(8,128)(2,1)S(1)}, u32[]{:S(2)}, u32[]{:S(2)}) collective-permute-start(bf16[256,256]{1,0:T(8,128)(2,1)S(1)} %bitcast.12), channel_id=1, source_target_pairs={{448,0},{465,1},{80,16},{65,17},{480,32},{497,33},{112,48},{97,49}... | collective-permute-start | bytes 393224 | tf_op jit(solution)/shard_map/ppermute | solution.py:686
  30.5 18.2 %collective-permute-start.3 = (bf16[4,1536,128]{2,1,0:T(8,128)(2,1)S(1)}, bf16[4,1536,128]{2,1,0:T(8,128)(2,1)S(1)}, u32[]{:S(2)}, u32[]{:S(2)}) collective-permute-start(bf16[4,1536,128]{2,1,0:T(8,128)(2,1)S(1)} %shard_map.88.weights_ref), channel_id=1, source_target_pairs={{0,1},{1,0},{2,3},{3,2},{4,5},{5,4},{6,7},{7,6},{8,9},{9,8},{10,11... | collective-permute-start | bytes 4718600 | tf_op jit(solution)/shard_map/ppermute | solution.py:690
